TPU v7x, 32 devices: a whole 2x2x4 slice. The times are simulated.
32 devices in a mesh: clip: 8 (over y, x, core), wt: 4 (over z).
Axes of the slice: x: 2, y: 2, z: 4, core: 2. Of those that a mesh axis runs over, the one named last changes fastest.
Arguments:
- encoded: bfloat16 [10048, 768], P(('clip', 'wt')), may hold values from -6 to 6
- visible_at: int32 [64, 157], P(('clip', 'wt')), may hold values from 0 to 1567, as said below
- project_weight: bfloat16 [768, 384], P('wt'), may hold values from -0.21875 to 0.21875
- mask_token: bfloat16 [384], P('wt'), may hold values from -6 to 6
- first_gain: bfloat16 [384], P('wt'), may hold values from 0.5 to 1.5
- first_shift: bfloat16 [384], P('wt'), may hold values from -1.75 to 1.75
- inputs_weight: bfloat16 [384, 1152], P('wt'), may hold values from -0.3125 to 0.3125
- query_bias: bfloat16 [384], P('wt'), may hold values from -1.75 to 1.75
- value_bias: bfloat16 [384], P('wt'), may hold values from -1.75 to 1.75
- merge_weight: bfloat16 [384, 384], P('wt'), may hold values from -1.25 to 1.25
- merge_bias: bfloat16 [384], P('wt'), may hold values from -1.75 to 1.75
- second_gain: bfloat16 [384], P('wt'), may hold values from 0.5 to 1.5
- second_shift: bfloat16 [384], P('wt'), may hold values from -1.75 to 1.75
- expand_weight: bfloat16 [384, 1536], P('wt'), may hold values from -0.3125 to 0.3125
- expand_bias: bfloat16 [1536], P('wt'), may hold values from -1.75 to 1.75
- reduce_weight: bfloat16 [1536, 384], P('wt'), may hold values from -0.15625 to 0.15625
- reduce_bias: bfloat16 [384], P('wt'), may hold values from -1.75 to 1.75
- upstream: bfloat16 [100352, 384], P(('clip', 'wt')), may hold values from -6 to 6
Outputs:
- decoded: bfloat16 [100352, 384], P(('clip', 'wt'))
- encoded_grad: bfloat16 [10048, 768], P(('clip', 'wt'))
- grad_project_weight: float32 [768, 384], P('wt')
- grad_mask_token: float32 [384], P('wt')
- grad_first_gain: float32 [384], P('wt')
- grad_first_shift: float32 [384], P('wt')
- grad_inputs_weight: float32 [384, 1152], P('wt')
- grad_query_bias: float32 [384], P('wt')
- grad_value_bias: float32 [384], P('wt')
- grad_merge_weight: float32 [384, 384], P('wt')
- grad_merge_bias: float32 [384], P('wt')
- grad_second_gain: float32 [384], P('wt')
- grad_second_shift: float32 [384], P('wt')
- grad_expand_weight: float32 [384, 1536], P('wt')
- grad_expand_bias: float32 [1536], P('wt')
- grad_reduce_weight: float32 [1536, 384], P('wt')
- grad_reduce_bias: float32 [384], P('wt')
Inputs may be any that keep to these rules, and one draw needn't show every extreme that they name: `visible_at`: each row names 157 distinct token places of one copy, in no particular order.
All inputs are finite; a program needn't handle non-finite values.
Results may differ from a plain program's by a relative error of at most 0.018.
Values may be sent and summed in bfloat16 or wider, within the bound.
A program may use at most 384 MiB of HBM per device.

v0:
```python
import math

import jax
import jax.numpy as jnp
from jax import lax
from jax.sharding import PartitionSpec as P

H = 6
HEAD = 64
L = 1568


EPSILON = 1e-06
INV_ROOT_TWO_PI = 1.0 / math.sqrt(2.0 * math.pi)
ROOT_HALF = math.sqrt(0.5)


def sinusoid_table(length, model_width):
    places = jnp.arange(length, dtype=jnp.int32).astype(jnp.float32)[:, None]
    columns = jnp.arange(model_width, dtype=jnp.int32)
    exponent = (2 * (columns // 2)).astype(jnp.float32) / model_width
    angles = places / jnp.power(10000.0, exponent)[None, :]
    return jnp.where(columns[None, :] % 2 == 0, jnp.sin(angles), jnp.cos(angles))


def normalize(inputs, gain_vector, shift_vector):
    center = inputs - jnp.mean(inputs, -1, keepdims=True)
    reciprocal = lax.rsqrt(jnp.mean(center * center, -1, keepdims=True) + EPSILON)
    scaled = center * reciprocal
    return (scaled * gain_vector + shift_vector, scaled, reciprocal)


def normalize_back(upward, scaled, reciprocal, gain_vector):
    grad_gain = jnp.sum(upward * scaled, 0)
    grad_shift = jnp.sum(upward, 0)
    lifted = upward * gain_vector
    result = reciprocal * (
        lifted
        - jnp.mean(lifted, -1, keepdims=True)
        - scaled * jnp.mean(lifted * scaled, -1, keepdims=True)
    )
    return (result, grad_gain, grad_shift)


def attend_forward(triple):
    query_rows, key_rows, value_rows = triple
    half_rows = query_rows.shape[0] // 2
    score_scale = 1.0 / math.sqrt(HEAD)
    outputs = []
    logsums = []
    for half_index in range(2):
        query_half = query_rows[half_index * half_rows : (half_index + 1) * half_rows]
        scores = (
            jnp.einsum("qhd,khd->hqk", query_half, key_rows, preferred_element_type=jnp.float32)
            * score_scale
        )
        row_max = jnp.max(scores, -1, keepdims=True)
        shifted = jnp.exp(scores - row_max)
        row_total = jnp.sum(shifted, -1, keepdims=True)
        weights = (shifted / row_total).astype(jnp.bfloat16)
        outputs.append(
            jnp.einsum("hqk,khd->qhd", weights, value_rows, preferred_element_type=jnp.float32)
        )
        logsums.append((row_max + jnp.log(row_total))[:, :, 0])
    return (jnp.concatenate(outputs, 0), jnp.concatenate(logsums, 1))


def attend_back(inputs):
    query_rows, key_rows, value_rows, logsum, grad_heads = inputs
    half_rows = query_rows.shape[0] // 2
    score_scale = 1.0 / math.sqrt(HEAD)
    grad_keys = jnp.zeros(key_rows.shape, jnp.float32)
    grad_values = jnp.zeros(value_rows.shape, jnp.float32)
    grad_queries = []
    for half_index in range(2):
        start_row = half_index * half_rows
        query_half = query_rows[start_row : start_row + half_rows]
        upward_half = grad_heads[start_row : start_row + half_rows]
        scores = (
            jnp.einsum("qhd,khd->hqk", query_half, key_rows, preferred_element_type=jnp.float32)
            * score_scale
        )
        probs_half = jnp.exp(scores - logsum[:, start_row : start_row + half_rows, None])
        weights = probs_half.astype(jnp.bfloat16)
        grad_values = grad_values + jnp.einsum(
            "hqk,qhd->khd", weights, upward_half, preferred_element_type=jnp.float32
        )
        grad_weights = jnp.einsum(
            "qhd,khd->hqk", upward_half, value_rows, preferred_element_type=jnp.float32
        )
        inner_sum = jnp.sum(probs_half * grad_weights, -1, keepdims=True)
        grad_scores = (probs_half * (grad_weights - inner_sum)).astype(jnp.bfloat16)
        grad_queries.append(
            jnp.einsum("hqk,khd->qhd", grad_scores, key_rows, preferred_element_type=jnp.float32)
            * score_scale
        )
        grad_keys = (
            grad_keys
            + jnp.einsum(
                "hqk,qhd->khd", grad_scores, query_half, preferred_element_type=jnp.float32
            )
            * score_scale
        )
    return (jnp.concatenate(grad_queries, 0), grad_keys, grad_values)


def per_device(
    encoded,
    visible_at,
    project_weight,
    mask_token,
    first_gain,
    first_shift,
    inputs_weight,
    query_bias,
    value_bias,
    merge_weight,
    merge_bias,
    second_gain,
    second_shift,
    expand_weight,
    expand_bias,
    reduce_weight,
    reduce_bias,
    upstream,
):
    clip_count = lax.axis_size("clip")
    my_clip = lax.axis_index("clip")
    held_rows = encoded.shape[0]
    width_in = encoded.shape[1]
    copy_count, seen_count = visible_at.shape
    length = L
    rows_total = copy_count * length
    capacity = (held_rows + clip_count - 1) // clip_count
    peer_ids = jnp.arange(clip_count, dtype=jnp.int32)[:, None]
    slot_ids = jnp.arange(capacity, dtype=jnp.int32)[None, :]
    first_out = (peer_ids * held_rows - my_clip + clip_count - 1) // clip_count
    out_index = first_out + slot_ids
    out_valid = (my_clip + clip_count * out_index < (peer_ids + 1) * held_rows).reshape(-1)
    picked = jnp.take(encoded, jnp.clip(out_index, 0, held_rows - 1).reshape(-1), axis=0)
    outgoing = jnp.where(out_valid[:, None], picked, jnp.zeros_like(picked)).reshape(
        clip_count, capacity, width_in
    )
    arrived = lax.all_to_all(outgoing, "clip", split_axis=0, concat_axis=0, tiled=True).reshape(
        clip_count * capacity, width_in
    )
    first_in = (my_clip * held_rows - peer_ids + clip_count - 1) // clip_count
    local_row = peer_ids + clip_count * (first_in + slot_ids) - my_clip * held_rows
    in_valid = (local_row < held_rows).reshape(-1)
    local_row = jnp.clip(local_row, 0, held_rows - 1).reshape(-1)
    target = jnp.take(visible_at.reshape(-1), local_row) + local_row // seen_count * length
    (
        embed_full,
        token_full,
        gain_first,
        shift_first,
        mixer_full,
        bias_query,
        bias_value,
        merge_full,
        bias_merge,
        gain_second,
        shift_second,
        expand_full,
        bias_expand,
        reduce_full,
        bias_reduce,
    ) = (
        lax.all_gather(project_weight, "wt", axis=0, tiled=True),
        lax.all_gather(mask_token, "wt", axis=0, tiled=True),
        lax.all_gather(first_gain, "wt", axis=0, tiled=True),
        lax.all_gather(first_shift, "wt", axis=0, tiled=True),
        lax.all_gather(inputs_weight, "wt", axis=0, tiled=True),
        lax.all_gather(query_bias, "wt", axis=0, tiled=True),
        lax.all_gather(value_bias, "wt", axis=0, tiled=True),
        lax.all_gather(merge_weight, "wt", axis=0, tiled=True),
        lax.all_gather(merge_bias, "wt", axis=0, tiled=True),
        lax.all_gather(second_gain, "wt", axis=0, tiled=True),
        lax.all_gather(second_shift, "wt", axis=0, tiled=True),
        lax.all_gather(expand_weight, "wt", axis=0, tiled=True),
        lax.all_gather(expand_bias, "wt", axis=0, tiled=True),
        lax.all_gather(reduce_weight, "wt", axis=0, tiled=True),
        lax.all_gather(reduce_bias, "wt", axis=0, tiled=True),
    )
    model_width = embed_full.shape[1]
    projected = jnp.dot(arrived, embed_full, preferred_element_type=jnp.float32).astype(
        jnp.bfloat16
    )
    placing = (target[None, :] == jnp.arange(rows_total, dtype=jnp.int32)[:, None]) & in_valid[
        None, :
    ]
    filled = jnp.dot(placing.astype(jnp.bfloat16), projected, preferred_element_type=jnp.float32)
    covered = jnp.sum(placing, 1, keepdims=True).astype(jnp.float32)
    positions = jnp.tile(sinusoid_table(length, model_width), (copy_count, 1))
    stream = filled + (1.0 - covered) * token_full.astype(jnp.float32)[None, :] + positions
    normed_first, scaled_first, recip_first = normalize(
        stream, gain_first.astype(jnp.float32), shift_first.astype(jnp.float32)
    )
    normed_first = normed_first.astype(jnp.bfloat16)
    zero_bias = jnp.zeros((model_width,), jnp.float32)
    mixer_bias = jnp.concatenate(
        [bias_query.astype(jnp.float32), zero_bias, bias_value.astype(jnp.float32)]
    )
    mixed = (
        jnp.dot(normed_first, mixer_full, preferred_element_type=jnp.float32) + mixer_bias
    ).astype(jnp.bfloat16)
    heads_view = mixed.reshape(copy_count, length, 3, H, HEAD)
    query_all = heads_view[:, :, 0]
    key_all = heads_view[:, :, 1]
    value_all = heads_view[:, :, 2]
    attended, logsum = lax.map(attend_forward, (query_all, key_all, value_all))
    context = attended.reshape(rows_total, model_width).astype(jnp.bfloat16)
    after_attn = (
        stream
        + jnp.dot(context, merge_full, preferred_element_type=jnp.float32)
        + bias_merge.astype(jnp.float32)
    )
    normed_second, scaled_second, recip_second = normalize(
        after_attn, gain_second.astype(jnp.float32), shift_second.astype(jnp.float32)
    )
    normed_second = normed_second.astype(jnp.bfloat16)
    lifted = jnp.dot(
        normed_second, expand_full, preferred_element_type=jnp.float32
    ) + bias_expand.astype(jnp.float32)
    activated = jax.nn.gelu(lifted, approximate=False).astype(jnp.bfloat16)
    result = (
        after_attn
        + jnp.dot(activated, reduce_full, preferred_element_type=jnp.float32)
        + bias_reduce.astype(jnp.float32)
    )
    decoded = result.astype(jnp.bfloat16)
    cotangent = upstream.astype(jnp.float32) * 0.5
    grad_reduced = cotangent.astype(jnp.bfloat16)
    sum_reduce_bias = jnp.sum(grad_reduced.astype(jnp.float32), 0)
    sum_reduce = jnp.einsum(
        "ra,rb->ab", activated, grad_reduced, preferred_element_type=jnp.float32
    )
    grad_active = jnp.einsum(
        "rb,ab->ra", grad_reduced, reduce_full, preferred_element_type=jnp.float32
    )
    slope = (
        0.5 * (1.0 + lax.erf(lifted * ROOT_HALF))
        + lifted * jnp.exp(-0.5 * lifted * lifted) * INV_ROOT_TWO_PI
    )
    grad_lifted = (grad_active * slope).astype(jnp.bfloat16)
    sum_expand_bias = jnp.sum(grad_lifted.astype(jnp.float32), 0)
    sum_expand = jnp.einsum(
        "ra,rb->ab", normed_second, grad_lifted, preferred_element_type=jnp.float32
    )
    grad_normed_second = jnp.einsum(
        "rb,ab->ra", grad_lifted, expand_full, preferred_element_type=jnp.float32
    )
    back_second, sum_gain_second, sum_shift_second = normalize_back(
        grad_normed_second, scaled_second, recip_second, gain_second.astype(jnp.float32)
    )
    grad_after = cotangent + back_second
    grad_merged = grad_after.astype(jnp.bfloat16)
    sum_merge_bias = jnp.sum(grad_merged.astype(jnp.float32), 0)
    sum_merge = jnp.einsum("ra,rb->ab", context, grad_merged, preferred_element_type=jnp.float32)
    grad_context = jnp.einsum(
        "rb,ab->ra", grad_merged, merge_full, preferred_element_type=jnp.float32
    ).astype(jnp.bfloat16)
    grad_heads = grad_context.reshape(copy_count, length, H, HEAD)
    grad_query, grad_key, grad_value = lax.map(
        attend_back, (query_all, key_all, value_all, logsum, grad_heads)
    )
    grad_mixed = (
        jnp.stack([grad_query, grad_key, grad_value], 2)
        .reshape(rows_total, 3 * model_width)
        .astype(jnp.bfloat16)
    )
    grad_mixed_wide = grad_mixed.astype(jnp.float32)
    sum_query = jnp.sum(grad_mixed_wide[:, :model_width], 0)
    sum_value = jnp.sum(grad_mixed_wide[:, 2 * model_width :], 0)
    sum_mixer = jnp.einsum(
        "ra,rb->ab", normed_first, grad_mixed, preferred_element_type=jnp.float32
    )
    grad_normed_first = jnp.einsum(
        "rb,ab->ra", grad_mixed, mixer_full, preferred_element_type=jnp.float32
    )
    back_first, sum_gain_first, sum_shift_first = normalize_back(
        grad_normed_first, scaled_first, recip_first, gain_first.astype(jnp.float32)
    )
    grad_stream = grad_after + back_first
    sum_token = jnp.sum((1.0 - covered) * grad_stream, 0)
    safe_target = jnp.clip(target, 0, rows_total - 1)
    grad_projected = jnp.where(
        in_valid[:, None], jnp.take(grad_stream, safe_target, axis=0), 0.0
    ).astype(jnp.bfloat16)
    sum_embed = jnp.einsum("ra,rb->ab", arrived, grad_projected, preferred_element_type=jnp.float32)
    grad_arrived = jnp.einsum(
        "rb,ab->ra", grad_projected, embed_full, preferred_element_type=jnp.float32
    ).astype(jnp.bfloat16)
    returned = lax.all_to_all(
        grad_arrived.reshape(clip_count, capacity, width_in),
        "clip",
        split_axis=0,
        concat_axis=0,
        tiled=True,
    )
    own_rows = jnp.arange(held_rows, dtype=jnp.int32)
    dest_of = (my_clip + clip_count * own_rows) // held_rows
    slot_of = own_rows - jnp.take(first_out[:, 0], dest_of)
    encoded_grad = jnp.take(
        returned.reshape(clip_count * capacity, width_in), dest_of * capacity + slot_of, axis=0
    )
    full_grads = (
        sum_embed,
        sum_token,
        sum_gain_first,
        sum_shift_first,
        sum_mixer,
        sum_query,
        sum_value,
        sum_merge,
        sum_merge_bias,
        sum_gain_second,
        sum_shift_second,
        sum_expand,
        sum_expand_bias,
        sum_reduce,
        sum_reduce_bias,
    )
    shard_sums = (
        lax.psum_scatter(
            full_grads[0].astype(jnp.bfloat16), "wt", scatter_dimension=0, tiled=True
        ).astype(jnp.float32),
        lax.psum_scatter(
            full_grads[1].astype(jnp.bfloat16), "wt", scatter_dimension=0, tiled=True
        ).astype(jnp.float32),
        lax.psum_scatter(
            full_grads[2].astype(jnp.bfloat16), "wt", scatter_dimension=0, tiled=True
        ).astype(jnp.float32),
        lax.psum_scatter(
            full_grads[3].astype(jnp.bfloat16), "wt", scatter_dimension=0, tiled=True
        ).astype(jnp.float32),
        lax.psum_scatter(
            full_grads[4].astype(jnp.bfloat16), "wt", scatter_dimension=0, tiled=True
        ).astype(jnp.float32),
        lax.psum_scatter(
            full_grads[5].astype(jnp.bfloat16), "wt", scatter_dimension=0, tiled=True
        ).astype(jnp.float32),
        lax.psum_scatter(
            full_grads[6].astype(jnp.bfloat16), "wt", scatter_dimension=0, tiled=True
        ).astype(jnp.float32),
        lax.psum_scatter(
            full_grads[7].astype(jnp.bfloat16), "wt", scatter_dimension=0, tiled=True
        ).astype(jnp.float32),
        lax.psum_scatter(
            full_grads[8].astype(jnp.bfloat16), "wt", scatter_dimension=0, tiled=True
        ).astype(jnp.float32),
        lax.psum_scatter(
            full_grads[9].astype(jnp.bfloat16), "wt", scatter_dimension=0, tiled=True
        ).astype(jnp.float32),
        lax.psum_scatter(
            full_grads[10].astype(jnp.bfloat16), "wt", scatter_dimension=0, tiled=True
        ).astype(jnp.float32),
        lax.psum_scatter(
            full_grads[11].astype(jnp.bfloat16), "wt", scatter_dimension=0, tiled=True
        ).astype(jnp.float32),
        lax.psum_scatter(
            full_grads[12].astype(jnp.bfloat16), "wt", scatter_dimension=0, tiled=True
        ).astype(jnp.float32),
        lax.psum_scatter(
            full_grads[13].astype(jnp.bfloat16), "wt", scatter_dimension=0, tiled=True
        ).astype(jnp.float32),
        lax.psum_scatter(
            full_grads[14].astype(jnp.bfloat16), "wt", scatter_dimension=0, tiled=True
        ).astype(jnp.float32),
    )
    totals = (
        lax.psum(shard_sums[0].astype(jnp.bfloat16), "clip").astype(jnp.float32),
        lax.psum(shard_sums[1].astype(jnp.bfloat16), "clip").astype(jnp.float32),
        lax.psum(shard_sums[2].astype(jnp.bfloat16), "clip").astype(jnp.float32),
        lax.psum(shard_sums[3].astype(jnp.bfloat16), "clip").astype(jnp.float32),
        lax.psum(shard_sums[4].astype(jnp.bfloat16), "clip").astype(jnp.float32),
        lax.psum(shard_sums[5].astype(jnp.bfloat16), "clip").astype(jnp.float32),
        lax.psum(shard_sums[6].astype(jnp.bfloat16), "clip").astype(jnp.float32),
        lax.psum(shard_sums[7].astype(jnp.bfloat16), "clip").astype(jnp.float32),
        lax.psum(shard_sums[8].astype(jnp.bfloat16), "clip").astype(jnp.float32),
        lax.psum(shard_sums[9].astype(jnp.bfloat16), "clip").astype(jnp.float32),
        lax.psum(shard_sums[10].astype(jnp.bfloat16), "clip").astype(jnp.float32),
        lax.psum(shard_sums[11].astype(jnp.bfloat16), "clip").astype(jnp.float32),
        lax.psum(shard_sums[12].astype(jnp.bfloat16), "clip").astype(jnp.float32),
        lax.psum(shard_sums[13].astype(jnp.bfloat16), "clip").astype(jnp.float32),
        lax.psum(shard_sums[14].astype(jnp.bfloat16), "clip").astype(jnp.float32),
    )
    return (
        decoded,
        encoded_grad,
        totals[0],
        totals[1],
        totals[2],
        totals[3],
        totals[4],
        totals[5],
        totals[6],
        totals[7],
        totals[8],
        totals[9],
        totals[10],
        totals[11],
        totals[12],
        totals[13],
        totals[14],
    )


def solution(mesh):
    return jax.shard_map(
        per_device,
        mesh=mesh,
        in_specs=(
            P(("clip", "wt"), None),
            P(("clip", "wt"), None),
            P("wt", None),
            P("wt"),
            P("wt"),
            P("wt"),
            P("wt", None),
            P("wt"),
            P("wt"),
            P("wt", None),
            P("wt"),
            P("wt"),
            P("wt"),
            P("wt", None),
            P("wt"),
            P("wt", None),
            P("wt"),
            P(("clip", "wt"), None),
        ),
        out_specs=(
            P(("clip", "wt"), None),
            P(("clip", "wt"), None),
            P("wt", None),
            P("wt"),
            P("wt"),
            P("wt"),
            P("wt", None),
            P("wt"),
            P("wt"),
            P("wt", None),
            P("wt"),
            P("wt"),
            P("wt"),
            P("wt", None),
            P("wt"),
            P("wt", None),
            P("wt"),
        ),
        check_vma=False,
    )
```

profile of v0, /device:TPU:0, one launch (start us, length us, event | category | flops | bytes accessed | tf_op | source)
XLA Modules:
  0.0 1137.6 jit_solution(10273195758027780802)
XLA Ops:
  21.2 13.0 %all-reduce.22 = (bf16[384]{0:T(512)(128)(2,1)S(1)}, bf16[384]{0:T(512)(128)(2,1)S(1)}, bf16[384]{0:T(512)(128)(2,1)S(1)}, bf16[384]{0:T(512)(128)(2,1)S(1)}, bf...) all-reduce(bf16[384]{0:T(512)(128)(2,1)S(1)} %dynamic-update-slice,, ...), channel_id=1, replica_groups=mesh['clip'=8,'wt'=4] {'wt'}, use_global_device_ids=true, to_apply=%add | all-reduce | flops 3072 | bytes 12288
  39.8 11.9 %all-gather = bf16[4,1,384]{2,1,0:T(2,128)(2,1)S(1)} all-gather(bf16[1,1,384]{2,1,0:T(2,128)(2,1)S(1)} %reshape.813), channel_id=1, replica_groups=mesh['clip'=8,'wt'=4] {'wt'}, dimensions={0}, use_global_device_ids=true | all-gather | bytes 3840 | tf_op jit(solution)/shard_map/all_gather | solution.py:181
  53.3 21.6 %all_gather.45 = bf16[768,384]{1,0:T(8,128)(2,1)S(1)} all-gather(bf16[192,384]{1,0:T(8,128)(2,1)S(1)} %copy-done.30), channel_id=1, replica_groups=mesh['clip'=8,'wt'=4] {'wt'}, dimensions={0}, use_global_device_ids=true | all-gather | bytes 737280 | tf_op jit(solution)/shard_map/all_gather | solution.py:169
  83.5 15.4 %all_gather.52 = bf16[384,384]{1,0:T(8,128)(2,1)} all-gather(bf16[96,384]{1,0:T(8,128)(2,1)S(1)} %copy-done.33), channel_id=1, replica_groups=mesh['clip'=8,'wt'=4] {'wt'}, dimensions={0}, use_global_device_ids=true | all-gather | bytes 368640 | tf_op jit(solution)/shard_map/all_gather | solution.py:176
  98.9 18.4 %all_gather.49 = bf16[384,1152]{1,0:T(8,128)(2,1)} all-gather(bf16[96,1152]{1,0:T(8,128)(2,1)} %param.28), channel_id=1, replica_groups=mesh['clip'=8,'wt'=4] {'wt'}, dimensions={0}, use_global_device_ids=true | all-gather | bytes 1105920 | tf_op jit(solution)/shard_map/all_gather | solution.py:173
  138.3 11.4 %copy.61 = bf16[3136,1152]{0,1:T(8,128)(2,1)} copy(bf16[3136,1152]{1,0:T(8,128)(2,1)} %fusion.90) | data formatting | bytes 14450688 | tf_op jit(solution)/shard_map/convert_element_type | solution.py:206
  149.7 16.8 %reshape.706 = bf16[2,1568,3,6,64]{1,0,4,3,2:T(2,128)(2,1)} reshape(bf16[3136,1152]{0,1:T(8,128)(2,1)} %copy.61) | data formatting | bytes 14450688 | tf_op jit(solution)/shard_map/reshape | solution.py:207
  181.3 171.6 %while.26 = (s32[]{:T(128)}, bf16[2,1568,6,64]{1,3,2,0:T(8,128)(2,1)}, f32[2,6,1568]{2,1,0:T(8,128)S(1)}, bf16[2,1568,6,64]{1,3,2,0:T(8,128)(2,1)}, bf16[2,1568,...) while((s32[]{:T(128)}, ...), condition=%wide.region_8.9_spmd, body=%wide.region_3.8_spmd.sunk | while | flops 3911620608 | bytes 191394416 | solution.py:211
  181.7 14.7 %multiply_reduce_fusion.17 = (f32[6,784]{1,0:T(8,128)S(1)}, f32[6,784,1568]{2,1,0:T(8,128)}) fusion(bf16[2,1568,6,64]{1,3,2,0:T(8,128)(2,1)S(1)} %get-tuple-element.427, s32[]{:T(128)S(6)} %copy.88, bf16[2,1568,6,64]{1,3,2,0:T(8,128)(2,1)} %get-tuple-element.426, s32[]{:T(128)S(6)} %add.904), kind=kOutput, calls=%fused_computation.8.clone.1 | convolution fusion | flops 958858624 | bytes 31489920 | tf_op jit(solution)/shard_map/while/body/eval_jaxpr/qhd,khd->hqk/dot_general | solution.py:54
  196.4 12.5 %fusion.191 = f32[6,784]{1,0:T(8,128)S(1)} fusion(f32[6,784,1568]{2,1,0:T(8,128)} %get-tuple-element.381, f32[6,784]{1,0:T(8,128)S(1)} %get-tuple-element.382), kind=kLoop, calls=%fused_computation.11.clone.1 | loop fusion | flops 22122912 | bytes 29541120 | tf_op jit(solution)/shard_map/while/body/eval_jaxpr/reduce_sum | solution.py:59
  209.0 14.4 %fusion.192 = bf16[784,6,64]{0,2,1:T(8,128)(2,1)} fusion(f32[6,784,1568]{2,1,0:T(8,128)} %get-tuple-element.381, f32[6,784]{1,0:T(8,128)S(1)} %fusion.191, f32[6,784]{1,0:T(8,128)S(1)} %get-tuple-element.382, bf16[2,1568,6,64]{1,3,2,0:T(8,128)(2,1)} %get-tuple-element.425, s32[]{:T(128)S(6)} %copy.88), kind=kOutput, calls=%fused_computation.16.clone.1 | convolution fusion | flops 973615104 | bytes 33227524 | tf_op jit(solution)/shard_map/while/body/eval_jaxpr/hqk,khd->qhd/dot_general | solution.py:62
  223.4 14.1 %multiply_reduce_fusion.18 = (f32[6,784]{1,0:T(8,128)S(1)}, f32[6,784,1568]{2,1,0:T(8,128)}) fusion(bf16[2,1568,6,64]{1,3,2,0:T(8,128)(2,1)S(1)} %get-tuple-element.427, s32[]{:T(128)S(6)} %copy.88, bf16[2,1568,6,64]{1,3,2,0:T(8,128)(2,1)} %get-tuple-element.426), kind=kOutput, calls=%fused_computation.9.clone.1 | convolution fusion | flops 958858624 | bytes 31489408 | tf_op jit(solution)/shard_map/while/body/eval_jaxpr/qhd,khd->hqk/dot_general | solution.py:54
  237.5 12.5 %fusion.193 = f32[6,784]{1,0:T(8,128)S(1)} fusion(f32[6,784,1568]{2,1,0:T(8,128)} %get-tuple-element.383, f32[6,784]{1,0:T(8,128)S(1)} %get-tuple-element.384), kind=kLoop, calls=%fused_computation.10.clone.1 | loop fusion | flops 22122912 | bytes 29541120 | tf_op jit(solution)/shard_map/while/body/eval_jaxpr/reduce_sum | solution.py:59
  250.0 14.4 %fusion.194 = bf16[784,6,64]{0,2,1:T(8,128)(2,1)} fusion(f32[6,784,1568]{2,1,0:T(8,128)} %get-tuple-element.383, f32[6,784]{1,0:T(8,128)S(1)} %fusion.193, f32[6,784]{1,0:T(8,128)S(1)} %get-tuple-element.384, bf16[2,1568,6,64]{1,3,2,0:T(8,128)(2,1)} %get-tuple-element.425, s32[]{:T(128)S(6)} %copy.88), kind=kOutput, calls=%fused_computation.17.clone.1 | convolution fusion | flops 973615104 | bytes 33227524 | tf_op jit(solution)/shard_map/while/body/eval_jaxpr/hqk,khd->qhd/dot_general | solution.py:62
  267.2 14.7 %multiply_reduce_fusion.17 = (f32[6,784]{1,0:T(8,128)S(1)}, f32[6,784,1568]{2,1,0:T(8,128)}) fusion(bf16[2,1568,6,64]{1,3,2,0:T(8,128)(2,1)S(1)} %get-tuple-element.427, s32[]{:T(128)S(6)} %copy.88, bf16[2,1568,6,64]{1,3,2,0:T(8,128)(2,1)} %get-tuple-element.426, s32[]{:T(128)S(6)} %add.904), kind=kOutput, calls=%fused_computation.8.clone.1 | convolution fusion | flops 958858624 | bytes 31489920 | tf_op jit(solution)/shard_map/while/body/eval_jaxpr/qhd,khd->hqk/dot_general | solution.py:54
  281.9 12.5 %fusion.191 = f32[6,784]{1,0:T(8,128)S(1)} fusion(f32[6,784,1568]{2,1,0:T(8,128)} %get-tuple-element.381, f32[6,784]{1,0:T(8,128)S(1)} %get-tuple-element.382), kind=kLoop, calls=%fused_computation.11.clone.1 | loop fusion | flops 22122912 | bytes 29541120 | tf_op jit(solution)/shard_map/while/body/eval_jaxpr/reduce_sum | solution.py:59
  294.5 14.4 %fusion.192 = bf16[784,6,64]{0,2,1:T(8,128)(2,1)} fusion(f32[6,784,1568]{2,1,0:T(8,128)} %get-tuple-element.381, f32[6,784]{1,0:T(8,128)S(1)} %fusion.191, f32[6,784]{1,0:T(8,128)S(1)} %get-tuple-element.382, bf16[2,1568,6,64]{1,3,2,0:T(8,128)(2,1)} %get-tuple-element.425, s32[]{:T(128)S(6)} %copy.88), kind=kOutput, calls=%fused_computation.16.clone.1 | convolution fusion | flops 973615104 | bytes 33227524 | tf_op jit(solution)/shard_map/while/body/eval_jaxpr/hqk,khd->qhd/dot_general | solution.py:62
  308.9 14.1 %multiply_reduce_fusion.18 = (f32[6,784]{1,0:T(8,128)S(1)}, f32[6,784,1568]{2,1,0:T(8,128)}) fusion(bf16[2,1568,6,64]{1,3,2,0:T(8,128)(2,1)S(1)} %get-tuple-element.427, s32[]{:T(128)S(6)} %copy.88, bf16[2,1568,6,64]{1,3,2,0:T(8,128)(2,1)} %get-tuple-element.426), kind=kOutput, calls=%fused_computation.9.clone.1 | convolution fusion | flops 958858624 | bytes 31489408 | tf_op jit(solution)/shard_map/while/body/eval_jaxpr/qhd,khd->hqk/dot_general | solution.py:54
  323.0 12.5 %fusion.193 = f32[6,784]{1,0:T(8,128)S(1)} fusion(f32[6,784,1568]{2,1,0:T(8,128)} %get-tuple-element.383, f32[6,784]{1,0:T(8,128)S(1)} %get-tuple-element.384), kind=kLoop, calls=%fused_computation.10.clone.1 | loop fusion | flops 22122912 | bytes 29541120 | tf_op jit(solution)/shard_map/while/body/eval_jaxpr/reduce_sum | solution.py:59
  335.5 14.4 %fusion.194 = bf16[784,6,64]{0,2,1:T(8,128)(2,1)} fusion(f32[6,784,1568]{2,1,0:T(8,128)} %get-tuple-element.383, f32[6,784]{1,0:T(8,128)S(1)} %fusion.193, f32[6,784]{1,0:T(8,128)S(1)} %get-tuple-element.384, bf16[2,1568,6,64]{1,3,2,0:T(8,128)(2,1)} %get-tuple-element.425, s32[]{:T(128)S(6)} %copy.88), kind=kOutput, calls=%fused_computation.17.clone.1 | convolution fusion | flops 973615104 | bytes 33227524 | tf_op jit(solution)/shard_map/while/body/eval_jaxpr/hqk,khd->qhd/dot_general | solution.py:62
  374.7 49.1 %fusion.76 = (bf16[3136,1536]{1,0:T(8,128)(2,1)}, f32[3136,1536]{1,0:T(8,128)}) fusion(f32[1536]{0:T(1024)S(1)} %copy-done.44, bf16[384,1536]{1,0:T(8,128)(2,1)} %all-gather.4.cloned.1.call-done, f32[3136,384]{1,0:T(8,128)} %copy-done.8, f32[384]{0:T(512)S(1)} %copy-done.53, f32[384]{0:T(512)S(1)} %copy-done.45, f32[3136]{0:T(1024)S(1)} %add_rsqrt_fusion, ...), kind=kOutput, calls=%fused_computation.102 | convolution fusion | flops 4023312384 | bytes 34932224 | tf_op jit(solution)/shard_map/dot_general | solution.py:222
  423.8 15.5 %fusion.135 = (bf16[1536]{0:T(1024)(128)(2,1)}, bf16[3136,1536]{1,0:T(8,128)(2,1)S(1)}) fusion(f32[3136,1536]{1,0:T(8,128)} %get-tuple-element.275, f32[1536]{0:T(1024)S(1)} %copy-done.44, bf16[1536,384]{1,0:T(8,128)(2,1)} %all-gather.6.cloned.1.call-done, bf16[3136,384]{1,0:T(8,128)(2,1)S(1)} %copy-done.19), kind=kOutput, calls=%fused_computation.275 | convolution fusion | flops 3760790016 | bytes 32498688 | tf_op jit(solution)/shard_map/rb,ab->ra/dot_general | solution.py:238
  474.3 418.7 %while.27 = (s32[]{:T(128)}, bf16[2,1568,6,64]{1,3,2,0:T(8,128)(2,1)}, bf16[2,1568,6,64]{1,3,2,0:T(8,128)(2,1)}, bf16[2,1568,6,64]{1,3,2,0:T(8,128)(2,1)}, bf16[...) while((s32[]{:T(128)}, ...), condition=%wide.region_16.17_spmd, body=%wide.region_13.16_spmd.sunk | while | flops 9623546880 | bytes 542753920 | solution.py:264
  493.7 13.8 %fusion.209 = f32[6,784,1568]{2,1,0:T(8,128)} fusion(bf16[2,1568,6,64]{1,3,2,0:T(8,128)(2,1)S(1)} %get-tuple-element.459, s32[]{:T(128)S(6)} %copy.99, bf16[2,1568,6,64]{1,3,2,0:T(8,128)(2,1)} %get-tuple-element.460), kind=kOutput, calls=%fused_computation.71.clone.1 | convolution fusion | flops 944111616 | bytes 31470592 | tf_op jit(solution)/shard_map/while/body/eval_jaxpr/qhd,khd->hqk/dot_general | solution.py:80
  507.5 14.2 %fusion.207 = f32[6,784,1568]{2,1,0:T(8,128)} fusion(bf16[2,1568,6,64]{1,3,2,0:T(8,128)(2,1)S(1)} %get-tuple-element.459, s32[]{:T(128)S(6)} %copy.99, bf16[2,1568,6,64]{1,3,2,0:T(8,128)(2,1)} %get-tuple-element.460, s32[]{:T(128)S(6)} %add.908), kind=kOutput, calls=%fused_computation.68.clone.1 | convolution fusion | flops 944111616 | bytes 31471104 | tf_op jit(solution)/shard_map/while/body/eval_jaxpr/qhd,khd->hqk/dot_general | solution.py:80
  521.7 12.1 %fusion.215 = f32[6,64,1568]{2,1,0:T(8,128)S(1)} fusion(f32[6,784,1568]{2,1,0:T(8,128)} %fusion.207, f32[6,784]{1,0:T(8,128)S(1)} %get-tuple-element.396, bf16[2,1568,6,64]{1,3,2,0:T(8,128)(2,1)S(1)} %copy-done.5, s32[]{:T(128)S(6)} %copy.99, s32[]{:T(128)S(6)} %add.908), kind=kOutput, calls=%fused_computation.48.clone.1 | convolution fusion | flops 966239232 | bytes 32628744 | tf_op jit(solution)/shard_map/while/body/eval_jaxpr/hqk,qhd->khd/dot_general | solution.py:85
  533.8 13.8 %fusion.216 = bf16[2,1568,6,64]{1,3,2,0:T(8,128)(2,1)} fusion(bf16[2,1568,6,64]{1,3,2,0:T(8,128)(2,1)} %get-tuple-element.446, s32[]{:T(128)S(6)} %copy.99, f32[6,64,1568]{2,1,0:T(8,128)S(1)} %fusion.215, f32[6,784,1568]{2,1,0:T(8,128)} %fusion.209, f32[6,784]{1,0:T(8,128)S(1)} %get-tuple-element.399, bf16[2,1568,6,64]{1,3,2,0:T(8,128)(2,1)S(1)} %copy-done.5), kind=kOutput, calls=%fused_computation.52.clone.1 | convolution fusion | flops 966841344 | bytes 36992000 | tf_op jit(solution)/shard_map/while/body/eval_jaxpr/hqk,qhd->khd/dot_general | solution.py:85
  547.7 25.3 %multiply_reduce_fusion.19 = (f32[6,784]{1,0:T(8,128)S(1)}, f32[6,784,1568]{2,1,0:T(8,128)}) fusion(f32[6,784,1568]{2,1,0:T(8,128)} %fusion.207, f32[6,784]{1,0:T(8,128)S(1)} %get-tuple-element.396, bf16[2,1568,6,64]{1,3,2,0:T(8,128)(2,1)} %get-tuple-element.463, s32[]{:T(128)S(6)} %copy.99, bf16[2,1568,6,64]{1,3,2,0:T(8,128)(2,1)S(1)} %copy-done.5, ...), kind=kOutput, calls=%fused_computation.41.clone.1 | convolution fusion | flops 973610368 | bytes 62828416 | tf_op jit(solution)/shard_map/while/body/eval_jaxpr/qhd,khd->hqk/dot_general | solution.py:88
  573.0 24.2 %multiply_reduce_fusion.20 = (f32[6,784]{1,0:T(8,128)S(1)}, f32[6,784,1568]{2,1,0:T(8,128)}) fusion(f32[6,784,1568]{2,1,0:T(8,128)} %fusion.209, f32[6,784]{1,0:T(8,128)S(1)} %get-tuple-element.399, bf16[2,1568,6,64]{1,3,2,0:T(8,128)(2,1)S(1)} %copy-done.6, s32[]{:T(128)S(6)} %copy.99, bf16[2,1568,6,64]{1,3,2,0:T(8,128)(2,1)S(1)} %copy-done.5), kind=kOutput, calls=%fused_computation.44.clone.1 | convolution fusion | flops 973610368 | bytes 61021568 | tf_op jit(solution)/shard_map/while/body/eval_jaxpr/qhd,khd->hqk/dot_general | solution.py:88
  597.1 50.4 %multiply_convert_fusion.3 = (bf16[6,784,1568]{2,1,0:T(8,128)(2,1)}, bf16[6,784,1568]{2,1,0:T(8,128)(2,1)}) fusion(f32[6,784,1568]{2,1,0:T(8,128)} %get-tuple-element.397, f32[6,784,1568]{2,1,0:T(8,128)} %fusion.207, f32[6,784]{1,0:T(8,128)S(1)} %get-tuple-element.398, f32[6,784]{1,0:T(8,128)S(1)} %get-tuple-element.396, ...), kind=kLoop, calls=%fused_computation.40.clone.1 | loop fusion | flops 73758720 | bytes 147592704 | tf_op jit(solution)/shard_map/while/body/eval_jaxpr/convert_element_type | solution.py:92
  647.6 11.0 fusion.210
  658.6 11.0 fusion.211
  690.7 13.8 %fusion.209 = f32[6,784,1568]{2,1,0:T(8,128)} fusion(bf16[2,1568,6,64]{1,3,2,0:T(8,128)(2,1)S(1)} %get-tuple-element.459, s32[]{:T(128)S(6)} %copy.99, bf16[2,1568,6,64]{1,3,2,0:T(8,128)(2,1)} %get-tuple-element.460), kind=kOutput, calls=%fused_computation.71.clone.1 | convolution fusion | flops 944111616 | bytes 31470592 | tf_op jit(solution)/shard_map/while/body/eval_jaxpr/qhd,khd->hqk/dot_general | solution.py:80
  704.5 14.2 %fusion.207 = f32[6,784,1568]{2,1,0:T(8,128)} fusion(bf16[2,1568,6,64]{1,3,2,0:T(8,128)(2,1)S(1)} %get-tuple-element.459, s32[]{:T(128)S(6)} %copy.99, bf16[2,1568,6,64]{1,3,2,0:T(8,128)(2,1)} %get-tuple-element.460, s32[]{:T(128)S(6)} %add.908), kind=kOutput, calls=%fused_computation.68.clone.1 | convolution fusion | flops 944111616 | bytes 31471104 | tf_op jit(solution)/shard_map/while/body/eval_jaxpr/qhd,khd->hqk/dot_general | solution.py:80
  718.8 12.1 %fusion.215 = f32[6,64,1568]{2,1,0:T(8,128)S(1)} fusion(f32[6,784,1568]{2,1,0:T(8,128)} %fusion.207, f32[6,784]{1,0:T(8,128)S(1)} %get-tuple-element.396, bf16[2,1568,6,64]{1,3,2,0:T(8,128)(2,1)S(1)} %copy-done.5, s32[]{:T(128)S(6)} %copy.99, s32[]{:T(128)S(6)} %add.908), kind=kOutput, calls=%fused_computation.48.clone.1 | convolution fusion | flops 966239232 | bytes 32628744 | tf_op jit(solution)/shard_map/while/body/eval_jaxpr/hqk,qhd->khd/dot_general | solution.py:85
  730.8 13.8 %fusion.216 = bf16[2,1568,6,64]{1,3,2,0:T(8,128)(2,1)} fusion(bf16[2,1568,6,64]{1,3,2,0:T(8,128)(2,1)} %get-tuple-element.446, s32[]{:T(128)S(6)} %copy.99, f32[6,64,1568]{2,1,0:T(8,128)S(1)} %fusion.215, f32[6,784,1568]{2,1,0:T(8,128)} %fusion.209, f32[6,784]{1,0:T(8,128)S(1)} %get-tuple-element.399, bf16[2,1568,6,64]{1,3,2,0:T(8,128)(2,1)S(1)} %copy-done.5), kind=kOutput, calls=%fused_computation.52.clone.1 | convolution fusion | flops 966841344 | bytes 36992000 | tf_op jit(solution)/shard_map/while/body/eval_jaxpr/hqk,qhd->khd/dot_general | solution.py:85
  744.7 25.3 %multiply_reduce_fusion.19 = (f32[6,784]{1,0:T(8,128)S(1)}, f32[6,784,1568]{2,1,0:T(8,128)}) fusion(f32[6,784,1568]{2,1,0:T(8,128)} %fusion.207, f32[6,784]{1,0:T(8,128)S(1)} %get-tuple-element.396, bf16[2,1568,6,64]{1,3,2,0:T(8,128)(2,1)} %get-tuple-element.463, s32[]{:T(128)S(6)} %copy.99, bf16[2,1568,6,64]{1,3,2,0:T(8,128)(2,1)S(1)} %copy-done.5, ...), kind=kOutput, calls=%fused_computation.41.clone.1 | convolution fusion | flops 973610368 | bytes 62828416 | tf_op jit(solution)/shard_map/while/body/eval_jaxpr/qhd,khd->hqk/dot_general | solution.py:88
  770.0 24.2 %multiply_reduce_fusion.20 = (f32[6,784]{1,0:T(8,128)S(1)}, f32[6,784,1568]{2,1,0:T(8,128)}) fusion(f32[6,784,1568]{2,1,0:T(8,128)} %fusion.209, f32[6,784]{1,0:T(8,128)S(1)} %get-tuple-element.399, bf16[2,1568,6,64]{1,3,2,0:T(8,128)(2,1)S(1)} %copy-done.6, s32[]{:T(128)S(6)} %copy.99, bf16[2,1568,6,64]{1,3,2,0:T(8,128)(2,1)S(1)} %copy-done.5), kind=kOutput, calls=%fused_computation.44.clone.1 | convolution fusion | flops 973610368 | bytes 61021568 | tf_op jit(solution)/shard_map/while/body/eval_jaxpr/qhd,khd->hqk/dot_general | solution.py:88
  794.1 50.4 %multiply_convert_fusion.3 = (bf16[6,784,1568]{2,1,0:T(8,128)(2,1)}, bf16[6,784,1568]{2,1,0:T(8,128)(2,1)}) fusion(f32[6,784,1568]{2,1,0:T(8,128)} %get-tuple-element.397, f32[6,784,1568]{2,1,0:T(8,128)} %fusion.207, f32[6,784]{1,0:T(8,128)S(1)} %get-tuple-element.398, f32[6,784]{1,0:T(8,128)S(1)} %get-tuple-element.396, ...), kind=kLoop, calls=%fused_computation.40.clone.1 | loop fusion | flops 73758720 | bytes 147592704 | tf_op jit(solution)/shard_map/while/body/eval_jaxpr/convert_element_type | solution.py:92
  855.6 11.0 fusion.211
  897.2 17.0 %copy.71 = bf16[2,1568,3,6,64]{1,0,4,3,2:T(2,128)(2,1)} copy(bf16[2,1568,3,6,64]{1,4,3,0,2:T(8,128)(2,1)S(1)} %pad_maximum_fusion) | data formatting | bytes 14450688 | tf_op jit(solution)/shard_map/stack | solution.py:268
  914.3 15.7 %convert_element_type.272 = bf16[3136,1152]{0,1:T(8,128)(2,1)} reshape(bf16[2,1568,3,6,64]{1,0,4,3,2:T(2,128)(2,1)} %copy.71) | data formatting | bytes 14450688 | tf_op jit(solution)/shard_map/convert_element_type | solution.py:270
  930.0 12.4 %multiply_reduce_fusion.5 = (bf16[384]{0:T(512)(128)(2,1)S(1)}, f32[3136]{0:T(1024)S(1)}, f32[3136]{0:T(1024)S(1)}, bf16[384]{0:T(512)(128)(2,1)S(1)}, f32[3136,384]{1,0:T(8,128)S(1)}) fusion(f32[3136,384]{1,0:T(8,128)} %get-tuple-element.271, f32[3136]{0:T(1024)S(1)} %copy-done.35, f32[3136]{0:T(1024)S(1)} %copy-done.29, f32[384]{0:T(512)S(1)} %copy-done.43, ...), kind=kOutput, calls=%fused_computation.137 | convolution fusion | flops 2785362944 | bytes 17797120 | tf_op jit(solution)/shard_map/rb,ab->ra/dot_general | solution.py:278
  1009.8 18.9 %all-reduce.21 = (bf16[384]{0:T(512)(128)(2,1)S(1)}, bf16[384]{0:T(512)(128)(2,1)S(1)}, bf16[384]{0:T(512)(128)(2,1)S(1)}, bf16[384]{0:T(512)(128)(2,1)S(1)}, bf...) all-reduce(bf16[384]{0:T(512)(128)(2,1)S(1)} %dynamic-update-slice., ...), channel_id=1, replica_groups=mesh['clip'=8,'wt'=4] {'wt'}, use_global_device_ids=true, to_apply=%add.8 | all-reduce | flops 5376 | bytes 21504
  1031.5 30.2 %reduce-scatter.14.cloned.1.call-done = bf16[384,384]{1,0:T(8,128)(2,1)} async-done(((bf16[1536,384]{1,0:T(8,128)(2,1)}), bf16[384,384]{1,0:T(8,128)(2,1)}) %reduce-scatter.14.cloned.1.call-update) | async-done | bytes 294928 | tf_op jit(solution)/shard_map/reduce_scatter | solution.py:364
  1061.8 11.0 fusion.94
  1073.6 13.8 %all-reduce.19 = (bf16[96]{0:T(256)(128)(2,1)S(1)}, bf16[96]{0:T(256)(128)(2,1)S(1)}, bf16[96]{0:T(256)(128)(2,1)S(1)}, bf16[96]{0:T(256)(128)(2,1)S(1)}, bf16[9...) all-reduce(bf16[96]{0:T(256)(128)(2,1)S(1)} %dynamic-slice.10, ...), channel_id=1, replica_groups=mesh['clip'=8,'wt'=4] {'clip'}, use_global_device_ids=true, to_apply=%region_23.24 | all-reduce | flops 1248 | bytes 4992 | tf_op jit(solution)/shard_map/psum | solution.py:373
  1095.5 26.4 %all-reduce.25.cloned.1.call-done = (bf16[192,384]{1,0:T(8,128)(2,1)}, bf16[96,1152]{1,0:T(8,128)(2,1)}, bf16[96,384]{1,0:T(8,128)(2,1)}, bf16[96,1536]{1,0:T(8,128)(2,1)}, bf16[384,384]{1,0:T(8,128)(2,1)}) async-done(((bf16[192,384]{1,0:T(8,128)(2,1)}, bf16[96,1152]{1,0:T(8,128)(2,1)}, bf16[96,384]{1,0:T(8,128)(2,1)}, bf16[96,1536]{1,0:T(8,128)(2,1)}, bf16[384,384]{1,0:T(8,128)(2,1)}), ...) | async-done | bytes 1032208 | tf_op jit(solution)/shard_map/psum | solution.py:372
  (347 shorter events, 269.9 us)
Async XLA Ops:
  7.2 12.2 %copy-start.65 = (bf16[96]{0:T(256)(128)(2,1)S(1)}, bf16[96]{0:T(256)(128)(2,1)}, u32[]{:S(2)}) copy-start(bf16[96]{0:T(256)(128)(2,1)} %param.34) | copy-start | bytes 580
  7.2 12.5 %copy-start.66 = (bf16[96]{0:T(256)(128)(2,1)S(1)}, bf16[96]{0:T(256)(128)(2,1)}, u32[]{:S(2)}) copy-start(bf16[96]{0:T(256)(128)(2,1)} %param.32) | copy-start | bytes 580
  7.3 12.7 %copy-start.67 = (bf16[96]{0:T(256)(128)(2,1)S(1)}, bf16[96]{0:T(256)(128)(2,1)}, u32[]{:S(2)}) copy-start(bf16[96]{0:T(256)(128)(2,1)} %param.26) | copy-start | bytes 580
  7.3 12.9 %copy-start.68 = (bf16[96]{0:T(256)(128)(2,1)S(1)}, bf16[96]{0:T(256)(128)(2,1)}, u32[]{:S(2)}) copy-start(bf16[96]{0:T(256)(128)(2,1)} %param.27) | copy-start | bytes 580
  7.3 13.2 %copy-start.69 = (bf16[96]{0:T(256)(128)(2,1)S(1)}, bf16[96]{0:T(256)(128)(2,1)}, u32[]{:S(2)}) copy-start(bf16[96]{0:T(256)(128)(2,1)} %param.29) | copy-start | bytes 580
  7.3 13.4 %copy-start.70 = (bf16[96]{0:T(256)(128)(2,1)S(1)}, bf16[96]{0:T(256)(128)(2,1)}, u32[]{:S(2)}) copy-start(bf16[96]{0:T(256)(128)(2,1)} %param.30) | copy-start | bytes 580
  7.3 13.7 %copy-start.71 = (bf16[96]{0:T(256)(128)(2,1)S(1)}, bf16[96]{0:T(256)(128)(2,1)}, u32[]{:S(2)}) copy-start(bf16[96]{0:T(256)(128)(2,1)} %param.25) | copy-start | bytes 580
  7.3 26.9 %copy-start.60 = (bf16[384]{0:T(512)(128)(2,1)S(1)}, bf16[384]{0:T(512)(128)(2,1)}, u32[]{:S(2)}) copy-start(bf16[384]{0:T(512)(128)(2,1)} %param.36) | copy-start | bytes 2308
  7.3 28.7 %copy-start.57 = (s32[2,157]{1,0:T(2,128)S(1)}, s32[2,157]{1,0:T(2,128)}, u32[]{:S(2)}) copy-start(s32[2,157]{1,0:T(2,128)} %param.23) | copy-start | bytes 3772
  7.3 46.0 %copy-start.30 = (bf16[192,384]{1,0:T(8,128)(2,1)S(1)}, bf16[192,384]{1,0:T(8,128)(2,1)}, u32[]{:S(2)}) copy-start(bf16[192,384]{1,0:T(8,128)(2,1)} %param.24) | copy-start | bytes 442372
  7.3 367.3 %all-gather.4.cloned.1.call-start = ((), (), s32[]{:S(2)}) async-start(), calls=%async_computation.7 | async-start | bytes 1474560 | tf_op jit(solution)/shard_map/all_gather | solution.py:180
  8.1 66.9 %copy-start.38 = (s32[8]{0:T(128)}, s32[8]{0:T(128)S(1)}, u32[]{:S(2)}) copy-start(s32[8]{0:T(128)S(1)} %get-tuple-element.280) | copy-start | bytes 100
  10.4 73.1 %copy-start.33 = (bf16[96,384]{1,0:T(8,128)(2,1)S(1)}, bf16[96,384]{1,0:T(8,128)(2,1)}, u32[]{:S(2)}) copy-start(bf16[96,384]{1,0:T(8,128)(2,1)} %param.31) | copy-start | bytes 221188
  11.5 105.9 %all-to-all-start = ((bf16[8,40,768]{2,1,0:T(8,128)(2,1)}), bf16[8,40,768]{2,1,0:T(8,128)(2,1)}, u32[]{:S(2)}, u32[]{:S(2)}) async-start(bf16[8,40,768]{2,1,0:T(8,128)(2,1)} %select_select_fusion), calls=%async_computation | async-start | bytes 983040 | tf_op jit(solution)/shard_map/all_to_all | solution.py:144
  16.6 407.1 %all-gather.6.cloned.1.call-start = ((), (), s32[]{:S(2)}) async-start(), calls=%async_computation.8 | async-start | bytes 1474560 | tf_op jit(solution)/shard_map/all_gather | solution.py:182
  17.4 1011.4 %reduce-scatter.10.cloned.1.call-start = ((), (), s32[]{:S(2)}) async-start(), calls=%async_computation.11 | async-start | bytes 368640 | tf_op jit(solution)/shard_map/reduce_scatter | solution.py:346
  17.9 101.9 %copy-start.50 = (pred[320]{0:T(512)(128)(4,1)}, pred[320]{0:T(512)(128)(4,1)S(1)}, u32[]{:S(2)}) copy-start(pred[320]{0:T(512)(128)(4,1)S(1)} %reshape.717) | copy-start | bytes 964
  34.2 96.5 %copy-start.42 = (f32[384]{0:T(512)}, f32[384]{0:T(512)S(1)}, u32[]{:S(2)}) copy-start(f32[384]{0:T(512)S(1)} %convert_element_type.251) | copy-start | bytes 4612
  34.8 95.9 %copy-start.55 = (f32[384]{0:T(512)}, f32[384]{0:T(512)S(1)}, u32[]{:S(2)}) copy-start(f32[384]{0:T(512)S(1)} %convert_element_type.252) | copy-start | bytes 4612
  53.3 66.5 %copy-start.26 = (f32[3136]{0:T(1024)}, f32[3136]{0:T(1024)S(1)}, u32[]{:S(2)}) copy-start(f32[3136]{0:T(1024)S(1)} %convert_subtract_fusion) | copy-start | bytes 37636
  75.0 44.9 %copy-start.21 = (bf16[768,384]{1,0:T(8,128)(2,1)}, bf16[768,384]{1,0:T(8,128)(2,1)S(1)}, u32[]{:S(2)}) copy-start(bf16[768,384]{1,0:T(8,128)(2,1)S(1)} %all_gather.45) | copy-start | bytes 1769476
  353.6 12.9 %copy-start.2 = (bf16[2,1568,6,64]{1,3,2,0:T(8,128)(2,1)}, bf16[2,1568,6,64]{1,3,2,0:T(8,128)(2,1)S(1)}, u32[]{:S(2)}) copy-start(bf16[2,1568,6,64]{1,3,2,0:T(8,128)(2,1)S(1)} %get-tuple-element.484) | copy-start | bytes 7225348
  353.6 12.9 %copy-start.17 = (bf16[384,384]{1,0:T(8,128)(2,1)S(1)}, bf16[384,384]{1,0:T(8,128)(2,1)}, u32[]{:S(2)}) copy-start(bf16[384,384]{1,0:T(8,128)(2,1)} %all_gather.52) | copy-start | bytes 884740
  353.6 12.9 %copy-start.40 = (f32[384]{0:T(512)S(1)}, f32[384]{0:T(512)}, u32[]{:S(2)}) copy-start(f32[384]{0:T(512)} %convert_element_type.259) | copy-start | bytes 4612
  371.5 74.2 %copy-start.31 = (f32[3136]{0:T(1024)}, f32[3136]{0:T(1024)S(1)}, u32[]{:S(2)}) copy-start(f32[3136]{0:T(1024)S(1)} %broadcast_multiply_fusion.4) | copy-start | bytes 37636
  374.6 71.1 %copy-start.36 = (f32[3136]{0:T(1024)}, f32[3136]{0:T(1024)S(1)}, u32[]{:S(2)}) copy-start(f32[3136]{0:T(1024)S(1)} %add_rsqrt_fusion) | copy-start | bytes 37636
  374.6 49.1 %copy-start.19 = (bf16[3136,384]{1,0:T(8,128)(2,1)S(1)}, bf16[3136,384]{1,0:T(8,128)(2,1)}, u32[]{:S(2)}) copy-start(bf16[3136,384]{1,0:T(8,128)(2,1)} %param.39) | copy-start | bytes 7225348
  423.8 15.5 %copy-start.9 = (f32[3136,384]{1,0:T(8,128)S(1)}, f32[3136,384]{1,0:T(8,128)}, u32[]{:S(2)}) copy-start(f32[3136,384]{1,0:T(8,128)} %copy-done.8) | copy-start | bytes 14450692
  423.8 15.5 %copy-start.63 = (bf16[384,1536]{1,0:T(8,128)(2,1)S(1)}, bf16[384,1536]{1,0:T(8,128)(2,1)}, u32[]{:S(2)}) copy-start(bf16[384,1536]{1,0:T(8,128)(2,1)} %all-gather.4.cloned.1.call-done) | copy-start | bytes 3538948
  457.3 571.5 %reduce-scatter.6.cloned.1.call-start = ((), (), s32[]{:S(2)}) async-start(), calls=%async_computation.9 | async-start | bytes 737280 | tf_op jit(solution)/shard_map/reduce_scatter | solution.py:325
  507.5 14.2 %copy-start.5 = (bf16[2,1568,6,64]{1,3,2,0:T(8,128)(2,1)S(1)}, bf16[2,1568,6,64]{1,3,2,0:T(8,128)(2,1)}, u32[]{:S(2)}) copy-start(bf16[2,1568,6,64]{1,3,2,0:T(8,128)(2,1)} %get-tuple-element.462) | copy-start | bytes 7225348 | tf_op jit(solution)/shard_map/while
  547.7 25.3 %copy-start.6 = (bf16[2,1568,6,64]{1,3,2,0:T(8,128)(2,1)S(1)}, bf16[2,1568,6,64]{1,3,2,0:T(8,128)(2,1)}, u32[]{:S(2)}) copy-start(bf16[2,1568,6,64]{1,3,2,0:T(8,128)(2,1)} %get-tuple-element.463) | copy-start | bytes 7225348 | tf_op jit(solution)/shard_map/while
  704.5 14.2 %copy-start.5 = (bf16[2,1568,6,64]{1,3,2,0:T(8,128)(2,1)S(1)}, bf16[2,1568,6,64]{1,3,2,0:T(8,128)(2,1)}, u32[]{:S(2)}) copy-start(bf16[2,1568,6,64]{1,3,2,0:T(8,128)(2,1)} %get-tuple-element.462) | copy-start | bytes 7225348 | tf_op jit(solution)/shard_map/while
  744.7 25.3 %copy-start.6 = (bf16[2,1568,6,64]{1,3,2,0:T(8,128)(2,1)S(1)}, bf16[2,1568,6,64]{1,3,2,0:T(8,128)(2,1)}, u32[]{:S(2)}) copy-start(bf16[2,1568,6,64]{1,3,2,0:T(8,128)(2,1)} %get-tuple-element.463) | copy-start | bytes 7225348 | tf_op jit(solution)/shard_map/while
  914.3 15.7 %copy-start.24 = (bf16[384,1152]{1,0:T(8,128)(2,1)S(1)}, bf16[384,1152]{1,0:T(8,128)(2,1)}, u32[]{:S(2)}) copy-start(bf16[384,1152]{1,0:T(8,128)(2,1)} %all_gather.49) | copy-start | bytes 2654212
  914.3 15.7 %copy-start.29 = (f32[3136]{0:T(1024)S(1)}, f32[3136]{0:T(1024)}, u32[]{:S(2)}) copy-start(f32[3136]{0:T(1024)} %copy-done.28) | copy-start | bytes 37636
  914.3 15.7 %copy-start.35 = (f32[3136]{0:T(1024)S(1)}, f32[3136]{0:T(1024)}, u32[]{:S(2)}) copy-start(f32[3136]{0:T(1024)} %copy-done.34) | copy-start | bytes 37636
  914.3 15.7 %copy-start.43 = (f32[384]{0:T(512)S(1)}, f32[384]{0:T(512)}, u32[]{:S(2)}) copy-start(f32[384]{0:T(512)} %copy-done.42) | copy-start | bytes 4612
  914.3 28.2 %slice-start = ((s8[4816896]{0:T(1024)(128)(4,1)}), s8[622592]{0:T(1024)(128)(4,1)S(1)}, s32[]{:S(2)}) async-start(s8[4816896]{0:T(1024)(128)(4,1)} %bitcast.227), calls=%async_computation.15 | async-start | bytes 1245184
  930.0 12.5 %slice-start.1 = ((s8[4816896]{0:T(1024)(128)(4,1)}), s8[4194304]{0:T(1024)(128)(4,1)S(1)}, s32[]{:S(2)}) async-start(s8[4816896]{0:T(1024)(128)(4,1)} %bitcast.227), calls=%async_computation.16 | async-start | bytes 8388608
  930.0 12.5 %copy-start.27 = (f32[3136]{0:T(1024)S(1)}, f32[3136]{0:T(1024)}, u32[]{:S(2)}) copy-start(f32[3136]{0:T(1024)} %copy-done.26) | copy-start | bytes 37636
  953.0 75.8 %reduce-scatter.8.cloned.1.call-start = ((), (), s32[]{:S(2)}) async-start(), calls=%async_computation.10 | async-start | bytes 1105920 | tf_op jit(solution)/shard_map/reduce_scatter | solution.py:337
  963.3 68.2 %reduce-scatter.12.cloned.1.call-start = ((), (), s32[]{:S(2)}) async-start(), calls=%async_computation.12 | async-start | bytes 1474560 | tf_op jit(solution)/shard_map/reduce_scatter | solution.py:358
  974.2 87.5 %reduce-scatter.14.cloned.1.call-start = ((), (), s32[]{:S(2)}) async-start(), calls=%async_computation.13 | async-start | bytes 1474560 | tf_op jit(solution)/shard_map/reduce_scatter | solution.py:364
  1001.3 91.2 %all-to-all-start.1 = ((bf16[8,40,768]{2,1,0:T(8,128)(2,1)}), bf16[8,40,768]{2,1,0:T(8,128)(2,1)S(1)}, u32[]{:S(2)}, u32[]{:S(2)}) async-start(bf16[8,40,768]{2,1,0:T(8,128)(2,1)} %bitcast.40), calls=%async_computation.1 | async-start | bytes 983040 | tf_op jit(solution)/shard_map/all_to_all | solution.py:294
  1004.8 56.9 %copy-start.62 = (bf16[1536,384]{1,0:T(8,128)(2,1)S(1)}, bf16[1536,384]{1,0:T(8,128)(2,1)}, u32[]{:S(2)}) copy-start(bf16[1536,384]{1,0:T(8,128)(2,1)} %all-gather.6.cloned.1.call-done) | copy-start | bytes 3538948
  1004.8 117.1 %all-reduce.25.cloned.1.call-start = ((), (), s32[]{:S(2)}) async-start(), calls=%async_computation.14 | async-start | bytes 2064384 | tf_op jit(solution)/shard_map/psum | solution.py:372
  1061.7 68.8 %copy-start.1 = (bf16[314,768]{1,0:T(8,128)(2,1)S(1)}, bf16[314,768]{1,0:T(8,128)(2,1)}, u32[]{:S(2)}) copy-start(bf16[314,768]{1,0:T(8,128)(2,1)} %param.22) | copy-start | bytes 1446916
  (46 other events, 308.6 us)
Sparse Core Ops, SparseCore 0:
  9.7 33.6 all-gather.3
  45.0 38.4 all-gather.5
  457.4 19.5 reduce-scatter.9
  953.1 21.6 reduce-scatter.5
  976.9 22.9 reduce-scatter.7
  1002.6 28.7 reduce-scatter.11
  1033.8 27.8 reduce-scatter.13
  1065.5 56.4 all-reduce.24
where the time goes:
time: 1150 us; the launch traced here: 1140 us
  matrix products  554 us (48%)
  other arithmetic  223 us (19%)
  local copies, waits for them, and re-layouts  134 us (12%)
  blocking collectives  113 us (10%)
  waiting for transfers between devices  60.9 us (5%)
  loops' own time  25.5 us (2%)
  between operations  17.5 us (2%)
    convert_element_type x2, other arithmetic, attend_back(): grad_scores = (probs_half * (grad_weights - inner_sum)).astype(jnp.bfloat16)  101 us
    dot_general x4, matrix products, attend_back(): jnp.einsum('qhd,khd->hqk', upward_half, value_rows, preferred_element_typ...  98.9 us
    dot_general x4, matrix products, attend_forward(): jnp.einsum('hqk,khd->qhd', weights, value_rows, preferred_element_type=jn...  57.7 us
    dot_general x4, matrix products, attend_forward(): jnp.einsum('qhd,khd->hqk', query_half, key_rows, preferred_element_type=j...  57.6 us
    dot_general x4, matrix products, attend_back(): jnp.einsum('qhd,khd->hqk', query_half, key_rows, preferred_element_type=j...  56.1 us
    dot_general x4, matrix products, attend_back(): jnp.einsum('hqk,qhd->khd', weights, upward_half, preferred_element_type=j...  51.8 us
    reduce_sum x4, other arithmetic, attend_forward(): row_total = jnp.sum(shifted, -1, keepdims=True)  50.1 us
    dot_general x1, matrix products, per_device(): jnp.dot(normed_second, expand_full, preferred_element_type=jnp.float32)  49.1 us
  transfers between devices with their start and end apart: 10, of which 3 were waited for; matrix products, arithmetic and copies ran while one was open for 76% of the time, Pallas kernels for 0%

commit v1 on v0

v1 whole, which is shorter than its diff:
```python
import math

import jax
import jax.numpy as jnp
import numpy as np
from jax import lax
from jax.experimental import pallas as pl
from jax.experimental.pallas import tpu as pltpu
from jax.sharding import PartitionSpec as P

H = 6
HEAD = 64
L = 1568
LANES = 128
LP = -(-L // LANES) * LANES
EPSILON = 1e-06
LOG2E = math.log2(math.e)
Q_SCALE = LOG2E / math.sqrt(HEAD)
ROOT_HALF = math.sqrt(0.5)
INV_ROOT_TWO_PI = 1.0 / math.sqrt(2.0 * math.pi)
SAFE_EXPONENT = 100.0
VMEM_LIMIT = 60 * 2**20
FFC = 256
Q_BLOCKS = ((0, 896), (896, LP - 896))
F32 = jnp.float32
BF16 = jnp.bfloat16


def params(**kw):
    return pltpu.CompilerParams(vmem_limit_bytes=VMEM_LIMIT, **kw)


def dg(a, b, ca, cb):
    return lax.dot_general(a, b, (((ca,), (cb,)), ((), ())), preferred_element_type=F32)


def position_table(width):
    places = np.arange(L, dtype=np.float64)[None, :]
    columns = np.arange(width)
    exponent = (2 * (columns // 2)).astype(np.float64) / width
    angles = places / np.power(10000.0, exponent)[:, None]
    return np.where(columns[:, None] % 2 == 0, np.sin(angles), np.cos(angles)).astype(np.float32)


def norm_stats(x):
    center = x - jnp.mean(x, 0, keepdims=True)
    recip = lax.rsqrt(jnp.mean(center * center, 0, keepdims=True) + EPSILON)
    return center * recip, recip


def norm_back(e, scaled, recip, gain):
    lifted = e * gain
    return recip * (
        lifted
        - jnp.mean(lifted, 0, keepdims=True)
        - scaled * jnp.mean(lifted * scaled, 0, keepdims=True)
    )


def split3(x):
    hi = x.astype(BF16)
    rest = x - hi.astype(F32)
    mid = rest.astype(BF16)
    low = (rest - mid.astype(F32)).astype(BF16)
    return hi, mid, low


def aug_rows(x):
    hi, mid, low = split3(x)
    row = lax.broadcasted_iota(jnp.int32, (16, x.shape[1]), 0)
    zero = jnp.zeros((16, x.shape[1]), F32)
    out = jnp.where(row == 0, hi.astype(F32), zero)
    out = jnp.where(row == 1, mid.astype(F32), out)
    out = jnp.where(row == 2, low.astype(F32), out)
    return out.astype(BF16)


def one_hot(target_ref, copy):
    place = lax.broadcasted_iota(jnp.int32, (target_ref.shape[0], L), 1)
    return (target_ref[...] - copy * L == place).astype(F32)


def pre_kernel(arrived, target, wp, cols, pos, win, bin_col, stream_out, q_out, kv_out, k_rows, v_rows):
    copy = pl.program_id(0)
    width = wp.shape[1]
    proj = dg(arrived[...], wp[...], 1, 0).astype(BF16)
    hot = one_hot(target, copy)
    covered = jnp.sum(hot, 0, keepdims=True)
    stream = dg(proj, hot.astype(BF16), 0, 0) + (1.0 - covered) * cols[:, 0:1] + pos[...]
    stream_out[0] = stream
    scaled, _ = norm_stats(stream)
    normed = (scaled * cols[:, 1:2] + cols[:, 2:3]).astype(BF16)
    lane = lax.broadcasted_iota(jnp.int32, (L, LANES), 1)
    ones = (lane < HEAD + 3).astype(BF16)
    for part in range(3):
        sl = slice(part * width, (part + 1) * width)
        mixed = dg(win[:, sl], normed, 0, 0) + bin_col[sl, :]
        if part == 0:
            q_out[0, :, :L] = (mixed * Q_SCALE).astype(BF16)
            q_out[0, :, L:] = jnp.zeros((width, LP - L), BF16)
        else:
            mixed = mixed.astype(BF16)
            kv_out[0, (part - 1) * width : part * width, :] = mixed
            dst = k_rows if part == 1 else v_rows
            for h in range(H):
                dst[0, h] = ones
                dst[0, h, :, :HEAD] = mixed[h * HEAD : (h + 1) * HEAD].T


def pre(arrived, target, wp, cols, pos, win, bin_col):
    a, e = arrived.shape
    d = wp.shape[1]
    const = lambda *s: pl.BlockSpec(s, lambda c: (0,) * len(s))
    lead = lambda *s: pl.BlockSpec((1,) + s, lambda c: (c,) + (0,) * len(s))
    return pl.pallas_call(
        pre_kernel,
        grid=(2,),
        in_specs=[const(a, e), const(a, 1), const(e, d), const(d, 8), const(d, L), const(d, 3 * d), const(3 * d, 1)],
        out_specs=[lead(d, L), lead(d, LP), lead(2 * d, L), lead(H, L, LANES), lead(H, L, LANES)],
        out_shape=[
            jax.ShapeDtypeStruct((2, d, L), F32),
            jax.ShapeDtypeStruct((2, d, LP), BF16),
            jax.ShapeDtypeStruct((2, 2 * d, L), BF16),
            jax.ShapeDtypeStruct((2, H, L, LANES), BF16),
            jax.ShapeDtypeStruct((2, H, L, LANES), BF16),
        ],
        compiler_params=params(),
    )(arrived, target, wp, cols, pos, win, bin_col)


def attend_kernel(k_rows, q, kt, vt, o_out, lse_out, v_aug):
    row = lax.broadcasted_iota(jnp.int32, (16, L), 0)
    v_aug[:HEAD] = vt[0]
    v_aug[HEAD:] = (row == 0).astype(F32).astype(BF16)
    qf = q[0].astype(F32)
    kf = kt[0].astype(F32)
    bound = jnp.max(jnp.sum(qf * qf, 0, keepdims=True)) * jnp.max(jnp.sum(kf * kf, 0, keepdims=True))
    safe = bound <= SAFE_EXPONENT * SAFE_EXPONENT

    def run(shift):
        for start, size in Q_BLOCKS:
            sl = slice(start, start + size)
            s = dg(k_rows[0, 0, :, :HEAD], q[0, :, sl], 1, 0)
            top = 0.0
            if shift:
                top = jnp.max(s, 0, keepdims=True)
                s = s - top
            e = jnp.exp2(s).astype(BF16)
            o = dg(v_aug[...], e, 1, 0)
            total = o[HEAD : HEAD + 1]
            o_out[0, :, sl] = o[:HEAD] * (1.0 / total)
            lse_out[0, 0, :, sl] = aug_rows(-(top + jnp.log2(total)))

    pl.when(safe)(lambda: run(False))
    pl.when(jnp.logical_not(safe))(lambda: run(True))


def attend(k_rows, q, kv):
    d = q.shape[1]
    head = lambda off: (lambda i: (i // H, i % H + off, 0))
    return pl.pallas_call(
        attend_kernel,
        grid=(2 * H,),
        in_specs=[
            pl.BlockSpec((1, 1, L, LANES), lambda i: (i // H, i % H, 0, 0)),
            pl.BlockSpec((1, HEAD, LP), head(0)),
            pl.BlockSpec((1, HEAD, L), head(0)),
            pl.BlockSpec((1, HEAD, L), head(H)),
        ],
        out_specs=[
            pl.BlockSpec((1, HEAD, LP), head(0)),
            pl.BlockSpec((1, 1, 16, LP), lambda i: (i // H, i % H, 0, 0)),
        ],
        out_shape=[
            jax.ShapeDtypeStruct((2, d, LP), F32),
            jax.ShapeDtypeStruct((2, H, 16, LP), BF16),
        ],
        scratch_shapes=[pltpu.VMEM((HEAD + 16, L), BF16)],
        compiler_params=params(),
    )(k_rows, q, kv, kv)


def attend_back_kernel(k_rows, v_rows, q, lse, do, dsum, kt, dq, dk, dv, q_aug, do_aug):
    q_aug[:HEAD] = q[0]
    q_aug[HEAD : HEAD + 16] = lse[0, 0]
    q_aug[HEAD + 16 :] = jnp.zeros((LANES - HEAD - 16, LP), BF16)
    do_aug[:HEAD] = do[0]
    do_aug[HEAD : HEAD + 16] = dsum[0, 0]
    do_aug[HEAD + 16 :] = jnp.zeros((LANES - HEAD - 16, LP), BF16)
    k_sum = None
    v_sum = None
    for start, size in Q_BLOCKS:
        sl = slice(start, start + size)
        p = jnp.exp2(dg(k_rows[0, 0], q_aug[:, sl], 1, 0))
        dp = dg(v_rows[0, 0], do_aug[:, sl], 1, 0)
        ds = (p * dp).astype(BF16)
        v_part = dg(do_aug[:HEAD, sl], p.astype(BF16), 1, 1)
        k_part = dg(q_aug[:HEAD, sl], ds, 1, 1)
        v_sum = v_part if v_sum is None else v_sum + v_part
        k_sum = k_part if k_sum is None else k_sum + k_part
        if start + size == LP:
            dq[0, :, start:] = (dg(kt[0], ds, 1, 0)[:, : L - start] * (1.0 / math.sqrt(HEAD))).astype(BF16)
        else:
            dq[0, :, sl] = (dg(kt[0], ds, 1, 0) * (1.0 / math.sqrt(HEAD))).astype(BF16)
    dk[0] = (k_sum * (1.0 / LOG2E)).astype(BF16)
    dv[0] = v_sum.astype(BF16)


def attend_back(k_rows, v_rows, q, lse, do, dsum, kv):
    d = q.shape[1]
    head = lambda i: (i // H, i % H, 0)
    wide = lambda i: (i // H, i % H, 0, 0)
    return pl.pallas_call(
        attend_back_kernel,
        grid=(2 * H,),
        in_specs=[
            pl.BlockSpec((1, 1, L, LANES), wide),
            pl.BlockSpec((1, 1, L, LANES), wide),
            pl.BlockSpec((1, HEAD, LP), head),
            pl.BlockSpec((1, 1, 16, LP), wide),
            pl.BlockSpec((1, HEAD, LP), head),
            pl.BlockSpec((1, 1, 16, LP), wide),
            pl.BlockSpec((1, HEAD, L), head),
        ],
        out_specs=[pl.BlockSpec((1, HEAD, L), head)] * 3,
        out_shape=[jax.ShapeDtypeStruct((2, d, L), BF16)] * 3,
        scratch_shapes=[pltpu.VMEM((LANES, LP), BF16)] * 2,
        compiler_params=params(),
    )(k_rows, v_rows, q, lse, do, dsum, kv)


def mid_kernel(o, stream, up, wm, we, wr, be, cols,
               dec, ga_out, do_out, dsum_out, dwm, dwe, dwr, dvec, dbe, drb,
               after, stats, n2, act_s, gl_s, g_s):
    copy = pl.program_id(0)
    ff = pl.program_id(1)
    last = pl.num_programs(1) - 1
    d = wm.shape[0]

    @pl.when((copy == 0) & (ff == 0))
    def _():
        dwm[...] = jnp.zeros_like(dwm)
        dwe[...] = jnp.zeros_like(dwe)
        dwr[...] = jnp.zeros_like(dwr)
        dvec[...] = jnp.zeros_like(dvec)
        dbe[...] = jnp.zeros_like(dbe)
        drb[...] = jnp.zeros_like(drb)

    @pl.when(ff == 0)
    def _():
        ctx = o[0, :, :L].astype(BF16)
        x = stream[0] + dg(wm[...], ctx, 0, 0) + cols[:, 3:4]
        after[...] = x
        mean = jnp.mean(x, 0, keepdims=True)
        center = x - mean
        recip = lax.rsqrt(jnp.mean(center * center, 0, keepdims=True) + EPSILON)
        stats[0:1] = mean
        stats[1:2] = recip
        n2[:d] = (center * recip * cols[:, 4:5] + cols[:, 5:6]).astype(BF16)
        row = lax.broadcasted_iota(jnp.int32, (16, L), 0)
        n2[d:] = (row == 0).astype(F32).astype(BF16)
        g = (up[0].astype(F32) * 0.5).astype(BF16)
        g_s[...] = g
        drb[...] += dg(jnp.ones((8, L), BF16), g, 1, 0)

    rows = pl.ds(pl.multiple_of(ff * FFC, FFC), FFC)
    g = g_s[...]
    lifted = dg(we[:, rows], n2[:d], 0, 0) + be[rows, :]
    bell = jnp.exp(-0.5 * lifted * lifted)
    cdf = 0.5 * (1.0 + lax.erf(lifted * ROOT_HALF))
    act = (lifted * cdf).astype(BF16)
    slope = cdf + lifted * bell * INV_ROOT_TWO_PI
    gl = (dg(wr[rows, :], g, 1, 1) * slope).astype(BF16)
    act_s[rows, :] = act
    gl_s[rows, :] = gl
    dwr[rows, :] += dg(act, g, 1, 0)
    grad = dg(n2[...], gl, 1, 1)
    dwe[:, rows] += grad[:d]
    dbe[:, rows] += grad[d : d + 8]

    @pl.when(ff == last)
    def _():
        x = after[...]
        out = x + dg(wr[...], act_s[...], 0, 0) + cols[:, 6:7]
        dec[0] = out.astype(BF16).T
        scaled = (x - stats[0:1]) * stats[1:2]
        e = dg(we[...], gl_s[...], 1, 0)
        dvec[:, 0:1] += jnp.sum(e * scaled, 1, keepdims=True)
        dvec[:, 1:2] += jnp.sum(e, 1, keepdims=True)
        back = norm_back(e, scaled, stats[1:2], cols[:, 4:5])
        ga = g_s[...].T.astype(F32) + back
        ga_out[0] = ga
        gm = ga.astype(BF16)
        dvec[:, 2:3] += jnp.sum(gm.astype(F32), 1, keepdims=True)
        ctx = o[0, :, :L]
        dwm[...] += dg(ctx.astype(BF16), gm, 1, 1)
        do = dg(wm[...], gm, 1, 0).astype(BF16)
        do_out[0, :, :L] = do
        do_out[0, :, L:] = jnp.zeros((d, LP - L), BF16)
        prod = do.astype(F32) * ctx
        for h in range(H):
            dsum_out[0, h, :, :L] = aug_rows(
                -jnp.sum(prod[h * HEAD : (h + 1) * HEAD], 0, keepdims=True)
            )
            dsum_out[0, h, :, L:] = jnp.zeros((16, LP - L), BF16)


def mid(o, stream, up, wm, we, wr, be, cols):
    d = wm.shape[0]
    f = we.shape[1]
    once = pl.Buffered(1)
    const = lambda *s: pl.BlockSpec(s, lambda c, k: (0,) * len(s), pipeline_mode=once)
    acc = lambda *s: pl.BlockSpec(s, lambda c, k: (0,) * len(s), pipeline_mode=once)
    lead = lambda *s: pl.BlockSpec((1,) + s, lambda c, k: (c,) + (0,) * len(s))
    shape = jax.ShapeDtypeStruct
    return pl.pallas_call(
        mid_kernel,
        grid=(2, f // FFC),
        in_specs=[lead(d, LP), lead(d, L), lead(L, d), const(d, d), const(d, f), const(f, d), const(f, 1), const(d, 8)],
        out_specs=[
            lead(L, d), lead(d, L), lead(d, LP), lead(H, 16, LP),
            acc(d, d), acc(d, f), acc(f, d), acc(d, LANES), acc(8, f), acc(8, d),
        ],
        out_shape=[
            shape((2, L, d), BF16), shape((2, d, L), F32), shape((2, d, LP), BF16), shape((2, H, 16, LP), BF16),
            shape((d, d), F32), shape((d, f), F32), shape((f, d), F32), shape((d, LANES), F32),
            shape((8, f), F32), shape((8, d), F32),
        ],
        scratch_shapes=[
            pltpu.VMEM((d, L), F32), pltpu.VMEM((8, L), F32), pltpu.VMEM((d + 16, L), BF16),
            pltpu.VMEM((f, L), BF16), pltpu.VMEM((f, L), BF16), pltpu.VMEM((L, d), BF16),
        ],
        compiler_params=params(),
    )(o, stream, up, wm, we, wr, be, cols)


def post_kernel(dq, dk, dv, stream, ga, target, arrived, win, cols, dwin, dbin, dvec, gp_out, dwp, n1, gp_s):
    copy = pl.program_id(0)
    d = win.shape[0]

    @pl.when(copy == 0)
    def _():
        dwin[...] = jnp.zeros_like(dwin)
        dbin[...] = jnp.zeros_like(dbin)
        dvec[...] = jnp.zeros_like(dvec)
        gp_s[...] = jnp.zeros_like(gp_s)

    x = stream[0]
    scaled, recip = norm_stats(x)
    n1[:d] = (scaled * cols[:, 1:2] + cols[:, 2:3]).astype(BF16)
    row = lax.broadcasted_iota(jnp.int32, (16, L), 0)
    n1[d:] = (row == 0).astype(F32).astype(BF16)
    e = None
    for part, ref in enumerate((dq, dk, dv)):
        sl = slice(part * d, (part + 1) * d)
        grad = dg(n1[...], ref[0], 1, 1)
        dwin[:, sl] += grad[:d]
        dbin[:, sl] += grad[d : d + 8]
        term = dg(win[:, sl], ref[0], 1, 0)
        e = term if e is None else e + term
    dvec[:, 0:1] += jnp.sum(e * scaled, 1, keepdims=True)
    dvec[:, 1:2] += jnp.sum(e, 1, keepdims=True)
    gs = ga[0] + norm_back(e, scaled, recip, cols[:, 1:2])
    hot = one_hot(target, copy)
    covered = jnp.sum(hot, 0, keepdims=True)
    dvec[:, 2:3] += jnp.sum(gs * (1.0 - covered), 1, keepdims=True)
    gp_s[...] += dg(hot.astype(BF16), gs.astype(BF16), 1, 1)

    @pl.when(copy == 1)
    def _():
        gp = gp_s[...].astype(BF16)
        gp_out[...] = gp
        dwp[...] = dg(arrived[...], gp, 0, 0)


def post(dq, dk, dv, stream, ga, target, arrived, win, cols):
    a, e = arrived.shape
    d = win.shape[0]
    once = pl.Buffered(1)
    const = lambda *s: pl.BlockSpec(s, lambda c: (0,) * len(s), pipeline_mode=once)
    lead = lambda *s: pl.BlockSpec((1,) + s, lambda c: (c,) + (0,) * len(s))
    shape = jax.ShapeDtypeStruct
    return pl.pallas_call(
        post_kernel,
        grid=(2,),
        in_specs=[lead(d, L), lead(d, L), lead(d, L), lead(d, L), lead(d, L), const(a, 1), const(a, e), const(d, 3 * d), const(d, 8)],
        out_specs=[const(d, 3 * d), const(8, 3 * d), const(d, LANES), const(a, d), const(e, d)],
        out_shape=[shape((d, 3 * d), F32), shape((8, 3 * d), F32), shape((d, LANES), F32), shape((a, d), BF16), shape((e, d), F32)],
        scratch_shapes=[pltpu.VMEM((d + 16, L), BF16), pltpu.VMEM((a, d), F32)],
        compiler_params=params(),
    )(dq, dk, dv, stream, ga, target, arrived, win, cols)


def layer(arrived, target, up, w):
    (wp, token, gain1, shift1, win, bq, bv, wm, bm, gain2, shift2, we, be, wr, br) = w
    d = wp.shape[1]
    f = lambda v: v.astype(F32)
    cols = jnp.stack([f(token), f(gain1), f(shift1), f(bm), f(gain2), f(shift2), f(br), jnp.zeros((d,), F32)], 1)
    bin_col = jnp.concatenate([f(bq), jnp.zeros((d,), F32), f(bv)])[:, None]
    pos = jnp.asarray(position_table(d))
    tcol = target[:, None]
    stream, q, kv, k_rows, v_rows = pre(arrived, tcol, wp, cols, pos, win, bin_col)
    o, lse = attend(k_rows, q, kv)
    dec, ga, do, dsum, dwm, dwe, dwr, vec2, dbe, drb = mid(
        o, stream, up.reshape(2, L, d), wm, we, wr, f(be)[:, None], cols
    )
    dq, dk, dv = attend_back(k_rows, v_rows, q, lse, do, dsum, kv)
    dwin, dbin, vec1, gp, dwp = post(dq, dk, dv, stream, ga, tcol, arrived, win, cols)
    grads = (
        dwp, vec1[:, 2], vec1[:, 0], vec1[:, 1], dwin, dbin[0, :d], dbin[0, 2 * d :], dwm, vec2[:, 2],
        vec2[:, 0], vec2[:, 1], dwe, dbe[0], dwr, drb[0],
    )
    return dec.reshape(2 * L, d), gp, grads


def per_device(encoded, visible_at, *rest):
    weights, upstream = rest[:-1], rest[-1]
    clip_count = lax.axis_size("clip")
    my_clip = lax.axis_index("clip")
    held, width_in = encoded.shape
    seen = visible_at.shape[1]
    d = weights[0].shape[1]
    cap = -(-held // clip_count)
    cap = -(-cap // 16) * 16
    peer = jnp.arange(clip_count, dtype=jnp.int32)[:, None]
    slot = jnp.arange(cap, dtype=jnp.int32)[None, :]
    first_out = (peer * held - my_clip + clip_count - 1) // clip_count
    picked = jnp.take(encoded, jnp.clip(first_out + slot, 0, held - 1).reshape(-1), axis=0)
    arrived = lax.all_to_all(
        picked.reshape(clip_count, cap, width_in), "clip", split_axis=0, concat_axis=0, tiled=True
    ).reshape(clip_count * cap, width_in)
    first_in = (my_clip * held - peer + clip_count - 1) // clip_count
    local = peer + clip_count * (first_in + slot) - my_clip * held
    valid = (local < held).reshape(-1)
    local = jnp.clip(local, 0, held - 1).reshape(-1)
    target = jnp.take(visible_at.reshape(-1), local) + local // seen * L
    target = jnp.where(valid, target, -1)
    big = [i for i, v in enumerate(weights) if v.ndim == 2]
    small = [i for i, v in enumerate(weights) if v.ndim == 1]
    full = {i: lax.all_gather(weights[i], "wt", axis=0, tiled=True) for i in big}
    packed = lax.all_gather(jnp.concatenate([weights[i] for i in small]), "wt", axis=0)
    at = 0
    for i in small:
        n = weights[i].shape[0]
        full[i] = packed[:, at : at + n].reshape(-1)
        at += n
    w = tuple(full[i] for i in range(len(weights)))
    decoded, gp, grads = layer(arrived, target, upstream, w)
    returned = lax.all_to_all(
        gp.reshape(clip_count, cap, d), "clip", split_axis=0, concat_axis=0, tiled=True
    ).reshape(clip_count * cap, d)
    own = jnp.arange(held, dtype=jnp.int32)
    dest = (my_clip + clip_count * own) // held
    place = dest * cap + own - jnp.take(first_out[:, 0], dest)
    hot = (place[:, None] == jnp.arange(clip_count * cap, dtype=jnp.int32)[None, :]).astype(BF16)
    own_grad = jnp.dot(hot, returned, preferred_element_type=F32).astype(BF16)
    encoded_grad = lax.dot_general(
        own_grad, w[0], (((1,), (1,)), ((), ())), preferred_element_type=F32
    ).astype(BF16)
    out = {}
    scatter = lambda v: lax.psum_scatter(v.astype(BF16), "wt", scatter_dimension=0, tiled=True)
    for i in big:
        out[i] = scatter(grads[i])
    wt = lax.axis_size("wt")
    pack = jnp.concatenate([grads[i].reshape(wt, -1) for i in small], 1)
    pack = scatter(pack)[0]
    total = lax.psum(tuple(out[i] for i in big) + (pack,), "clip")
    for k, i in enumerate(big):
        out[i] = total[k].astype(F32)
    at = 0
    for i in small:
        n = weights[i].shape[0]
        out[i] = total[-1][at : at + n].astype(F32)
        at += n
    return (decoded, encoded_grad) + tuple(out[i] for i in range(len(weights)))


def solution(mesh):
    both, wt = P(("clip", "wt"), None), P("wt")
    mat = P("wt", None)
    params_in = (mat, wt, wt, wt, mat, wt, wt, mat, wt, wt, wt, mat, wt, mat, wt)
    return jax.shard_map(
        per_device,
        mesh=mesh,
        in_specs=(both, both) + params_in + (both,),
        out_specs=(both, both) + params_in,
        check_vma=False,
    )
```

time: 1150 us -> 505 us (0.44)
  matrix products: 554 us -> 1.47 us
  Pallas kernels: 0 us -> 208 us
  other arithmetic: 223 us -> 26 us
  local copies, waits for them, and re-layouts: 134 us -> 15.6 us
  waiting for transfers between devices: 60.9 us -> 118 us
  loops' own time: 25.5 us -> 0 us
    dot_general x43 -> x1, matrix products: 554 us -> 1.47 us  [per_device(): lax.dot_general(own_grad, w[0], (((1,), (1,)), ((), ())), preferred_eleme...]
    pallas_call x0 -> x5, Pallas kernels: none -> 208 us  [the longest x1 82.8 us: attend_back(): pl.pallas_call(attend_back_kernel, grid=(2 * H,), in_specs=[pl.BlockSpec(...]
    convert_element_type x29 -> x13, other arithmetic: 126 us -> 18.2 us  [the longest x5 9.23 us: per_device(): v.astype(BF16)]
    reduce_sum x10 -> x0, other arithmetic: 69.4 us -> none  [the longest x4 50.1 us: attend_forward(): row_total = jnp.sum(shifted, -1, keepdims=True)]
    convert_element_type x6 -> x9, local copies, waits for them, and re-layouts: 44.9 us -> 0.75 us  [layer(): f = lambda v: v.astype(F32)]
    psum x1, waiting for transfers between devices: 26.4 us -> 57.4 us  [per_device(): total = lax.psum(tuple((out[i] for i in big)) + (pack,), 'clip')]
    reduce_scatter x5, waiting for transfers between devices: 33 us -> 59.2 us  [per_device(): lax.psum_scatter(v.astype(BF16), 'wt', scatter_dimension=0, tiled=True)]
    another operation x2 -> x0, loops' own time: 25.5 us -> none  [the longest x1 24.9 us: per_device(): lax.map(attend_back, (query_all, key_all, value_all, logsum, grad_heads))]
  transfers between devices with their start and end apart: 10 -> 10, of which waited for: 3 -> 3; matrix products, arithmetic and copies ran while one was open for 76% -> 7% of each run, Pallas kernels for 0% -> 31%
where the time goes in v1:
time: 505 us; the launch traced here: 500 us
  Pallas kernels  208 us (41%)
  waiting for transfers between devices  118 us (23%)
  blocking collectives  106 us (21%)
  other arithmetic  26 us (5%)
  local copies, waits for them, and re-layouts  15.6 us (3%)
  between operations  15.5 us (3%)
  starting transfers between devices  9.42 us (2%)
    pallas_call x1, Pallas kernels, attend_back(): pl.pallas_call(attend_back_kernel, grid=(2 * H,), in_specs=[pl.BlockSpec(...  82.8 us
    reduce_scatter x5, waiting for transfers between devices, per_device(): lax.psum_scatter(v.astype(BF16), 'wt', scatter_dimension=0, tiled=True)  59.2 us
    all_gather x3, blocking collectives, per_device(): lax.all_gather(weights[i], 'wt', axis=0, tiled=True)  57.5 us
    psum x1, waiting for transfers between devices, per_device(): total = lax.psum(tuple((out[i] for i in big)) + (pack,), 'clip')  57.4 us
    pallas_call x1, Pallas kernels, mid(): pl.pallas_call(mid_kernel, grid=(2, f // FFC), in_specs=[lead(d, LP), lea...  53.6 us
    unnamed x2, blocking collectives  36.7 us
    pallas_call x1, Pallas kernels, attend(): pl.pallas_call(attend_kernel, grid=(2 * H,), in_specs=[pl.BlockSpec((1, 1...  34.7 us
    pallas_call x1, Pallas kernels, post(): pl.pallas_call(post_kernel, grid=(2,), in_specs=[lead(d, L), lead(d, L),...  22.1 us
  transfers between devices with their start and end apart: 10, of which 3 were waited for; matrix products, arithmetic and copies ran while one was open for 7% of the time, Pallas kernels for 31%

profile of v1, /device:TPU:0, one launch (start us, length us, event | category | flops | bytes accessed | tf_op | source)
XLA Modules:
  0.0 500.4 jit_solution(7060961167756338566)
XLA Ops:
  7.3 0.7 all-gather.4.cloned.1.call-update
  8.3 2.2 gather_fusion
  10.7 0.9 broadcast_select_fusion
  11.7 5.2 %all-to-all-start = ((bf16[8,48,768]{2,1,0:T(8,128)(2,1)}), bf16[8,48,768]{2,1,0:T(8,128)(2,1)S(1)}, u32[]{:S(2)}, u32[]{:S(2)}) async-start(bf16[8,48,768]{2,1,0:T(8,128)(2,1)} %broadcast_select_fusion), calls=%async_computation | async-start | bytes 1179648 | tf_op jit(solution)/shard_map/all_to_all | solution.py:429
  16.9 0.7 all-gather.6.cloned.1.call-update
  17.7 0.6 fusion.15
  19.1 0.3 dynamic-update-slice
  19.4 19.5 %all-reduce = bf16[4992]{0:T(1024)(128)(2,1)S(1)} all-reduce(bf16[4992]{0:T(1024)(128)(2,1)S(1)} %dynamic-update-slice), channel_id=2, replica_groups=mesh['clip'=8,'wt'=4] {'wt'}, use_global_device_ids=true, to_apply=%add | all-reduce | flops 4992 | bytes 19968
  39.8 0.8 copy.67.cols
  41.2 1.0 broadcast_in_dim.42.bin_col
  42.3 1.2 copy.73
  43.7 2.8 gather_fusion.1
  46.5 16.7 %all_gather.25.wm = bf16[384,384]{1,0:T(8,128)(2,1)} all-gather(bf16[96,384]{1,0:T(8,128)(2,1)S(1)} %copy-done.11), channel_id=1, replica_groups=mesh['clip'=8,'wt'=4] {'wt'}, dimensions={0}, use_global_device_ids=true | all-gather | bytes 368640 | tf_op jit(solution)/shard_map/all_gather | solution.py:440
  63.1 0.9 fusion.4.target
  64.0 22.2 %all_gather.21.wp = bf16[768,384]{1,0:T(8,128)(2,1)} all-gather(bf16[192,384]{1,0:T(8,128)(2,1)S(1)} %copy-done.9), channel_id=1, replica_groups=mesh['clip'=8,'wt'=4] {'wt'}, dimensions={0}, use_global_device_ids=true | all-gather | bytes 737280 | tf_op jit(solution)/shard_map/all_gather | solution.py:440
  86.2 18.6 %all_gather.24.win = bf16[384,1152]{1,0:T(8,128)(2,1)} all-gather(bf16[96,1152]{1,0:T(8,128)(2,1)S(1)} %copy-done.6), channel_id=1, replica_groups=mesh['clip'=8,'wt'=4] {'wt'}, dimensions={0}, use_global_device_ids=true | all-gather | bytes 1105920 | tf_op jit(solution)/shard_map/all_gather | solution.py:440
  104.9 0.8 copy-done.2
  105.7 14.9 %shard_map.314 = (f32[2,384,1568]{2,1,0:T(8,128)}, bf16[2,384,1664]{2,1,0:T(8,128)(2,1)}, bf16[2,768,1568]{2,1,0:T(8,128)(2,1)}, bf16[2,6,1568,128]{3,2,1,0:T(8,128)(2,1)}, bf16[2,6,1568,128]{3,2,1,0:T(8,128)(2,1)}) custom-call(bf16[384,768]{1,0:T(8,128)(2,1)} %bitcast.23, s32[384,1]{1,0:T(8,128)} %fusion.4.target, bf16[768,384]{1,0:T(8,128)(2,1)} %all_gather.21.wp, ...), custom_call_target="tpu_custom_call" | custom-call | tf_op jit(solution)/shard_map/pallas_call | solution.py:115
  120.6 34.7 %shard_map.315 = (f32[2,384,1664]{2,1,0:T(8,128)}, bf16[2,6,16,1664]{3,2,1,0:T(8,128)(2,1)}) custom-call(bf16[2,6,1568,128]{3,2,1,0:T(8,128)(2,1)} %get-tuple-element.42.k_rows, bf16[2,384,1664]{2,1,0:T(8,128)(2,1)} %get-tuple-element.43.q, bf16[2,768,1568]{2,1,0:T(8,128)(2,1)} %get-tuple-element.44.kt.vt, bf16[2,768,1568]{2,1,0:T(8,128)(2,1)} %get-tuple-element.44.kt.vt), custom_call_target="tpu_custom_call" | custom-call | tf_op jit(solution)/shard_map/pallas_call | solution.py:161
  155.4 53.6 %shard_map.316 = (bf16[2,1568,384]{2,1,0:T(8,128)(2,1)}, f32[2,384,1568]{2,1,0:T(8,128)}, bf16[2,384,1664]{2,1,0:T(8,128)(2,1)}, bf16[2,6,16,1664]{3,2,1,0:T(8,1...) custom-call(f32[2,384,1664]{2,1,0:T(8,128)} %get-tuple-element.45.o,, ...), custom_call_target="tpu_custom_call" | custom-call | tf_op jit(solution)/shard_map/pallas_call | solution.py:316
  208.9 1.8 convert_element_type.215
  210.8 82.8 %shard_map.317 = (bf16[2,384,1568]{2,1,0:T(8,128)(2,1)}, bf16[2,384,1568]{2,1,0:T(8,128)(2,1)}, bf16[2,384,1568]{2,1,0:T(8,128)(2,1)}) custom-call(bf16[2,6,1568,128]{3,2,1,0:T(8,128)(2,1)} %get-tuple-element.42.k_rows, bf16[2,6,1568,128]{3,2,1,0:T(8,128)(2,1)} %get-tuple-element.48.v_rows, bf16[2,384,1664]{2,1,0:T(8,128)(2,1)} %get-tuple-element.43.q, ...), custom_call_target="tpu_custom_call" | custom-call | tf_op jit(solution)/shard_map/pallas_call | solution.py:213
  293.6 22.1 %shard_map.318 = (f32[384,1152]{1,0:T(8,128)}, f32[8,1152]{1,0:T(8,128)}, f32[384,128]{1,0:T(8,128)}, bf16[384,384]{1,0:T(8,128)(2,1)}, f32[768,384]{1,0:T(8,128)}) custom-call(bf16[2,384,1568]{2,1,0:T(8,128)(2,1)} %get-tuple-element.52.dq, bf16[2,384,1568]{2,1,0:T(8,128)(2,1)} %get-tuple-element.53.dk, bf16[2,384,1568]{2,1,0:T(8,128)(2,1)} %get-tuple-element.54.dv, ...), custom_call_target="tpu_custom_call" | custom-call | tf_op jit(solution)/shard_map/pallas_call | solution.py:383
  315.6 2.3 convert_element_type.206
  318.0 1.0 convert_element_type.211
  319.1 3.0 convert_element_type.220
  322.2 1.2 convert_element_type.223
  323.4 0.6 fusion.16
  324.0 4.6 fusion.13
  328.6 0.7 fusion.11
  329.3 0.3 slice_reduce_fusion.3
  330.6 0.8 fusion.8
  331.4 0.7 fusion.14
  332.2 3.9 all-to-all-start.1
  336.3 17.2 %all-reduce.1 = bf16[4,1248]{1,0:T(4,128)(2,1)S(1)} all-reduce(bf16[4,1248]{1,0:T(4,128)(2,1)S(1)} %concatenate.12), channel_id=4, replica_groups=mesh['clip'=8,'wt'=4] {'wt'}, use_global_device_ids=true, to_apply=%region_2.3.clone | all-reduce | flops 4992 | bytes 19968
  353.5 0.7 dynamic-slice_reduce_fusion
  354.2 12.2 %psum.43 = bf16[1248]{0:T(1024)(128)(2,1)S(1)} all-reduce(bf16[1248]{0:T(1024)(128)(2,1)S(1)} %dynamic-slice_reduce_fusion), channel_id=1, replica_groups=mesh['clip'=8,'wt'=4] {'clip'}, use_global_device_ids=true, to_apply=%region_3.4 | all-reduce | flops 1248 | bytes 4992 | tf_op jit(solution)/shard_map/psum | solution.py:467
  366.5 28.9 %reduce-scatter.12.cloned.1.call-done = bf16[96,1536]{1,0:T(8,128)(2,1)} async-done(((bf16[384,1536]{1,0:T(8,128)(2,1)}), bf16[96,1536]{1,0:T(8,128)(2,1)}) %reduce-scatter.12.cloned.1.call-update) | async-done | bytes 294928 | tf_op jit(solution)/shard_map/reduce_scatter | solution.py:461
  395.4 30.2 %reduce-scatter.14.cloned.1.call-done = bf16[384,384]{1,0:T(8,128)(2,1)} async-done(((bf16[1536,384]{1,0:T(8,128)(2,1)}), bf16[384,384]{1,0:T(8,128)(2,1)}) %reduce-scatter.14.cloned.1.call-update) | async-done | bytes 294928 | tf_op jit(solution)/shard_map/reduce_scatter | solution.py:461
  425.7 0.6 slice_convert_fusion.2
  426.2 0.6 slice_convert_fusion.12
  426.9 1.5 convolution_convert_fusion
  428.3 57.4 %all-reduce.5.cloned.1.call-done = (bf16[192,384]{1,0:T(8,128)(2,1)}, bf16[96,1152]{1,0:T(8,128)(2,1)}, bf16[96,384]{1,0:T(8,128)(2,1)}, bf16[96,1536]{1,0:T(8,128)(2,1)}, bf16[384,384]{1,0:T(8,128)(2,1)}) async-done(((bf16[192,384]{1,0:T(8,128)(2,1)}, bf16[96,1152]{1,0:T(8,128)(2,1)}, bf16[96,384]{1,0:T(8,128)(2,1)}, bf16[96,1536]{1,0:T(8,128)(2,1)}, bf16[384,384]{1,0:T(8,128)(2,1)}), ...) | async-done | bytes 1032208 | tf_op jit(solution)/shard_map/psum | solution.py:467
  485.7 1.9 convert_element_type.221
  487.6 1.8 convert_element_type.224
  489.4 1.7 convert_element_type.212
  491.1 1.6 convert_element_type.207
  492.7 0.7 convert_element_type.216
  (120 shorter events, 4.1 us)
Async XLA Ops:
  7.2 1.1 copy-start
  7.2 148.1 %all-gather.4.cloned.1.call-start = ((), (), s32[]{:S(2)}) async-start(), calls=%async_computation.7 | async-start | bytes 1474560 | tf_op jit(solution)/shard_map/all_gather | solution.py:440
  10.5 7.2 %copy-start.13 = (u32[32]{0:T(128)S(1)}, u32[32]{0:T(128)}, u32[]{:S(2)}) copy-start(u32[32]{0:T(128)} %constant.121) | copy-start | bytes 388
  10.5 8.4 %copy-start.15 = (bf16[384]{0:T(512)(128)(2,1)S(1)}, bf16[384]{0:T(512)(128)(2,1)}, u32[]{:S(2)}) copy-start(bf16[384]{0:T(512)(128)(2,1)} %param.33) | copy-start | bytes 2308
  10.5 8.4 %copy-start.16 = (bf16[96]{0:T(256)(128)(2,1)S(1)}, bf16[96]{0:T(256)(128)(2,1)}, u32[]{:S(2)}) copy-start(bf16[96]{0:T(256)(128)(2,1)} %param.22) | copy-start | bytes 580
  10.5 8.4 %copy-start.17 = (bf16[96]{0:T(256)(128)(2,1)S(1)}, bf16[96]{0:T(256)(128)(2,1)}, u32[]{:S(2)}) copy-start(bf16[96]{0:T(256)(128)(2,1)} %param.23) | copy-start | bytes 580
  10.5 8.4 %copy-start.18 = (bf16[96]{0:T(256)(128)(2,1)S(1)}, bf16[96]{0:T(256)(128)(2,1)}, u32[]{:S(2)}) copy-start(bf16[96]{0:T(256)(128)(2,1)} %param.24) | copy-start | bytes 580
  10.6 8.4 %copy-start.19 = (bf16[96]{0:T(256)(128)(2,1)S(1)}, bf16[96]{0:T(256)(128)(2,1)}, u32[]{:S(2)}) copy-start(bf16[96]{0:T(256)(128)(2,1)} %param.26) | copy-start | bytes 580
  10.6 8.4 %copy-start.20 = (bf16[96]{0:T(256)(128)(2,1)S(1)}, bf16[96]{0:T(256)(128)(2,1)}, u32[]{:S(2)}) copy-start(bf16[96]{0:T(256)(128)(2,1)} %param.27) | copy-start | bytes 580
  10.6 8.4 %copy-start.21 = (bf16[96]{0:T(256)(128)(2,1)S(1)}, bf16[96]{0:T(256)(128)(2,1)}, u32[]{:S(2)}) copy-start(bf16[96]{0:T(256)(128)(2,1)} %param.29) | copy-start | bytes 580
  10.6 8.4 %copy-start.22 = (bf16[96]{0:T(256)(128)(2,1)S(1)}, bf16[96]{0:T(256)(128)(2,1)}, u32[]{:S(2)}) copy-start(bf16[96]{0:T(256)(128)(2,1)} %param.30) | copy-start | bytes 580
  10.6 8.4 %copy-start.23 = (bf16[96]{0:T(256)(128)(2,1)S(1)}, bf16[96]{0:T(256)(128)(2,1)}, u32[]{:S(2)}) copy-start(bf16[96]{0:T(256)(128)(2,1)} %param.31) | copy-start | bytes 580
  10.6 8.4 %copy-start.24 = (bf16[96]{0:T(256)(128)(2,1)S(1)}, bf16[96]{0:T(256)(128)(2,1)}, u32[]{:S(2)}) copy-start(bf16[96]{0:T(256)(128)(2,1)} %param.35) | copy-start | bytes 580
  10.6 30.1 %copy-start.14 = (s32[2,157]{1,0:T(2,128)S(1)}, s32[2,157]{1,0:T(2,128)}, u32[]{:S(2)}) copy-start(s32[2,157]{1,0:T(2,128)} %param.20) | copy-start | bytes 3772
  11.7 93.2 %all-to-all-start = ((bf16[8,48,768]{2,1,0:T(8,128)(2,1)}), bf16[8,48,768]{2,1,0:T(8,128)(2,1)S(1)}, u32[]{:S(2)}, u32[]{:S(2)}) async-start(bf16[8,48,768]{2,1,0:T(8,128)(2,1)} %broadcast_select_fusion), calls=%async_computation | async-start | bytes 1179648 | tf_op jit(solution)/shard_map/all_to_all | solution.py:429
  16.8 29.6 %copy-start.11 = (bf16[96,384]{1,0:T(8,128)(2,1)S(1)}, bf16[96,384]{1,0:T(8,128)(2,1)}, u32[]{:S(2)}) copy-start(bf16[96,384]{1,0:T(8,128)(2,1)} %param.28) | copy-start | bytes 221188
  16.8 138.5 %all-gather.6.cloned.1.call-start = ((), (), s32[]{:S(2)}) async-start(), calls=%async_computation.8 | async-start | bytes 1474560 | tf_op jit(solution)/shard_map/all_gather | solution.py:440
  17.6 348.9 %reduce-scatter.10.cloned.1.call-start = ((), (), s32[]{:S(2)}) async-start(), calls=%async_computation.11 | async-start | bytes 368640 | tf_op jit(solution)/shard_map/reduce_scatter | solution.py:461
  39.1 25.0 %copy-start.9 = (bf16[192,384]{1,0:T(8,128)(2,1)S(1)}, bf16[192,384]{1,0:T(8,128)(2,1)}, u32[]{:S(2)}) copy-start(bf16[192,384]{1,0:T(8,128)(2,1)} %param.21) | copy-start | bytes 442372
  41.2 45.0 %copy-start.6 = (bf16[96,1152]{1,0:T(8,128)(2,1)S(1)}, bf16[96,1152]{1,0:T(8,128)(2,1)}, u32[]{:S(2)}) copy-start(bf16[96,1152]{1,0:T(8,128)(2,1)} %param.25) | copy-start | bytes 663556
  104.9 0.8 copy-start.2
  210.8 155.7 %reduce-scatter.6.cloned.1.call-start = ((), (), s32[]{:S(2)}) async-start(), calls=%async_computation.9 | async-start | bytes 737280 | tf_op jit(solution)/shard_map/reduce_scatter | solution.py:461
  315.6 2.4 copy-start.5
  317.9 48.6 %reduce-scatter.8.cloned.1.call-start = ((), (), s32[]{:S(2)}) async-start(), calls=%async_computation.10 | async-start | bytes 1105920 | tf_op jit(solution)/shard_map/reduce_scatter | solution.py:461
  319.0 3.1 copy-start.3
  319.0 76.3 %reduce-scatter.12.cloned.1.call-start = ((), (), s32[]{:S(2)}) async-start(), calls=%async_computation.12 | async-start | bytes 1474560 | tf_op jit(solution)/shard_map/reduce_scatter | solution.py:461
  322.1 7.2 %copy-start.8 = (f32[384,128]{1,0:T(8,128)S(1)}, f32[384,128]{1,0:T(8,128)}, u32[]{:S(2)}) copy-start(f32[384,128]{1,0:T(8,128)} %get-tuple-element.58) | copy-start | bytes 589828
  322.1 103.5 %reduce-scatter.14.cloned.1.call-start = ((), (), s32[]{:S(2)}) async-start(), calls=%async_computation.13 | async-start | bytes 1474560 | tf_op jit(solution)/shard_map/reduce_scatter | solution.py:461
  322.1 7.7 %copy-start.12 = (f32[8,1152]{1,0:T(8,128)S(1)}, f32[8,1152]{1,0:T(8,128)}, u32[]{:S(2)}) copy-start(f32[8,1152]{1,0:T(8,128)} %get-tuple-element.59) | copy-start | bytes 110596
  322.1 7.9 %copy-start.7 = (f32[384,128]{1,0:T(8,128)S(1)}, f32[384,128]{1,0:T(8,128)}, u32[]{:S(2)}) copy-start(f32[384,128]{1,0:T(8,128)} %get-tuple-element.60) | copy-start | bytes 589828
  323.3 103.5 %copy-start.4 = (bf16[768,384]{1,0:T(8,128)(2,1)S(1)}, bf16[768,384]{1,0:T(8,128)(2,1)}, u32[]{:S(2)}) copy-start(bf16[768,384]{1,0:T(8,128)(2,1)} %all_gather.21.wp) | copy-start | bytes 1769476
  332.2 94.6 %all-to-all-start.1 = ((bf16[8,48,384]{2,1,0:T(8,128)(2,1)}), bf16[8,48,384]{2,1,0:T(8,128)(2,1)S(1)}, u32[]{:S(2)}, u32[]{:S(2)}) async-start(bf16[8,48,384]{2,1,0:T(8,128)(2,1)} %bitcast.13), calls=%async_computation.1 | async-start | bytes 589824 | tf_op jit(solution)/shard_map/all_to_all | solution.py:449
  336.2 149.5 %all-reduce.5.cloned.1.call-start = ((), (), s32[]{:S(2)}) async-start(), calls=%async_computation.14 | async-start | bytes 2064384 | tf_op jit(solution)/shard_map/psum | solution.py:467
  425.6 67.8 %copy-start.1 = (bf16[314,768]{1,0:T(8,128)(2,1)S(1)}, bf16[314,768]{1,0:T(8,128)(2,1)}, u32[]{:S(2)}) copy-start(bf16[314,768]{1,0:T(8,128)(2,1)} %param.19) | copy-start | bytes 1446916
  485.7 7.0 %copy-start.10 = (bf16[96,384]{1,0:T(8,128)(2,1)S(1)}, bf16[96,384]{1,0:T(8,128)(2,1)}, u32[]{:S(2)}) copy-start(bf16[96,384]{1,0:T(8,128)(2,1)} %get-tuple-element.77) | copy-start | bytes 221188
Sparse Core Ops, SparseCore 0:
  9.6 33.6 all-gather.3
  44.9 41.9 all-gather.5
  210.9 19.5 reduce-scatter.9
  318.1 21.6 reduce-scatter.5
  341.9 22.9 reduce-scatter.7
  367.1 28.2 reduce-scatter.11
  397.7 27.8 reduce-scatter.13
  429.4 56.2 all-reduce.4

commit v2 on v1

v2 whole, which is shorter than its diff:
```python
import functools
import math

import jax
import jax.numpy as jnp
import numpy as np
from jax import lax
from jax.experimental import pallas as pl
from jax.experimental.pallas import tpu as pltpu
from jax.sharding import PartitionSpec as P

H = 6
HEAD = 64
L = 1568
LANES = 128
LP = -(-L // LANES) * LANES
EPSILON = 1e-06
LOG2E = math.log2(math.e)
Q_SCALE = LOG2E / math.sqrt(HEAD)
ROOT_HALF = math.sqrt(0.5)
INV_ROOT_TWO_PI = 1.0 / math.sqrt(2.0 * math.pi)
SAFE_EXPONENT = 100.0
VMEM_LIMIT = 60 * 2**20
FFC = 256
Q_BLOCKS = ((0, 896), (896, LP - 896))
F32 = jnp.float32
BF16 = jnp.bfloat16


SEG = 16
ROWS = 384
MESH = pl.DeviceIdType.MESH
TOKEN, GAIN1, SHIFT1, BIAS_Q, BIAS_V, BIAS_M, GAIN2, SHIFT2, BIAS_R, BIAS_E = range(10)


def params(**kw):
    return pltpu.CompilerParams(vmem_limit_bytes=VMEM_LIMIT, **kw)


def cost(flops, moved=0):
    return pl.CostEstimate(flops=int(flops), bytes_accessed=int(moved), transcendentals=0)


def up16(x):
    return -(-x // SEG) * SEG


def segments(parts, share):
    out = []
    at = 0
    for name, rows in parts:
        for r in range(0, rows, SEG):
            out.append((name, r, at // share, at % share))
            at += SEG
    return out


def dg(a, b, ca, cb):
    return lax.dot_general(a, b, (((ca,), (cb,)), ((), ())), preferred_element_type=F32)


def position_table(width):
    places = np.arange(L, dtype=np.float64)[None, :]
    columns = np.arange(width)
    exponent = (2 * (columns // 2)).astype(np.float64) / width
    angles = places / np.power(10000.0, exponent)[:, None]
    return np.where(columns[:, None] % 2 == 0, np.sin(angles), np.cos(angles)).astype(np.float32)


def norm_stats(x):
    center = x - jnp.mean(x, 0, keepdims=True)
    recip = lax.rsqrt(jnp.mean(center * center, 0, keepdims=True) + EPSILON)
    return center * recip, recip


def norm_back(e, scaled, recip, gain):
    lifted = e * gain
    return recip * (
        lifted
        - jnp.mean(lifted, 0, keepdims=True)
        - scaled * jnp.mean(lifted * scaled, 0, keepdims=True)
    )


def split3(x):
    hi = x.astype(BF16)
    rest = x - hi.astype(F32)
    mid = rest.astype(BF16)
    low = (rest - mid.astype(F32)).astype(BF16)
    return hi, mid, low


def aug_rows(x):
    hi, mid, low = split3(x)
    row = lax.broadcasted_iota(jnp.int32, (16, x.shape[1]), 0)
    zero = jnp.zeros((16, x.shape[1]), F32)
    out = jnp.where(row == 0, hi.astype(F32), zero)
    out = jnp.where(row == 1, mid.astype(F32), out)
    out = jnp.where(row == 2, low.astype(F32), out)
    return out.astype(BF16)


def one_hot(vis, width):
    place = lax.broadcasted_iota(jnp.int32, (vis.shape[0], width), 1).astype(F32)
    return (vis == place).astype(F32)


def first_slot(dest, held, clip, n):
    return (dest * held - clip + n - 1) // n


def interleave(rows, cols, clip, source, held, seen, seen_pad, n, by_row):
    first = (clip * held - source + n - 1) // n
    base = source + n * first - clip * held
    place = lax.broadcasted_iota(jnp.int32, (rows, cols), 0 if by_row else 1)
    slot = lax.broadcasted_iota(jnp.int32, (rows, cols), 1 if by_row else 0)
    second = place >= seen_pad
    local = jnp.where(second, place - (seen_pad - seen), place)
    good = (place < seen) | (second & (place < seen_pad + seen))
    return (good & (local == base + n * slot)).astype(F32).astype(BF16)


def greet(n, m, clip, wt):
    barrier = pltpu.get_barrier_semaphore()
    for k in range(1, n):
        pl.semaphore_signal(barrier, inc=1, device_id=(lax.rem(clip + k, n), wt), device_id_type=MESH)
    for k in range(1, m):
        pl.semaphore_signal(barrier, inc=1, device_id=(clip, lax.rem(wt + k, m)), device_id_type=MESH)
    pl.semaphore_wait(barrier, n + m - 2)


def remote(src, dst, send, recv, clip, wt):
    return pltpu.make_async_remote_copy(
        src_ref=src, dst_ref=dst, send_sem=send, recv_sem=recv, device_id=(clip, wt), device_id_type=MESH
    )


def enter_kernel(n, m, share, cap, seen_pad, *refs):
    (enc, vis_in, wp_in, win_in, *vecs) = refs[:14]
    (seen_out, vis_out, wp, win, cols, be) = refs[14:20]
    (pack, gath, out_rows, in_rows, vec_s, vis_s, zs, zr, bs, br, fs, fr, rs, rr) = refs[20:]
    clip = lax.axis_index("clip")
    wt = lax.axis_index("wt")
    held = enc.shape[0]
    seen = vis_in.shape[1]
    wp_rows = wp_in.shape[0]
    win_rows = win_in.shape[0]
    half = n // 2
    plan = segments(
        [("wp", wp_rows)] + [(j, win_rows) for j in range(3)] + [("vec", SEG)], share
    )
    vec_s[...] = jnp.zeros_like(vec_s)
    for i, ref in enumerate(vecs):
        vec_s[i : i + 1, : ref.shape[1]] = ref[...].astype(F32)
    for name, r, slot, at in plan:
        if name == "wp":
            piece = wp_in[r : r + SEG]
        elif name == "vec":
            piece = vec_s[...].astype(BF16)
        else:
            piece = win_in[r : r + SEG, name * ROWS : (name + 1) * ROWS]
        pack[slot, at : at + SEG] = piece
    for at in range(len(plan) * SEG, n * share, SEG):
        pack[at // share, at % share : at % share + SEG] = jnp.zeros((SEG, ROWS), BF16)
    greet(n, m, clip, wt)

    sends = []
    for k in range(1, m):
        copy = remote(pack.at[clip], gath.at[clip, wt], zs.at[k], zr.at[k], clip, lax.rem(wt + k, m))
        copy.start()
        sends.append(copy)
    gath[clip, wt] = pack[clip]

    rows_at = lax.broadcasted_iota(jnp.int32, (cap, held), 0)
    cols_at = lax.broadcasted_iota(jnp.int32, (cap, held), 1)
    row_sends = []
    for k in [*range(2, n, 2), *range(3, n, 2), 1, 0] if n > 2 else range(n - 1, -1, -1):
        dest = lax.rem(clip + k, n)
        hot = (rows_at + first_slot(dest, held, clip, n) == cols_at).astype(F32).astype(BF16)
        rows = dg(hot, enc[...], 1, 0).astype(BF16)
        if k == 0:
            in_rows[clip] = rows
        else:
            out_rows[k] = rows
            copy = remote(out_rows.at[k], in_rows.at[clip], rs.at[k], rr.at[k], dest, wt)
            copy.start()
            row_sends.append(copy)

    for k in range(1, m):
        source = lax.rem(wt - k + m, m)
        remote(pack.at[clip], gath.at[clip, source], zs.at[k], zr.at[k], clip, source).wait_recv()
    for j in range(1, half):
        copy = remote(gath.at[clip], gath.at[clip], bs.at[j], br.at[j], lax.rem(clip + 2 * j, n), wt)
        copy.start()
        sends.append(copy)
    partner = clip + 1 - 2 * lax.rem(clip, 2)
    copy = remote(gath.at[clip], gath.at[clip], fs.at[0], fr.at[0], partner, wt)
    copy.start()
    sends.append(copy)

    vis_s[...] = jnp.full(vis_s.shape, -1.0, F32)
    vis_s[0:2, :seen] = vis_in[...].astype(F32)
    turned = vis_s[...].T
    for copy_at in range(2):
        vis_out[copy_at] = turned[:seen_pad, copy_at : copy_at + 1]

    for j in range(1, half):
        source = lax.rem(clip - 2 * j + n, n)
        remote(gath.at[source], gath.at[source], bs.at[j], br.at[j], source, wt).wait_recv()
        copy = remote(gath.at[source], gath.at[source], fs.at[j], fr.at[j], partner, wt)
        copy.start()
        sends.append(copy)

    for k in range(1, n):
        source = lax.rem(clip - k + n, n)
        remote(out_rows.at[k], in_rows.at[source], rs.at[k], rr.at[k], source, wt).wait_recv()
    total = None
    for source in range(n):
        hot = interleave(2 * seen_pad, cap, clip, source, held, seen, seen_pad, n, True)
        part = dg(hot, in_rows[source], 1, 0)
        total = part if total is None else total + part
    total = total.astype(BF16)
    seen_out[0] = total[:seen_pad]
    seen_out[1] = total[seen_pad:]

    for j in range(half):
        source = lax.rem(partner - 2 * j + n, n)
        remote(gath.at[source], gath.at[source], fs.at[j], fr.at[j], partner, wt).wait_recv()
    for z in range(m):
        for name, r, slot, at in plan:
            piece = gath[slot, z, at : at + SEG]
            if name == "wp":
                wp[z * wp_rows + r : z * wp_rows + r + SEG] = piece
            elif name == "vec":
                turned = piece.astype(F32).T
                small = vecs[0].shape[1]
                cols[z * small : (z + 1) * small] = turned[:small]
                large = vecs[BIAS_E].shape[1]
                be[z * large : (z + 1) * large] = turned[:large, BIAS_E : BIAS_E + 1]
            else:
                win[z * win_rows + r : z * win_rows + r + SEG, name * ROWS : (name + 1) * ROWS] = piece
    for copy in sends + row_sends:
        copy.wait_send()


def enter(n, m, enc, vis, wp, win, vecs):
    held, e = enc.shape
    seen = vis.shape[1]
    seen_pad = up16(seen)
    d = wp.shape[1]
    cap = up16(-(-held // n))
    share = up16(-(-(wp.shape[0] + 3 * win.shape[0] + SEG) // n))
    whole = pl.BlockSpec(memory_space=pltpu.VMEM)
    shape = jax.ShapeDtypeStruct
    dma = pltpu.SemaphoreType.DMA
    ins = (enc, vis, wp, win, *[v[None, :] for v in vecs])
    return pl.pallas_call(
        functools.partial(enter_kernel, n, m, share, cap, seen_pad),
        in_specs=[whole] * len(ins),
        out_specs=[whole] * 6,
        out_shape=[
            shape((2, seen_pad, e), BF16), shape((2, seen_pad, 1), F32), shape((e, d), BF16),
            shape((d, 3 * d), BF16), shape((d, 16), F32), shape((vecs[BIAS_E].shape[0] * m, 1), F32),
        ],
        scratch_shapes=[
            pltpu.VMEM((n, share, ROWS), BF16), pltpu.VMEM((n, m, share, ROWS), BF16),
            pltpu.VMEM((n, cap, e), BF16), pltpu.VMEM((n, cap, e), BF16),
            pltpu.VMEM((SEG, ROWS), F32), pltpu.VMEM((8, 2 * LANES), F32),
            dma((m,)), dma((m,)), dma((n // 2,)), dma((n // 2,)), dma((n // 2,)), dma((n // 2,)), dma((n,)), dma((n,)),
        ],
        compiler_params=params(collective_id=0, has_side_effects=True),
        cost_estimate=cost(6e9, 4e6),
    )(*ins)


def pre_kernel(seen, vis, wp, cols, pos, win, stream_out, q_out, kv_out, k_rows, v_rows):
    width = wp.shape[1]
    proj = dg(seen[0], wp[...], 1, 0).astype(BF16)
    hot = one_hot(vis[0], L)
    covered = jnp.sum(hot, 0, keepdims=True)
    stream = dg(proj, hot.astype(BF16), 0, 0) + (1.0 - covered) * cols[:, TOKEN : TOKEN + 1] + pos[...]
    stream_out[0] = stream
    scaled, _ = norm_stats(stream)
    normed = (scaled * cols[:, GAIN1 : GAIN1 + 1] + cols[:, SHIFT1 : SHIFT1 + 1]).astype(BF16)
    lane = lax.broadcasted_iota(jnp.int32, (L, LANES), 1)
    ones = (lane < HEAD + 3).astype(F32).astype(BF16)
    for part in range(3):
        sl = slice(part * width, (part + 1) * width)
        mixed = dg(win[:, sl], normed, 0, 0)
        if part == 0:
            q_out[0, :, :L] = ((mixed + cols[:, BIAS_Q : BIAS_Q + 1]) * Q_SCALE).astype(BF16)
            q_out[0, :, L:] = jnp.zeros((width, LP - L), BF16)
        else:
            if part == 2:
                mixed = mixed + cols[:, BIAS_V : BIAS_V + 1]
            mixed = mixed.astype(BF16)
            kv_out[0, (part - 1) * width : part * width, :] = mixed
            dst = k_rows if part == 1 else v_rows
            for h in range(H):
                dst[0, h] = ones
                dst[0, h, :, :HEAD] = mixed[h * HEAD : (h + 1) * HEAD].T


def pre(seen, vis, wp, cols, pos, win):
    _, a, e = seen.shape
    d = wp.shape[1]
    const = lambda *s: pl.BlockSpec(s, lambda c: (0,) * len(s))
    lead = lambda *s: pl.BlockSpec((1,) + s, lambda c: (c,) + (0,) * len(s))
    return pl.pallas_call(
        pre_kernel,
        grid=(2,),
        in_specs=[lead(a, e), lead(a, 1), const(e, d), const(d, 16), const(d, L), const(d, 3 * d)],
        out_specs=[lead(d, L), lead(d, LP), lead(2 * d, L), lead(H, L, LANES), lead(H, L, LANES)],
        out_shape=[
            jax.ShapeDtypeStruct((2, d, L), F32),
            jax.ShapeDtypeStruct((2, d, LP), BF16),
            jax.ShapeDtypeStruct((2, 2 * d, L), BF16),
            jax.ShapeDtypeStruct((2, H, L, LANES), BF16),
            jax.ShapeDtypeStruct((2, H, L, LANES), BF16),
        ],
        compiler_params=params(),
        cost_estimate=cost(12e9, 2e7),
    )(seen, vis, wp, cols, pos, win)


def attend_kernel(k_rows, q, kt, vt, o_out, lse_out, v_aug):
    row = lax.broadcasted_iota(jnp.int32, (16, L), 0)
    v_aug[:HEAD] = vt[0]
    v_aug[HEAD:] = (row == 0).astype(F32).astype(BF16)
    qf = q[0].astype(F32)
    kf = kt[0].astype(F32)
    bound = jnp.max(jnp.sum(qf * qf, 0, keepdims=True)) * jnp.max(jnp.sum(kf * kf, 0, keepdims=True))
    safe = bound <= SAFE_EXPONENT * SAFE_EXPONENT

    def run(shift):
        for start, size in Q_BLOCKS:
            sl = slice(start, start + size)
            s = dg(k_rows[0, 0, :, :HEAD], q[0, :, sl], 1, 0)
            top = 0.0
            if shift:
                top = jnp.max(s, 0, keepdims=True)
                s = s - top
            e = jnp.exp2(s).astype(BF16)
            o = dg(v_aug[...], e, 1, 0)
            total = o[HEAD : HEAD + 1]
            o_out[0, :, sl] = o[:HEAD] * (1.0 / total)
            lse_out[0, 0, :, sl] = aug_rows(-(top + jnp.log2(total)))

    pl.when(safe)(lambda: run(False))
    pl.when(jnp.logical_not(safe))(lambda: run(True))


def attend(k_rows, q, kv):
    d = q.shape[1]
    head = lambda off: (lambda i: (i // H, i % H + off, 0))
    return pl.pallas_call(
        attend_kernel,
        grid=(2 * H,),
        in_specs=[
            pl.BlockSpec((1, 1, L, LANES), lambda i: (i // H, i % H, 0, 0)),
            pl.BlockSpec((1, HEAD, LP), head(0)),
            pl.BlockSpec((1, HEAD, L), head(0)),
            pl.BlockSpec((1, HEAD, L), head(H)),
        ],
        out_specs=[
            pl.BlockSpec((1, HEAD, LP), head(0)),
            pl.BlockSpec((1, 1, 16, LP), lambda i: (i // H, i % H, 0, 0)),
        ],
        out_shape=[
            jax.ShapeDtypeStruct((2, d, LP), F32),
            jax.ShapeDtypeStruct((2, H, 16, LP), BF16),
        ],
        scratch_shapes=[pltpu.VMEM((HEAD + 16, L), BF16)],
        compiler_params=params(),
        cost_estimate=cost(3e10, 2e7),
    )(k_rows, q, kv, kv)


def attend_back_kernel(k_rows, v_rows, q, lse, do, dsum, kt, dq, dk, dv, q_aug, do_aug):
    q_aug[:HEAD] = q[0]
    q_aug[HEAD : HEAD + 16] = lse[0, 0]
    q_aug[HEAD + 16 :] = jnp.zeros((LANES - HEAD - 16, LP), BF16)
    do_aug[:HEAD] = do[0]
    do_aug[HEAD : HEAD + 16] = dsum[0, 0]
    do_aug[HEAD + 16 :] = jnp.zeros((LANES - HEAD - 16, LP), BF16)
    k_sum = None
    v_sum = None
    for start, size in Q_BLOCKS:
        sl = slice(start, start + size)
        p = jnp.exp2(dg(k_rows[0, 0], q_aug[:, sl], 1, 0))
        dp = dg(v_rows[0, 0], do_aug[:, sl], 1, 0)
        ds = (p * dp).astype(BF16)
        v_part = dg(do_aug[:HEAD, sl], p.astype(BF16), 1, 1)
        k_part = dg(q_aug[:HEAD, sl], ds, 1, 1)
        v_sum = v_part if v_sum is None else v_sum + v_part
        k_sum = k_part if k_sum is None else k_sum + k_part
        if start + size == LP:
            dq[0, :, start:] = (dg(kt[0], ds, 1, 0)[:, : L - start] * (1.0 / math.sqrt(HEAD))).astype(BF16)
        else:
            dq[0, :, sl] = (dg(kt[0], ds, 1, 0) * (1.0 / math.sqrt(HEAD))).astype(BF16)
    dk[0] = (k_sum * (1.0 / LOG2E)).astype(BF16)
    dv[0] = v_sum.astype(BF16)


def attend_back(k_rows, v_rows, q, lse, do, dsum, kv):
    d = q.shape[1]
    head = lambda i: (i // H, i % H, 0)
    wide = lambda i: (i // H, i % H, 0, 0)
    return pl.pallas_call(
        attend_back_kernel,
        grid=(2 * H,),
        in_specs=[
            pl.BlockSpec((1, 1, L, LANES), wide),
            pl.BlockSpec((1, 1, L, LANES), wide),
            pl.BlockSpec((1, HEAD, LP), head),
            pl.BlockSpec((1, 1, 16, LP), wide),
            pl.BlockSpec((1, HEAD, LP), head),
            pl.BlockSpec((1, 1, 16, LP), wide),
            pl.BlockSpec((1, HEAD, L), head),
        ],
        out_specs=[pl.BlockSpec((1, HEAD, L), head)] * 3,
        out_shape=[jax.ShapeDtypeStruct((2, d, L), BF16)] * 3,
        scratch_shapes=[pltpu.VMEM((LANES, LP), BF16)] * 2,
        compiler_params=params(),
        cost_estimate=cost(8e10, 4e7),
    )(k_rows, v_rows, q, lse, do, dsum, kv)


def mlp_parts(d, f, m):
    return [("wm", d // m)] + [(j, d // m) for j in range(f // ROWS)] + [("wr", f // m)]


def mid_kernel(n, m, share, o, stream, up, wpack, be, cols,
               dec, ga_out, do_out, dsum_out, gpack, vec_out,
               wm, we, wr, dwm, dwe, dwr, dvec, dbe, drb, stats, n2, act_s, gl_s, g_s):
    copy = pl.program_id(0)
    ff = pl.program_id(1)
    last = pl.num_programs(1) - 1
    d = wm.shape[0]
    f = wr.shape[0]
    parts = mlp_parts(d, f, m)

    @pl.when((copy == 0) & (ff == 0))
    def _():
        for z in range(m):
            at = 0
            for name, rows in parts:
                piece = wpack[z, at : at + rows]
                dst = slice(z * rows, (z + 1) * rows)
                if name == "wm":
                    wm[dst] = piece
                elif name == "wr":
                    wr[dst] = piece
                else:
                    we[dst, name * ROWS : (name + 1) * ROWS] = piece
                at += rows
        dwm[...] = jnp.zeros_like(dwm)
        dwe[...] = jnp.zeros_like(dwe)
        dwr[...] = jnp.zeros_like(dwr)
        dvec[...] = jnp.zeros_like(dvec)
        dbe[...] = jnp.zeros_like(dbe)
        drb[...] = jnp.zeros_like(drb)

    @pl.when(ff == 0)
    def _():
        ctx = o[0, :, :L].astype(BF16)
        x = stream[0] + dg(wm[...], ctx, 0, 0) + cols[:, BIAS_M : BIAS_M + 1]
        ga_out[0] = x
        mean = jnp.mean(x, 0, keepdims=True)
        center = x - mean
        recip = lax.rsqrt(jnp.mean(center * center, 0, keepdims=True) + EPSILON)
        stats[0:1] = mean
        stats[1:2] = recip
        n2[:d] = (center * recip * cols[:, GAIN2 : GAIN2 + 1] + cols[:, SHIFT2 : SHIFT2 + 1]).astype(BF16)
        row = lax.broadcasted_iota(jnp.int32, (16, L), 0)
        n2[d:] = (row == 0).astype(F32).astype(BF16)
        g = (up[0].astype(F32) * 0.5).astype(BF16)
        g_s[...] = g
        drb[...] += dg(jnp.ones((8, L), BF16), g, 1, 0)

    rows = pl.ds(pl.multiple_of(ff * FFC, FFC), FFC)
    g = g_s[...]
    lifted = dg(we[:, rows], n2[:d], 0, 0) + be[rows, :]
    bell = jnp.exp(-0.5 * lifted * lifted)
    cdf = 0.5 * (1.0 + lax.erf(lifted * ROOT_HALF))
    act = (lifted * cdf).astype(BF16)
    slope = cdf + lifted * bell * INV_ROOT_TWO_PI
    gl = (dg(wr[rows, :], g, 1, 1) * slope).astype(BF16)
    act_s[rows, :] = act
    gl_s[rows, :] = gl
    dwr[rows, :] += dg(act, g, 1, 0)
    grad = dg(n2[...], gl, 1, 1)
    dwe[:, rows] += grad[:d]
    dbe[:, rows] += grad[d : d + 8]

    @pl.when(ff == last)
    def _():
        x = ga_out[0]
        out = x + dg(wr[...], act_s[...], 0, 0) + cols[:, BIAS_R : BIAS_R + 1]
        dec[0] = out.astype(BF16).T
        scaled = (x - stats[0:1]) * stats[1:2]
        e = dg(we[...], gl_s[...], 1, 0)
        dvec[:, 0:1] += jnp.sum(e * scaled, 1, keepdims=True)
        dvec[:, 1:2] += jnp.sum(e, 1, keepdims=True)
        back = norm_back(e, scaled, stats[1:2], cols[:, GAIN2 : GAIN2 + 1])
        ga = g_s[...].T.astype(F32) + back
        ga_out[0] = ga
        gm = ga.astype(BF16)
        dvec[:, 2:3] += jnp.sum(gm.astype(F32), 1, keepdims=True)
        ctx = o[0, :, :L]
        dwm[...] += dg(ctx.astype(BF16), gm, 1, 1)
        do = dg(wm[...], gm, 1, 0).astype(BF16)
        do_out[0, :, :L] = do
        do_out[0, :, L:] = jnp.zeros((d, LP - L), BF16)
        prod = do.astype(F32) * ctx
        for h in range(H):
            dsum_out[0, h, :, :L] = aug_rows(
                -jnp.sum(prod[h * HEAD : (h + 1) * HEAD], 0, keepdims=True)
            )
            dsum_out[0, h, :, L:] = jnp.zeros((16, LP - L), BF16)

    @pl.when((ff == last) & (copy == 1))
    def _():
        plan = segments(parts, share)
        for z in range(m):
            for name, r, slot, at in plan:
                if name == "wm":
                    piece = dwm[z * (d // m) + r : z * (d // m) + r + SEG]
                elif name == "wr":
                    piece = dwr[z * (f // m) + r : z * (f // m) + r + SEG]
                else:
                    piece = dwe[z * (d // m) + r : z * (d // m) + r + SEG, name * ROWS : (name + 1) * ROWS]
                gpack[slot, z, at : at + SEG] = piece.astype(BF16)
            for at in range(len(plan) * SEG, n * share, SEG):
                gpack[at // share, z, at % share : at % share + SEG] = jnp.zeros((SEG, ROWS), BF16)
        turned = dvec[...].T
        vec_out[...] = jnp.zeros_like(vec_out)
        vec_out[BIAS_M : BIAS_M + 1] = turned[2:3]
        vec_out[GAIN2 : GAIN2 + 1] = turned[0:1]
        vec_out[SHIFT2 : SHIFT2 + 1] = turned[1:2]
        vec_out[BIAS_R : BIAS_R + 1] = drb[0:1]
        for j in range(f // ROWS):
            vec_out[BIAS_E + j : BIAS_E + j + 1] = dbe[0:1, j * ROWS : (j + 1) * ROWS]


def mid(n, m, share, o, stream, up, wpack, be, cols):
    d = cols.shape[0]
    f = be.shape[0]
    once = pl.Buffered(1)
    const = lambda *s: pl.BlockSpec(s, lambda c, k: (0,) * len(s), pipeline_mode=once)
    lead = lambda *s: pl.BlockSpec((1,) + s, lambda c, k: (c,) + (0,) * len(s))
    shape = jax.ShapeDtypeStruct
    vm = pltpu.VMEM
    return pl.pallas_call(
        functools.partial(mid_kernel, n, m, share),
        grid=(2, f // FFC),
        in_specs=[lead(d, LP), lead(d, L), lead(L, d), const(*wpack.shape), const(f, 1), const(d, 16)],
        out_specs=[
            lead(L, d), lead(d, L), lead(d, LP), lead(H, 16, LP), const(n, m, share, ROWS), const(16, d),
        ],
        out_shape=[
            shape((2, L, d), BF16), shape((2, d, L), F32), shape((2, d, LP), BF16), shape((2, H, 16, LP), BF16),
            shape((n, m, share, ROWS), BF16), shape((16, d), F32),
        ],
        scratch_shapes=[
            vm((d, d), BF16), vm((d, f), BF16), vm((f, d), BF16),
            vm((d, d), F32), vm((d, f), F32), vm((f, d), F32), vm((d, LANES), F32), vm((8, f), F32), vm((8, d), F32),
            vm((8, L), F32), vm((d + 16, L), BF16),
            vm((f, L), BF16), vm((f, L), BF16), vm((L, d), BF16),
        ],
        compiler_params=params(),
        cost_estimate=cost(5e10, 4e7),
    )(o, stream, up, wpack, be, cols)


def post_kernel(n, m, share, held, seen_len, dq, dk, dv, stream, ga, seen, vis, win, cols, vec_in,
                gpack, gp_out, dwin, dbin, dvec, dwp, n1, gp_s):
    copy = pl.program_id(0)
    clip = lax.axis_index("clip")
    d = win.shape[0]
    e_width = dwp.shape[0]
    seen_pad = seen.shape[1]
    cap = gp_out.shape[1]

    @pl.when(copy == 0)
    def _():
        dwin[...] = jnp.zeros_like(dwin)
        dbin[...] = jnp.zeros_like(dbin)
        dvec[...] = jnp.zeros_like(dvec)
        dwp[...] = jnp.zeros_like(dwp)

    x = stream[0]
    scaled, recip = norm_stats(x)
    n1[:d] = (scaled * cols[:, GAIN1 : GAIN1 + 1] + cols[:, SHIFT1 : SHIFT1 + 1]).astype(BF16)
    row = lax.broadcasted_iota(jnp.int32, (16, L), 0)
    n1[d:] = (row == 0).astype(F32).astype(BF16)
    e = None
    for part, ref in enumerate((dq, dk, dv)):
        sl = slice(part * d, (part + 1) * d)
        grad = dg(n1[...], ref[0], 1, 1)
        dwin[:, sl] += grad[:d]
        dbin[:, sl] += grad[d : d + 8]
        term = dg(win[:, sl], ref[0], 1, 0)
        e = term if e is None else e + term
    dvec[:, 0:1] += jnp.sum(e * scaled, 1, keepdims=True)
    dvec[:, 1:2] += jnp.sum(e, 1, keepdims=True)
    gs = ga[0] + norm_back(e, scaled, recip, cols[:, GAIN1 : GAIN1 + 1])
    hot = one_hot(vis[0], L)
    covered = jnp.sum(hot, 0, keepdims=True)
    dvec[:, 2:3] += jnp.sum(gs * (1.0 - covered), 1, keepdims=True)
    gp = dg(hot.astype(BF16), gs.astype(BF16), 1, 1).astype(BF16)
    gp_s[pl.ds(pl.multiple_of(copy * seen_pad, SEG), seen_pad), :] = gp
    dwp[...] += dg(seen[0], gp, 0, 0)

    @pl.when(copy == 1)
    def _():
        for source in range(n):
            pick = interleave(cap, 2 * seen_pad, clip, source, held, seen_len, seen_pad, n, False)
            gp_out[source] = dg(pick, gp_s[...], 1, 0).astype(BF16)
        turned = dvec[...].T
        row = lax.broadcasted_iota(jnp.int32, (16, d), 0)
        vec = vec_in[...]
        vec = jnp.where(row == TOKEN, turned[2:3], vec)
        vec = jnp.where(row == GAIN1, turned[0:1], vec)
        vec = jnp.where(row == SHIFT1, turned[1:2], vec)
        vec = jnp.where(row == BIAS_Q, dbin[0:1, :d], vec)
        vec = jnp.where(row == BIAS_V, dbin[0:1, 2 * d :], vec).astype(BF16)
        wp_rows = e_width // m
        win_rows = d // m
        plan = segments([("wp", wp_rows)] + [(j, win_rows) for j in range(3)] + [("vec", SEG)], share)
        for z in range(m):
            for name, r, slot, at in plan:
                if name == "wp":
                    piece = dwp[z * wp_rows + r : z * wp_rows + r + SEG].astype(BF16)
                elif name == "vec":
                    piece = vec
                else:
                    piece = dwin[
                        z * win_rows + r : z * win_rows + r + SEG, name * ROWS : (name + 1) * ROWS
                    ].astype(BF16)
                gpack[slot, z, at : at + SEG] = piece
            for at in range(len(plan) * SEG, n * share, SEG):
                gpack[at // share, z, at % share : at % share + SEG] = jnp.zeros((SEG, ROWS), BF16)


def post(n, m, share, held, seen_len, dq, dk, dv, stream, ga, seen, vis, win, cols, vec_in):
    _, a, e = seen.shape
    d = win.shape[0]
    cap = up16(-(-held // n))
    once = pl.Buffered(1)
    const = lambda *s: pl.BlockSpec(s, lambda c: (0,) * len(s), pipeline_mode=once)
    lead = lambda *s: pl.BlockSpec((1,) + s, lambda c: (c,) + (0,) * len(s))
    shape = jax.ShapeDtypeStruct
    vm = pltpu.VMEM
    return pl.pallas_call(
        functools.partial(post_kernel, n, m, share, held, seen_len),
        grid=(2,),
        in_specs=[
            lead(d, L), lead(d, L), lead(d, L), lead(d, L), lead(d, L), lead(a, e), lead(a, 1),
            const(d, 3 * d), const(d, 16), const(16, d),
        ],
        out_specs=[const(n, m, share, ROWS), const(n, cap, d)],
        out_shape=[shape((n, m, share, ROWS), BF16), shape((n, cap, d), BF16)],
        scratch_shapes=[
            vm((d, 3 * d), F32), vm((8, 3 * d), F32), vm((d, LANES), F32), vm((e, d), F32),
            vm((d + 16, L), BF16), vm((2 * a, d), BF16),
        ],
        compiler_params=params(),
        cost_estimate=cost(2e10, 2e7),
    )(dq, dk, dv, stream, ga, seen, vis, win, cols, vec_in)


def leave_kernel(n, m, gpack, gp, mlp, fin, ret, mlp_out, a1, a2s, a2r, tot, tot_b, brecv, fin_s, ret_s, mlp_s,
                 gs, gr, s1, r1, s2, r2, sb, rb, sc, rc, sm, rm, sf, rf):
    clip = lax.axis_index("clip")
    wt = lax.axis_index("wt")
    half = n // 2
    core = lax.rem(clip, 2)
    chip = clip // 2
    partner = clip + 1 - 2 * core
    mlp_s[clip] = mlp[...]
    greet(n, m, clip, wt)
    sends = []
    order = [*range(1, half), 0]
    for j in order:
        spot = lax.rem(chip + j, half)
        copy = remote(gpack.at[2 * spot + 1 - core], a1.at[j], s1.at[j], r1.at[j], partner, wt)
        copy.start()
        sends.append(copy)
    for k in [*range(2, n, 2), *range(1, n, 2)]:
        dest = lax.rem(clip + k, n)
        copy = remote(gp.at[dest], ret_s.at[clip], gs.at[k], gr.at[k], dest, wt)
        copy.start()
        sends.append(copy)
    ret_s[clip] = gp[clip]
    for j in range(1, half):
        copy = remote(mlp_s.at[clip], mlp_s.at[clip], sm.at[j], rm.at[j], lax.rem(clip + 2 * j, n), wt)
        copy.start()
        sends.append(copy)
    copy = remote(mlp_s.at[clip], mlp_s.at[clip], sf.at[0], rf.at[0], partner, wt)
    copy.start()
    sends.append(copy)
    for j in order:
        spot = lax.rem(chip + j, half)
        mine = 2 * spot + core
        remote(gpack.at[mine], a1.at[j], s1.at[j], r1.at[j], partner, wt).wait_recv()
        both = gpack[mine].astype(F32) + a1[j].astype(F32)
        if j == 0:
            tot[...] = both
        else:
            a2s[j] = both.astype(BF16)
            copy = remote(a2s.at[j], a2r.at[j], s2.at[j], r2.at[j], mine, wt)
            copy.start()
            sends.append(copy)
    for j in range(1, half):
        source = lax.rem(clip - 2 * j + n, n)
        remote(a2s.at[j], a2r.at[j], s2.at[j], r2.at[j], source, wt).wait_recv()
        tot[...] += a2r[j].astype(F32)
    tot_b[...] = tot[...].astype(BF16)
    for k in range(1, m):
        zz = lax.rem(wt + k, m)
        copy = remote(tot_b.at[zz], brecv.at[k], sb.at[k], rb.at[k], clip, zz)
        copy.start()
        sends.append(copy)
    for j in range(1, half):
        source = lax.rem(clip - 2 * j + n, n)
        remote(mlp_s.at[source], mlp_s.at[source], sm.at[j], rm.at[j], source, wt).wait_recv()
        copy = remote(mlp_s.at[source], mlp_s.at[source], sf.at[j], rf.at[j], partner, wt)
        copy.start()
        sends.append(copy)
    total = tot[wt]
    for k in range(1, m):
        source = lax.rem(wt - k + m, m)
        remote(tot_b.at[source], brecv.at[k], sb.at[k], rb.at[k], clip, source).wait_recv()
        total = total + brecv[k].astype(F32)
    fin_s[clip] = total.astype(BF16)
    for k in [*range(2, n, 2), *range(1, n, 2)]:
        dest = lax.rem(clip + k, n)
        copy = remote(fin_s.at[clip], fin_s.at[clip], sc.at[k], rc.at[k], dest, wt)
        copy.start()
        sends.append(copy)
    for k in range(1, n):
        source = lax.rem(clip - k + n, n)
        remote(gp.at[source], ret_s.at[source], gs.at[k], gr.at[k], source, wt).wait_recv()
    ret[...] = ret_s[...]
    for j in range(half):
        source = lax.rem(partner - 2 * j + n, n)
        remote(mlp_s.at[source], mlp_s.at[source], sf.at[j], rf.at[j], partner, wt).wait_recv()
    mlp_out[...] = mlp_s[...]
    for k in range(1, n):
        source = lax.rem(clip - k + n, n)
        remote(fin_s.at[source], fin_s.at[source], sc.at[k], rc.at[k], source, wt).wait_recv()
    fin[...] = fin_s[...]
    for copy in sends:
        copy.wait_send()


def leave(n, m, gpack, gp, mlp):
    _, _, share, _ = gpack.shape
    _, cap, d = gp.shape
    whole = pl.BlockSpec(memory_space=pltpu.VMEM)
    shape = jax.ShapeDtypeStruct
    vm = pltpu.VMEM
    dma = pltpu.SemaphoreType.DMA
    half = n // 2
    return pl.pallas_call(
        functools.partial(leave_kernel, n, m),
        in_specs=[whole] * 3,
        out_specs=[whole] * 3,
        out_shape=[shape((n, share, ROWS), BF16), shape((n, cap, d), BF16), shape((n,) + mlp.shape, BF16)],
        scratch_shapes=[
            vm((half, m, share, ROWS), BF16), vm((half, m, share, ROWS), BF16), vm((half, m, share, ROWS), BF16),
            vm((m, share, ROWS), F32), vm((m, share, ROWS), BF16), vm((m, share, ROWS), BF16),
            vm((n, share, ROWS), BF16), vm((n, cap, d), BF16), vm((n,) + mlp.shape, BF16),
            dma((n,)), dma((n,)), dma((half,)), dma((half,)), dma((half,)), dma((half,)),
            dma((m,)), dma((m,)), dma((n,)), dma((n,)),
            dma((half,)), dma((half,)), dma((half,)), dma((half,)),
        ],
        compiler_params=params(collective_id=1, has_side_effects=True),
        cost_estimate=cost(4e9, 4e6),
    )(gpack, gp, mlp)


def finish_kernel(n, m, plan, mlp_plan, fin, ret, mlp, wp, egrad, dwp, dwin, dwm, dwe, dwr, *vecs):
    clip = lax.axis_index("clip")
    wt = lax.axis_index("wt")
    held = egrad.shape[0]
    cap = ret.shape[1]
    row = lax.broadcasted_iota(jnp.int32, (held, cap), 0)
    col = lax.broadcasted_iota(jnp.int32, (held, cap), 1)
    own = None
    for dest in range(n):
        start = first_slot(dest, held, clip, n)
        stop = first_slot(dest + 1, held, clip, n)
        hot = ((row - start == col) & (row < stop)).astype(F32).astype(BF16)
        part = dg(hot, ret[dest], 1, 0)
        own = part if own is None else own + part
    egrad[...] = dg(own.astype(BF16), wp[...], 1, 1).astype(BF16)
    for name, r, slot, at in plan:
        piece = fin[slot, at : at + SEG].astype(F32)
        if name == "wp":
            dwp[r : r + SEG] = piece
        elif name != "vec":
            dwin[r : r + SEG, name * ROWS : (name + 1) * ROWS] = piece
        else:
            for z in range(m):
                @pl.when(wt == z)
                def _():
                    for i, ref in enumerate(vecs[:BIAS_E]):
                        w = ref.shape[1]
                        ref[...] = piece[i : i + 1, z * w : (z + 1) * w]
                    w = vecs[BIAS_E].shape[1]
                    line = BIAS_E + z * w // ROWS
                    vecs[BIAS_E][...] = piece[line : line + 1, z * w % ROWS : z * w % ROWS + w]
    for name, r, slot, at in mlp_plan:
        piece = mlp[slot, at : at + SEG].astype(F32)
        if name == "wm":
            dwm[r : r + SEG] = piece
        elif name == "wr":
            dwr[r : r + SEG] = piece
        else:
            dwe[r : r + SEG, name * ROWS : (name + 1) * ROWS] = piece


def finish(n, m, held, fin, ret, mlp, wp, f):
    e, d = wp.shape
    whole = pl.BlockSpec(memory_space=pltpu.VMEM)
    shape = jax.ShapeDtypeStruct
    plan = segments([("wp", e // m)] + [(j, d // m) for j in range(3)] + [("vec", SEG)], fin.shape[1])
    mlp_plan = segments(mlp_parts(d, f, m), mlp.shape[1])
    outs = [shape((held, e), BF16)] + [
        shape((r // m, c), F32) for r, c in ((e, d), (d, 3 * d), (d, d), (d, f), (f, d))
    ] + [shape((1, d // m), F32)] * BIAS_E + [shape((1, f // m), F32)]
    return pl.pallas_call(
        functools.partial(finish_kernel, n, m, plan, mlp_plan),
        in_specs=[whole] * 4,
        out_specs=[whole] * len(outs),
        out_shape=outs,
        compiler_params=params(),
        cost_estimate=cost(1e9, 4e6),
    )(fin, ret, mlp, wp)


def per_device(encoded, visible_at, wp, token, gain1, shift1, win, bq, bv, wm, bm, gain2, shift2, we, be, wr, br, upstream):
    n = lax.axis_size("clip")
    m = lax.axis_size("wt")
    held = encoded.shape[0]
    seen_len = visible_at.shape[1]
    d = wp.shape[1]
    f = be.shape[0] * m
    pieces = [wm] + [we[:, j * ROWS : (j + 1) * ROWS] for j in range(f // ROWS)] + [wr]
    local = jnp.concatenate(pieces, 0)
    wpack = lax.all_gather(local, "wt", axis=0, tiled=True).reshape(m, local.shape[0], ROWS)
    vecs = (token, gain1, shift1, bq, bv, bm, gain2, shift2, br, be)
    seen, vis, wp_full, win_full, cols, be_col = enter(n, m, encoded, visible_at, wp, win, vecs)
    pos = jnp.asarray(position_table(d))
    stream, q, kv, k_rows, v_rows = pre(seen, vis, wp_full, cols, pos, win_full)
    o, lse = attend(k_rows, q, kv)
    share = up16(-(-local.shape[0] // n))
    dec, ga, do, dsum, mlp, vec2 = mid(n, m, share, o, stream, upstream.reshape(2, L, d), wpack, be_col, cols)
    mlp = mlp.reshape(n * m * share, ROWS)
    mlp = lax.psum_scatter(mlp, "clip", scatter_dimension=0, tiled=True)
    mlp = lax.psum_scatter(mlp, "wt", scatter_dimension=0, tiled=True)
    dq, dk, dv = attend_back(k_rows, v_rows, q, lse, do, dsum, kv)
    share = up16(-(-(wp.shape[0] + 3 * win.shape[0] + SEG) // n))
    gpack, gp = post(n, m, share, held, seen_len, dq, dk, dv, stream, ga, seen, vis, win_full, cols, vec2)
    fin, ret, mlp = leave(n, m, gpack, gp, mlp)
    egrad, dwp, dwin, dwm, dwe, dwr, *small = finish(n, m, held, fin, ret, mlp, wp_full, f)
    t, g1, s1, vq, vv, vm, g2, s2, vr, ve = [v.reshape(-1) for v in small]
    return (
        dec.reshape(2 * L, d), egrad, dwp, t, g1, s1, dwin, vq, vv, dwm, vm, g2, s2, dwe, ve, dwr, vr,
    )


def solution(mesh):
    both, wt = P(("clip", "wt"), None), P("wt")
    mat = P("wt", None)
    params_in = (mat, wt, wt, wt, mat, wt, wt, mat, wt, wt, wt, mat, wt, mat, wt)
    return jax.shard_map(
        per_device,
        mesh=mesh,
        in_specs=(both, both) + params_in + (both,),
        out_specs=(both, both) + params_in,
        check_vma=False,
    )
```

time: 505 us -> 306 us (0.61)
  waiting for transfers between devices: 118 us -> 0.07 us
  blocking collectives: 106 us -> 0 us
  Pallas kernels: 208 us -> 279 us
  other arithmetic: 26 us -> 1.2 us
  starting transfers between devices: 9.42 us -> 0.12 us
  local copies, waits for them, and re-layouts: 15.6 us -> 7.59 us
    pallas_call x3 -> x6, Pallas kernels: 90.5 us -> 151 us  [the longest x1 53.1 us: mid(): pl.pallas_call(functools.partial(mid_kernel, n, m, share), grid=(2, f //...]
    reduce_scatter x5 -> x2, waiting for transfers between devices: 59.2 us -> 0.02 us  [the longest x1 0.02 us: per_device(): mlp = lax.psum_scatter(mlp, 'clip', scatter_dimension=0, tiled=True)]
    all_gather x3 -> x0, blocking collectives: 57.5 us -> none  [per_device(): lax.all_gather(weights[i], 'wt', axis=0, tiled=True)]
    psum x1 -> x0, waiting for transfers between devices: 57.4 us -> none  [per_device(): total = lax.psum(tuple((out[i] for i in big)) + (pack,), 'clip')]
    unnamed x2 -> x0, blocking collectives: 36.7 us -> none
    convert_element_type x13 -> x0, other arithmetic: 18.2 us -> none  [the longest x5 9.23 us: per_device(): v.astype(BF16)]
    psum x1 -> x0, blocking collectives: 12.2 us -> none  [per_device(): total = lax.psum(tuple((out[i] for i in big)) + (pack,), 'clip')]
    pallas_call x1, Pallas kernels: 82.8 us -> 93.1 us  [attend_back(): pl.pallas_call(attend_back_kernel, grid=(2 * H,), in_specs=[pl.BlockSpec(...]
  transfers between devices with their start and end apart: 10 -> 3, of which waited for: 3 -> 0; matrix products, arithmetic and copies ran while one was open for 7% -> 0% of each run, Pallas kernels for 31% -> 63%
where the time goes in v2:
time: 306 us; the launch traced here: 302 us
  Pallas kernels  279 us (91%)
  between operations  14 us (5%)
  local copies, waits for them, and re-layouts  7.59 us (2%)
    pallas_call x1, Pallas kernels, attend_back(): pl.pallas_call(attend_back_kernel, grid=(2 * H,), in_specs=[pl.BlockSpec(...  93.1 us
    pallas_call x1, Pallas kernels, mid(): pl.pallas_call(functools.partial(mid_kernel, n, m, share), grid=(2, f //...  53.1 us
    pallas_call x1, Pallas kernels, attend(): pl.pallas_call(attend_kernel, grid=(2 * H,), in_specs=[pl.BlockSpec((1, 1...  34.8 us
    pallas_call x1, Pallas kernels, leave(): pl.pallas_call(functools.partial(leave_kernel, n, m), in_specs=[whole] *...  32.1 us
    pallas_call x1, Pallas kernels, enter(): pl.pallas_call(functools.partial(enter_kernel, n, m, share, cap, seen_pad...  27.3 us
    pallas_call x1, Pallas kernels, post(): pl.pallas_call(functools.partial(post_kernel, n, m, share, held, seen_len...  20.7 us
    pallas_call x1, Pallas kernels, pre(): pl.pallas_call(pre_kernel, grid=(2,), in_specs=[lead(a, e), lead(a, 1), c...  13.7 us
  transfers between devices with their start and end apart: 3, of which 0 were waited for; matrix products, arithmetic and copies ran while one was open for 0% of the time, Pallas kernels for 63%

profile of v2, /device:TPU:0, one launch (start us, length us, event | category | flops | bytes accessed | tf_op | source)
XLA Modules:
  0.0 302.0 jit_solution(2500226677396048569)
XLA Ops:
  7.2 0.0 all-gather.2.cloned.1.call-start
  7.2 0.9 constant_dynamic-update-slice_fusion.1
  8.1 0.9 slice_dynamic-update-slice_fusion.3
  9.0 0.9 slice_dynamic-update-slice_fusion.2
  9.9 0.9 slice_dynamic-update-slice_fusion.1
  10.8 0.9 slice_dynamic-update-slice_fusion
  11.7 1.0 constant_dynamic-update-slice_fusion
  12.8 0.0 copy-start
  12.8 0.8 copy-done
  13.6 0.0 all-gather.2.cloned.1.call-update
  13.6 0.0 reduce-scatter.3.cloned.1.call-start
  13.7 1.2 broadcast_in_dim.39.refs_13_
  14.9 27.3 %shard_map.314 = (bf16[2,160,768]{2,1,0:T(8,128)(2,1)}, f32[2,160,1]{2,1,0:T(8,128)}, bf16[768,384]{1,0:T(8,128)(2,1)}, bf16[384,1152]{1,0:T(8,128)(2,1)}, f32[384,16]{1,0:T(8,128)}, /*index=5*/f32[1536,1]{1,0:T(8,128)}) custom-call(bf16[314,768]{1,0:T(8,128)(2,1)} %refs_0_.1, s32[2,157]{1,0:T(2,128)} %refs_1_.1, bf16[192,384]{1,0:T(8,128)(2,1)} %refs_2_.1, ...), custom_call_target="tpu_custom_call" | custom-call | flops 6000000000 | bytes 4000000 | tf_op jit(solution)/shard_map/pallas_call | solution.py:257
  42.2 13.7 %shard_map.315 = (f32[2,384,1568]{2,1,0:T(8,128)}, bf16[2,384,1664]{2,1,0:T(8,128)(2,1)}, bf16[2,768,1568]{2,1,0:T(8,128)(2,1)}, bf16[2,6,1568,128]{3,2,1,0:T(8,128)(2,1)}, bf16[2,6,1568,128]{3,2,1,0:T(8,128)(2,1)}) custom-call(bf16[2,160,768]{2,1,0:T(8,128)(2,1)} %get-tuple-element.60.seen, f32[2,160,1]{2,1,0:T(8,128)} %get-tuple-element.61.vis, ...), custom_call_target="tpu_custom_call" | custom-call | flops 12000000000 | bytes 20000000 | tf_op jit(solution)/shard_map/pallas_call | solution.py:309
  55.9 34.8 %shard_map.316 = (f32[2,384,1664]{2,1,0:T(8,128)}, bf16[2,6,16,1664]{3,2,1,0:T(8,128)(2,1)}) custom-call(bf16[2,6,1568,128]{3,2,1,0:T(8,128)(2,1)} %get-tuple-element.65.k_rows, bf16[2,384,1664]{2,1,0:T(8,128)(2,1)} %get-tuple-element.66.q, bf16[2,768,1568]{2,1,0:T(8,128)(2,1)} %get-tuple-element.67.kt.vt, bf16[2,768,1568]{2,1,0:T(8,128)(2,1)} %get-tuple-element.67.kt.vt), custom_call_target="tpu_custom_call" | custom-call | flops 30000001024 | bytes 20000000 | tf_op jit(solution)/shard_map/pallas_call | solution.py:356
  90.7 0.0 all-gather.2.cloned.1.call-done
  90.7 53.1 %shard_map.317 = (bf16[2,1568,384]{2,1,0:T(8,128)(2,1)}, f32[2,384,1568]{2,1,0:T(8,128)}, bf16[2,384,1664]{2,1,0:T(8,128)(2,1)}, bf16[2,6,16,1664]{3,2,1,0:T(8,1...) custom-call(f32[2,384,1664]{2,1,0:T(8,128)} %get-tuple-element.68.o, ...), custom_call_target="tpu_custom_call" | custom-call | flops 49999998976 | bytes 40000000 | tf_op jit(solution)/shard_map/pallas_call | solution.py:554
  143.8 0.0 reduce-scatter.3.cloned.1.call-update
  143.8 0.0 reduce-scatter.5.cloned.1.call-start
  143.9 93.1 %shard_map.318 = (bf16[2,384,1568]{2,1,0:T(8,128)(2,1)}, bf16[2,384,1568]{2,1,0:T(8,128)(2,1)}, bf16[2,384,1568]{2,1,0:T(8,128)(2,1)}) custom-call(bf16[2,6,1568,128]{3,2,1,0:T(8,128)(2,1)} %get-tuple-element.65.k_rows, bf16[2,6,1568,128]{3,2,1,0:T(8,128)(2,1)} %get-tuple-element.72.v_rows, bf16[2,384,1664]{2,1,0:T(8,128)(2,1)} %get-tuple-element.66.q, ...), custom_call_target="tpu_custom_call" | custom-call | flops 80000000000 | bytes 40000000 | tf_op jit(solution)/shard_map/pallas_call | solution.py:409
  236.9 0.0 reduce-scatter.3.cloned.1.call-done
  237.0 0.0 reduce-scatter.5.cloned.1.call-update
  237.0 20.7 %shard_map.319 = (bf16[8,4,64,384]{3,2,1,0:T(8,128)(2,1)}, bf16[8,48,384]{2,1,0:T(8,128)(2,1)}) custom-call(bf16[2,384,1568]{2,1,0:T(8,128)(2,1)} %get-tuple-element.76.dq, bf16[2,384,1568]{2,1,0:T(8,128)(2,1)} %get-tuple-element.77.dk, bf16[2,384,1568]{2,1,0:T(8,128)(2,1)} %get-tuple-element.78.dv, f32[2,384,1568]{2,1,0:T(8,128)} %get-tuple-element.69.stream, ...), custom_call_target="tpu_custom_call" | custom-call | flops 20000000000 | bytes 20000000 | tf_op jit(solution)/shard_map/pallas_call | solution.py:655
  257.7 0.0 reduce-scatter.5.cloned.1.call-done.mlp
  257.7 32.1 %shard_map.320 = (bf16[8,64,384]{2,1,0:T(8,128)(2,1)}, bf16[8,48,384]{2,1,0:T(8,128)(2,1)}, bf16[8,112,384]{2,1,0:T(8,128)(2,1)}) custom-call(bf16[8,4,64,384]{3,2,1,0:T(8,128)(2,1)} %get-tuple-element.81.gpack, bf16[8,48,384]{2,1,0:T(8,128)(2,1)} %get-tuple-element.82.gp, bf16[112,384]{1,0:T(8,128)(2,1)} %reduce-scatter.5.cloned.1.call-done.mlp), custom_call_target="tpu_custom_call" | custom-call | flops 4000000000 | bytes 4000000 | tf_op jit(solution)/shard_map/pallas_call | solution.py:766
  289.8 4.2 %shard_map.321 = (bf16[314,768]{1,0:T(8,128)(2,1)}, f32[192,384]{1,0:T(8,128)}, f32[96,1152]{1,0:T(8,128)}, f32[96,384]{1,0:T(8,128)}, f32[96,1536]{1,0:T(8,128)...) custom-call(bf16[8,64,384]{2,1,0:T(8,128)(2,1)} %get-tuple-element.8, ...), custom_call_target="tpu_custom_call" | custom-call | flops 1000000000 | bytes 4000000 | tf_op jit(solution)/shard_map/pallas_call | solution.py:834
  294.0 1.2 reduce
Async XLA Ops:
  7.2 83.5 %all-gather.2.cloned.1.call-start = ((), (), s32[]{:S(2)}) async-start(), calls=%async_computation.2 | async-start | bytes 3317760 | tf_op jit(solution)/shard_map/all_gather | solution.py:853
  12.8 0.8 copy-start
  13.6 223.3 %reduce-scatter.3.cloned.1.call-start = ((), (), s32[]{:S(2)}) async-start(), calls=%async_computation.3 | async-start | bytes 3096576 | tf_op jit(solution)/shard_map/reduce_scatter | solution.py:862
  143.8 113.8 %reduce-scatter.5.cloned.1.call-start = ((), (), s32[]{:S(2)}) async-start(), calls=%async_computation.4 | async-start | bytes 430080 | tf_op jit(solution)/shard_map/reduce_scatter | solution.py:863
Sparse Core Ops, SparseCore 0:
  13.7 58.0 all-gather.1
  143.9 43.6 reduce-scatter.2
  237.1 19.7 reduce-scatter.4

commit v3 on v2

--- a/solution.py
+++ b/solution.py
@@ -14,14 +14,15 @@
 L = 1568
 LANES = 128
 LP = -(-L // LANES) * LANES
+KP = L
 EPSILON = 1e-06
 LOG2E = math.log2(math.e)
 Q_SCALE = LOG2E / math.sqrt(HEAD)
 ROOT_HALF = math.sqrt(0.5)
 INV_ROOT_TWO_PI = 1.0 / math.sqrt(2.0 * math.pi)
-SAFE_EXPONENT = 100.0
+SAFE_EXPONENT = 60.0
 VMEM_LIMIT = 60 * 2**20
-FFC = 256
+FFC = 512
 Q_BLOCKS = ((0, 896), (896, LP - 896))
 F32 = jnp.float32
 BF16 = jnp.bfloat16
@@ -60,7 +61,7 @@
 
 
 def position_table(width):
-    places = np.arange(L, dtype=np.float64)[None, :]
+    places = np.arange(LP, dtype=np.float64)[None, :]
     columns = np.arange(width)
     exponent = (2 * (columns // 2)).astype(np.float64) / width
     angles = places / np.power(10000.0, exponent)[:, None]
@@ -151,7 +152,7 @@
     )
     vec_s[...] = jnp.zeros_like(vec_s)
     for i, ref in enumerate(vecs):
-        vec_s[i : i + 1, : ref.shape[1]] = ref[...].astype(F32)
+        vec_s[i, : ref.shape[0]] = ref[...].astype(F32)
     for name, r, slot, at in plan:
         if name == "wp":
             piece = wp_in[r : r + SEG]
@@ -165,11 +166,23 @@
     greet(n, m, clip, wt)
 
     sends = []
+    partner = clip + 1 - 2 * lax.rem(clip, 2)
     for k in range(1, m):
         copy = remote(pack.at[clip], gath.at[clip, wt], zs.at[k], zr.at[k], clip, lax.rem(wt + k, m))
         copy.start()
         sends.append(copy)
     gath[clip, wt] = pack[clip]
+
+    def spread(k):
+        z = lax.rem(wt - k + m, m)
+        for j in [*range(1, half), 0]:
+            piece = gath.at[clip, z]
+            dest = lax.rem(clip + 2 * j, n) if j else partner
+            copy = remote(piece, piece, bs.at[j, k], br.at[j, k], dest, wt)
+            copy.start()
+            sends.append(copy)
+
+    spread(0)
 
     rows_at = lax.broadcasted_iota(jnp.int32, (cap, held), 0)
     cols_at = lax.broadcasted_iota(jnp.int32, (cap, held), 1)
@@ -189,14 +202,7 @@
     for k in range(1, m):
         source = lax.rem(wt - k + m, m)
         remote(pack.at[clip], gath.at[clip, source], zs.at[k], zr.at[k], clip, source).wait_recv()
-    for j in range(1, half):
-        copy = remote(gath.at[clip], gath.at[clip], bs.at[j], br.at[j], lax.rem(clip + 2 * j, n), wt)
-        copy.start()
-        sends.append(copy)
-    partner = clip + 1 - 2 * lax.rem(clip, 2)
-    copy = remote(gath.at[clip], gath.at[clip], fs.at[0], fr.at[0], partner, wt)
-    copy.start()
-    sends.append(copy)
+        spread(k)
 
     vis_s[...] = jnp.full(vis_s.shape, -1.0, F32)
     vis_s[0:2, :seen] = vis_in[...].astype(F32)
@@ -204,12 +210,15 @@
     for copy_at in range(2):
         vis_out[copy_at] = turned[:seen_pad, copy_at : copy_at + 1]
 
-    for j in range(1, half):
-        source = lax.rem(clip - 2 * j + n, n)
-        remote(gath.at[source], gath.at[source], bs.at[j], br.at[j], source, wt).wait_recv()
-        copy = remote(gath.at[source], gath.at[source], fs.at[j], fr.at[j], partner, wt)
-        copy.start()
-        sends.append(copy)
+    for k in range(m):
+        z = lax.rem(wt - k + m, m)
+        for j in range(1, half):
+            source = lax.rem(clip - 2 * j + n, n)
+            piece = gath.at[source, z]
+            remote(piece, piece, bs.at[j, k], br.at[j, k], source, wt).wait_recv()
+            copy = remote(piece, piece, fs.at[j, k], fr.at[j, k], partner, wt)
+            copy.start()
+            sends.append(copy)
 
     for k in range(1, n):
         source = lax.rem(clip - k + n, n)
@@ -223,9 +232,13 @@
     seen_out[0] = total[:seen_pad]
     seen_out[1] = total[seen_pad:]
 
-    for j in range(half):
-        source = lax.rem(partner - 2 * j + n, n)
-        remote(gath.at[source], gath.at[source], fs.at[j], fr.at[j], partner, wt).wait_recv()
+    for k in range(m):
+        z = lax.rem(wt - k + m, m)
+        for j in range(half):
+            source = lax.rem(partner - 2 * j + n, n)
+            piece = gath.at[source, z]
+            sems = (fs.at[j, k], fr.at[j, k]) if j else (bs.at[0, k], br.at[0, k])
+            remote(piece, piece, *sems, partner, wt).wait_recv()
     for z in range(m):
         for name, r, slot, at in plan:
             piece = gath[slot, z, at : at + SEG]
@@ -233,14 +246,40 @@
                 wp[z * wp_rows + r : z * wp_rows + r + SEG] = piece
             elif name == "vec":
                 turned = piece.astype(F32).T
-                small = vecs[0].shape[1]
+                small = vecs[0].shape[0]
                 cols[z * small : (z + 1) * small] = turned[:small]
-                large = vecs[BIAS_E].shape[1]
+                large = vecs[BIAS_E].shape[0]
                 be[z * large : (z + 1) * large] = turned[:large, BIAS_E : BIAS_E + 1]
             else:
                 win[z * win_rows + r : z * win_rows + r + SEG, name * ROWS : (name + 1) * ROWS] = piece
     for copy in sends + row_sends:
         copy.wait_send()
+
+
+def pack_kernel(wm, we, wr, out, sems):
+    rows = wm.shape[0]
+    moves = [(wm, 0, rows)]
+    moves += [(we.at[:, j * ROWS : (j + 1) * ROWS], rows * (j + 1), rows) for j in range(we.shape[1] // ROWS)]
+    moves += [(wr, rows * len(moves), wr.shape[0])]
+    copies = []
+    for i, (src, at, size) in enumerate(moves):
+        copy = pltpu.make_async_copy(src, out.at[at : at + size], sems.at[i])
+        copy.start()
+        copies.append(copy)
+    for copy in copies:
+        copy.wait()
+
+
+def pack_mlp(wm, we, wr):
+    rows = wm.shape[0] + wm.shape[0] * (we.shape[1] // ROWS) + wr.shape[0]
+    return pl.pallas_call(
+        pack_kernel,
+        in_specs=[pl.BlockSpec(memory_space=pl.ANY)] * 3,
+        out_specs=pl.BlockSpec(memory_space=pl.ANY),
+        out_shape=jax.ShapeDtypeStruct((rows, ROWS), BF16),
+        scratch_shapes=[pltpu.SemaphoreType.DMA((2 + we.shape[1] // ROWS,))],
+        cost_estimate=cost(0, 1.3e6),
+    )(wm, we, wr)
 
 
 def enter(n, m, enc, vis, wp, win, vecs):
@@ -253,7 +292,7 @@
     whole = pl.BlockSpec(memory_space=pltpu.VMEM)
     shape = jax.ShapeDtypeStruct
     dma = pltpu.SemaphoreType.DMA
-    ins = (enc, vis, wp, win, *[v[None, :] for v in vecs])
+    ins = (enc, vis, wp, win, *vecs)
     return pl.pallas_call(
         functools.partial(enter_kernel, n, m, share, cap, seen_pad),
         in_specs=[whole] * len(ins),
@@ -266,7 +305,8 @@
             pltpu.VMEM((n, share, ROWS), BF16), pltpu.VMEM((n, m, share, ROWS), BF16),
             pltpu.VMEM((n, cap, e), BF16), pltpu.VMEM((n, cap, e), BF16),
             pltpu.VMEM((SEG, ROWS), F32), pltpu.VMEM((8, 2 * LANES), F32),
-            dma((m,)), dma((m,)), dma((n // 2,)), dma((n // 2,)), dma((n // 2,)), dma((n // 2,)), dma((n,)), dma((n,)),
+            dma((m,)), dma((m,)), dma((n // 2, m)), dma((n // 2, m)), dma((n // 2, m)), dma((n // 2, m)),
+            dma((n,)), dma((n,)),
         ],
         compiler_params=params(collective_id=0, has_side_effects=True),
         cost_estimate=cost(6e9, 4e6),
@@ -276,29 +316,30 @@
 def pre_kernel(seen, vis, wp, cols, pos, win, stream_out, q_out, kv_out, k_rows, v_rows):
     width = wp.shape[1]
     proj = dg(seen[0], wp[...], 1, 0).astype(BF16)
-    hot = one_hot(vis[0], L)
+    hot = one_hot(vis[0], LP)
     covered = jnp.sum(hot, 0, keepdims=True)
     stream = dg(proj, hot.astype(BF16), 0, 0) + (1.0 - covered) * cols[:, TOKEN : TOKEN + 1] + pos[...]
     stream_out[0] = stream
     scaled, _ = norm_stats(stream)
     normed = (scaled * cols[:, GAIN1 : GAIN1 + 1] + cols[:, SHIFT1 : SHIFT1 + 1]).astype(BF16)
-    lane = lax.broadcasted_iota(jnp.int32, (L, LANES), 1)
-    ones = (lane < HEAD + 3).astype(F32).astype(BF16)
+    lane = lax.broadcasted_iota(jnp.int32, (KP, LANES), 1)
+    token = lax.broadcasted_iota(jnp.int32, (KP, LANES), 0)
+    ones = ((lane < HEAD + 3) & (token < L)).astype(F32).astype(BF16)
     for part in range(3):
         sl = slice(part * width, (part + 1) * width)
         mixed = dg(win[:, sl], normed, 0, 0)
         if part == 0:
-            q_out[0, :, :L] = ((mixed + cols[:, BIAS_Q : BIAS_Q + 1]) * Q_SCALE).astype(BF16)
-            q_out[0, :, L:] = jnp.zeros((width, LP - L), BF16)
+            q_out[0] = ((mixed + cols[:, BIAS_Q : BIAS_Q + 1]) * Q_SCALE).astype(BF16)
         else:
             if part == 2:
                 mixed = mixed + cols[:, BIAS_V : BIAS_V + 1]
             mixed = mixed.astype(BF16)
-            kv_out[0, (part - 1) * width : part * width, :] = mixed
+            kv_out[0, (part - 1) * width : part * width, :L] = mixed[:, :L]
+            kv_out[0, (part - 1) * width : part * width, L:] = jnp.zeros((width, LP - L), BF16)
             dst = k_rows if part == 1 else v_rows
             for h in range(H):
                 dst[0, h] = ones
-                dst[0, h, :, :HEAD] = mixed[h * HEAD : (h + 1) * HEAD].T
+                dst[0, h, :L, :HEAD] = mixed[h * HEAD : (h + 1) * HEAD].T[:L]
 
 
 def pre(seen, vis, wp, cols, pos, win):
@@ -309,24 +350,25 @@
     return pl.pallas_call(
         pre_kernel,
         grid=(2,),
-        in_specs=[lead(a, e), lead(a, 1), const(e, d), const(d, 16), const(d, L), const(d, 3 * d)],
-        out_specs=[lead(d, L), lead(d, LP), lead(2 * d, L), lead(H, L, LANES), lead(H, L, LANES)],
+        in_specs=[lead(a, e), lead(a, 1), const(e, d), const(d, 16), const(d, LP), const(d, 3 * d)],
+        out_specs=[lead(d, LP), lead(d, LP), lead(2 * d, LP), lead(H, KP, LANES), lead(H, KP, LANES)],
         out_shape=[
-            jax.ShapeDtypeStruct((2, d, L), F32),
+            jax.ShapeDtypeStruct((2, d, LP), F32),
             jax.ShapeDtypeStruct((2, d, LP), BF16),
-            jax.ShapeDtypeStruct((2, 2 * d, L), BF16),
-            jax.ShapeDtypeStruct((2, H, L, LANES), BF16),
-            jax.ShapeDtypeStruct((2, H, L, LANES), BF16),
+            jax.ShapeDtypeStruct((2, 2 * d, LP), BF16),
+            jax.ShapeDtypeStruct((2, H, KP, LANES), BF16),
+            jax.ShapeDtypeStruct((2, H, KP, LANES), BF16),
         ],
         compiler_params=params(),
         cost_estimate=cost(12e9, 2e7),
     )(seen, vis, wp, cols, pos, win)
 
 
-def attend_kernel(k_rows, q, kt, vt, o_out, lse_out, v_aug):
-    row = lax.broadcasted_iota(jnp.int32, (16, L), 0)
-    v_aug[:HEAD] = vt[0]
-    v_aug[HEAD:] = (row == 0).astype(F32).astype(BF16)
+def attend_kernel(k_rows, q, kt, vt, o_out, inv_out, e_out, v_aug):
+    row = lax.broadcasted_iota(jnp.int32, (16, KP), 0)
+    token = lax.broadcasted_iota(jnp.int32, (16, KP), 1)
+    v_aug[:HEAD] = vt[0, :, :KP]
+    v_aug[HEAD:] = ((row == 0) & (token < L)).astype(F32).astype(BF16)
     qf = q[0].astype(F32)
     kf = kt[0].astype(F32)
     bound = jnp.max(jnp.sum(qf * qf, 0, keepdims=True)) * jnp.max(jnp.sum(kf * kf, 0, keepdims=True))
@@ -336,15 +378,16 @@
         for start, size in Q_BLOCKS:
             sl = slice(start, start + size)
             s = dg(k_rows[0, 0, :, :HEAD], q[0, :, sl], 1, 0)
-            top = 0.0
             if shift:
-                top = jnp.max(s, 0, keepdims=True)
-                s = s - top
+                key = lax.broadcasted_iota(jnp.int32, (KP, size), 0)
+                s = jnp.where(key < L, s, -jnp.inf)
+                s = s - jnp.max(s, 0, keepdims=True)
             e = jnp.exp2(s).astype(BF16)
+            e_out[0, 0, :, sl] = e
             o = dg(v_aug[...], e, 1, 0)
-            total = o[HEAD : HEAD + 1]
-            o_out[0, :, sl] = o[:HEAD] * (1.0 / total)
-            lse_out[0, 0, :, sl] = aug_rows(-(top + jnp.log2(total)))
+            inv = 1.0 / o[HEAD : HEAD + 1]
+            o_out[0, :, sl] = o[:HEAD] * inv
+            inv_out[0, 0, :, sl] = inv
 
     pl.when(safe)(lambda: run(False))
     pl.when(jnp.logical_not(safe))(lambda: run(True))
@@ -353,33 +396,33 @@
 def attend(k_rows, q, kv):
     d = q.shape[1]
     head = lambda off: (lambda i: (i // H, i % H + off, 0))
+    wide = lambda i: (i // H, i % H, 0, 0)
     return pl.pallas_call(
         attend_kernel,
         grid=(2 * H,),
         in_specs=[
-            pl.BlockSpec((1, 1, L, LANES), lambda i: (i // H, i % H, 0, 0)),
+            pl.BlockSpec((1, 1, KP, LANES), wide),
             pl.BlockSpec((1, HEAD, LP), head(0)),
-            pl.BlockSpec((1, HEAD, L), head(0)),
-            pl.BlockSpec((1, HEAD, L), head(H)),
+            pl.BlockSpec((1, HEAD, LP), head(0)),
+            pl.BlockSpec((1, HEAD, LP), head(H)),
         ],
         out_specs=[
             pl.BlockSpec((1, HEAD, LP), head(0)),
-            pl.BlockSpec((1, 1, 16, LP), lambda i: (i // H, i % H, 0, 0)),
+            pl.BlockSpec((1, 1, 1, LP), wide),
+            pl.BlockSpec((1, 1, KP, LP), wide),
         ],
         out_shape=[
             jax.ShapeDtypeStruct((2, d, LP), F32),
-            jax.ShapeDtypeStruct((2, H, 16, LP), BF16),
-        ],
-        scratch_shapes=[pltpu.VMEM((HEAD + 16, L), BF16)],
+            jax.ShapeDtypeStruct((2, H, 1, LP), F32),
+            jax.ShapeDtypeStruct((2, H, KP, LP), BF16),
+        ],
+        scratch_shapes=[pltpu.VMEM((HEAD + 16, KP), BF16)],
         compiler_params=params(),
         cost_estimate=cost(3e10, 2e7),
     )(k_rows, q, kv, kv)
 
 
-def attend_back_kernel(k_rows, v_rows, q, lse, do, dsum, kt, dq, dk, dv, q_aug, do_aug):
-    q_aug[:HEAD] = q[0]
-    q_aug[HEAD : HEAD + 16] = lse[0, 0]
-    q_aug[HEAD + 16 :] = jnp.zeros((LANES - HEAD - 16, LP), BF16)
+def attend_back_kernel(e, v_rows, q, do, dsum, kt, dq, dk, dv, do_aug):
     do_aug[:HEAD] = do[0]
     do_aug[HEAD : HEAD + 16] = dsum[0, 0]
     do_aug[HEAD + 16 :] = jnp.zeros((LANES - HEAD - 16, LP), BF16)
@@ -387,22 +430,20 @@
     v_sum = None
     for start, size in Q_BLOCKS:
         sl = slice(start, start + size)
-        p = jnp.exp2(dg(k_rows[0, 0], q_aug[:, sl], 1, 0))
+        p = e[0, 0, :, sl]
         dp = dg(v_rows[0, 0], do_aug[:, sl], 1, 0)
-        ds = (p * dp).astype(BF16)
-        v_part = dg(do_aug[:HEAD, sl], p.astype(BF16), 1, 1)
-        k_part = dg(q_aug[:HEAD, sl], ds, 1, 1)
+        ds = (p.astype(F32) * dp).astype(BF16)
+        v_part = dg(do_aug[:HEAD, sl], p, 1, 1)
+        k_part = dg(q[0, :, sl], ds, 1, 1)
         v_sum = v_part if v_sum is None else v_sum + v_part
         k_sum = k_part if k_sum is None else k_sum + k_part
-        if start + size == LP:
-            dq[0, :, start:] = (dg(kt[0], ds, 1, 0)[:, : L - start] * (1.0 / math.sqrt(HEAD))).astype(BF16)
-        else:
-            dq[0, :, sl] = (dg(kt[0], ds, 1, 0) * (1.0 / math.sqrt(HEAD))).astype(BF16)
-    dk[0] = (k_sum * (1.0 / LOG2E)).astype(BF16)
-    dv[0] = v_sum.astype(BF16)
-
-
-def attend_back(k_rows, v_rows, q, lse, do, dsum, kv):
+        dq[0, :, sl] = (dg(kt[0, :, :KP], ds, 1, 0) * (1.0 / math.sqrt(HEAD))).astype(BF16)
+    for dst, total in ((dk, k_sum * (1.0 / LOG2E)), (dv, v_sum)):
+        dst[0, :, :L] = total[:, :L].astype(BF16)
+        dst[0, :, L:] = jnp.zeros((HEAD, LP - L), BF16)
+
+
+def attend_back(e, v_rows, q, do, dsum, kv):
     d = q.shape[1]
     head = lambda i: (i // H, i % H, 0)
     wide = lambda i: (i // H, i % H, 0, 0)
@@ -410,27 +451,26 @@
         attend_back_kernel,
         grid=(2 * H,),
         in_specs=[
-            pl.BlockSpec((1, 1, L, LANES), wide),
-            pl.BlockSpec((1, 1, L, LANES), wide),
+            pl.BlockSpec((1, 1, KP, LP), wide),
+            pl.BlockSpec((1, 1, KP, LANES), wide),
+            pl.BlockSpec((1, HEAD, LP), head),
             pl.BlockSpec((1, HEAD, LP), head),
             pl.BlockSpec((1, 1, 16, LP), wide),
             pl.BlockSpec((1, HEAD, LP), head),
-            pl.BlockSpec((1, 1, 16, LP), wide),
-            pl.BlockSpec((1, HEAD, L), head),
-        ],
-        out_specs=[pl.BlockSpec((1, HEAD, L), head)] * 3,
-        out_shape=[jax.ShapeDtypeStruct((2, d, L), BF16)] * 3,
-        scratch_shapes=[pltpu.VMEM((LANES, LP), BF16)] * 2,
+        ],
+        out_specs=[pl.BlockSpec((1, HEAD, LP), head)] * 3,
+        out_shape=[jax.ShapeDtypeStruct((2, d, LP), BF16)] * 3,
+        scratch_shapes=[pltpu.VMEM((LANES, LP), BF16)],
         compiler_params=params(),
         cost_estimate=cost(8e10, 4e7),
-    )(k_rows, v_rows, q, lse, do, dsum, kv)
+    )(e, v_rows, q, do, dsum, kv)
 
 
 def mlp_parts(d, f, m):
     return [("wm", d // m)] + [(j, d // m) for j in range(f // ROWS)] + [("wr", f // m)]
 
 
-def mid_kernel(n, m, share, o, stream, up, wpack, be, cols,
+def mid_kernel(n, m, share, o, inv, stream, up, wpack, be, cols,
                dec, ga_out, do_out, dsum_out, gpack, vec_out,
                wm, we, wr, dwm, dwe, dwr, dvec, dbe, drb, stats, n2, act_s, gl_s, g_s):
     copy = pl.program_id(0)
@@ -463,7 +503,7 @@
 
     @pl.when(ff == 0)
     def _():
-        ctx = o[0, :, :L].astype(BF16)
+        ctx = o[0].astype(BF16)
         x = stream[0] + dg(wm[...], ctx, 0, 0) + cols[:, BIAS_M : BIAS_M + 1]
         ga_out[0] = x
         mean = jnp.mean(x, 0, keepdims=True)
@@ -472,10 +512,11 @@
         stats[0:1] = mean
         stats[1:2] = recip
         n2[:d] = (center * recip * cols[:, GAIN2 : GAIN2 + 1] + cols[:, SHIFT2 : SHIFT2 + 1]).astype(BF16)
-        row = lax.broadcasted_iota(jnp.int32, (16, L), 0)
+        row = lax.broadcasted_iota(jnp.int32, (16, LP), 0)
         n2[d:] = (row == 0).astype(F32).astype(BF16)
         g = (up[0].astype(F32) * 0.5).astype(BF16)
-        g_s[...] = g
+        g_s[:L] = g
+        g_s[L:] = jnp.zeros((LP - L, d), BF16)
         drb[...] += dg(jnp.ones((8, L), BF16), g, 1, 0)
 
     rows = pl.ds(pl.multiple_of(ff * FFC, FFC), FFC)
@@ -488,16 +529,16 @@
     gl = (dg(wr[rows, :], g, 1, 1) * slope).astype(BF16)
     act_s[rows, :] = act
     gl_s[rows, :] = gl
-    dwr[rows, :] += dg(act, g, 1, 0)
-    grad = dg(n2[...], gl, 1, 1)
-    dwe[:, rows] += grad[:d]
-    dbe[:, rows] += grad[d : d + 8]
 
     @pl.when(ff == last)
     def _():
         x = ga_out[0]
+        dwr[...] += dg(act_s[...], g_s[...], 1, 0)
+        grad = dg(n2[...], gl_s[...], 1, 1)
+        dwe[...] += grad[:d]
+        dbe[...] += grad[d : d + 8]
         out = x + dg(wr[...], act_s[...], 0, 0) + cols[:, BIAS_R : BIAS_R + 1]
-        dec[0] = out.astype(BF16).T
+        dec[0] = out.astype(BF16).T[:L]
         scaled = (x - stats[0:1]) * stats[1:2]
         e = dg(we[...], gl_s[...], 1, 0)
         dvec[:, 0:1] += jnp.sum(e * scaled, 1, keepdims=True)
@@ -507,17 +548,14 @@
         ga_out[0] = ga
         gm = ga.astype(BF16)
         dvec[:, 2:3] += jnp.sum(gm.astype(F32), 1, keepdims=True)
-        ctx = o[0, :, :L]
+        ctx = o[0]
         dwm[...] += dg(ctx.astype(BF16), gm, 1, 1)
-        do = dg(wm[...], gm, 1, 0).astype(BF16)
-        do_out[0, :, :L] = do
-        do_out[0, :, L:] = jnp.zeros((d, LP - L), BF16)
-        prod = do.astype(F32) * ctx
+        do = dg(wm[...], gm, 1, 0)
         for h in range(H):
-            dsum_out[0, h, :, :L] = aug_rows(
-                -jnp.sum(prod[h * HEAD : (h + 1) * HEAD], 0, keepdims=True)
-            )
-            dsum_out[0, h, :, L:] = jnp.zeros((16, LP - L), BF16)
+            hs = slice(h * HEAD, (h + 1) * HEAD)
+            part = (do[hs] * inv[0, h]).astype(BF16)
+            do_out[0, hs] = part
+            dsum_out[0, h] = aug_rows(-jnp.sum(part.astype(F32) * ctx[hs], 0, keepdims=True))
 
     @pl.when((ff == last) & (copy == 1))
     def _():
@@ -543,7 +581,7 @@
             vec_out[BIAS_E + j : BIAS_E + j + 1] = dbe[0:1, j * ROWS : (j + 1) * ROWS]
 
 
-def mid(n, m, share, o, stream, up, wpack, be, cols):
+def mid(n, m, share, o, inv, stream, up, wpack, be, cols):
     d = cols.shape[0]
     f = be.shape[0]
     once = pl.Buffered(1)
@@ -554,23 +592,23 @@
     return pl.pallas_call(
         functools.partial(mid_kernel, n, m, share),
         grid=(2, f // FFC),
-        in_specs=[lead(d, LP), lead(d, L), lead(L, d), const(*wpack.shape), const(f, 1), const(d, 16)],
+        in_specs=[lead(d, LP), lead(H, 1, LP), lead(d, LP), lead(L, d), const(*wpack.shape), const(f, 1), const(d, 16)],
         out_specs=[
-            lead(L, d), lead(d, L), lead(d, LP), lead(H, 16, LP), const(n, m, share, ROWS), const(16, d),
+            lead(L, d), lead(d, LP), lead(d, LP), lead(H, 16, LP), const(n, m, share, ROWS), const(16, d),
         ],
         out_shape=[
-            shape((2, L, d), BF16), shape((2, d, L), F32), shape((2, d, LP), BF16), shape((2, H, 16, LP), BF16),
+            shape((2, L, d), BF16), shape((2, d, LP), F32), shape((2, d, LP), BF16), shape((2, H, 16, LP), BF16),
             shape((n, m, share, ROWS), BF16), shape((16, d), F32),
         ],
         scratch_shapes=[
             vm((d, d), BF16), vm((d, f), BF16), vm((f, d), BF16),
             vm((d, d), F32), vm((d, f), F32), vm((f, d), F32), vm((d, LANES), F32), vm((8, f), F32), vm((8, d), F32),
-            vm((8, L), F32), vm((d + 16, L), BF16),
-            vm((f, L), BF16), vm((f, L), BF16), vm((L, d), BF16),
+            vm((8, LP), F32), vm((d + 16, LP), BF16),
+            vm((f, LP), BF16), vm((f, LP), BF16), vm((LP, d), BF16),
         ],
         compiler_params=params(),
         cost_estimate=cost(5e10, 4e7),
-    )(o, stream, up, wpack, be, cols)
+    )(o, inv, stream, up, wpack, be, cols)
 
 
 def post_kernel(n, m, share, held, seen_len, dq, dk, dv, stream, ga, seen, vis, win, cols, vec_in,
@@ -592,7 +630,7 @@
     x = stream[0]
     scaled, recip = norm_stats(x)
     n1[:d] = (scaled * cols[:, GAIN1 : GAIN1 + 1] + cols[:, SHIFT1 : SHIFT1 + 1]).astype(BF16)
-    row = lax.broadcasted_iota(jnp.int32, (16, L), 0)
+    row = lax.broadcasted_iota(jnp.int32, (16, LP), 0)
     n1[d:] = (row == 0).astype(F32).astype(BF16)
     e = None
     for part, ref in enumerate((dq, dk, dv)):
@@ -605,9 +643,10 @@
     dvec[:, 0:1] += jnp.sum(e * scaled, 1, keepdims=True)
     dvec[:, 1:2] += jnp.sum(e, 1, keepdims=True)
     gs = ga[0] + norm_back(e, scaled, recip, cols[:, GAIN1 : GAIN1 + 1])
-    hot = one_hot(vis[0], L)
-    covered = jnp.sum(hot, 0, keepdims=True)
-    dvec[:, 2:3] += jnp.sum(gs * (1.0 - covered), 1, keepdims=True)
+    hot = one_hot(vis[0], LP)
+    token = lax.broadcasted_iota(jnp.int32, (1, LP), 1)
+    masked = jnp.where(token < L, 1.0 - jnp.sum(hot, 0, keepdims=True), 0.0)
+    dvec[:, 2:3] += jnp.sum(gs * masked, 1, keepdims=True)
     gp = dg(hot.astype(BF16), gs.astype(BF16), 1, 1).astype(BF16)
     gp_s[pl.ds(pl.multiple_of(copy * seen_pad, SEG), seen_pad), :] = gp
     dwp[...] += dg(seen[0], gp, 0, 0)
@@ -656,14 +695,14 @@
         functools.partial(post_kernel, n, m, share, held, seen_len),
         grid=(2,),
         in_specs=[
-            lead(d, L), lead(d, L), lead(d, L), lead(d, L), lead(d, L), lead(a, e), lead(a, 1),
+            lead(d, LP), lead(d, LP), lead(d, LP), lead(d, LP), lead(d, LP), lead(a, e), lead(a, 1),
             const(d, 3 * d), const(d, 16), const(16, d),
         ],
         out_specs=[const(n, m, share, ROWS), const(n, cap, d)],
         out_shape=[shape((n, m, share, ROWS), BF16), shape((n, cap, d), BF16)],
         scratch_shapes=[
             vm((d, 3 * d), F32), vm((8, 3 * d), F32), vm((d, LANES), F32), vm((e, d), F32),
-            vm((d + 16, L), BF16), vm((2 * a, d), BF16),
+            vm((d + 16, LP), BF16), vm((2 * a, d), BF16),
         ],
         compiler_params=params(),
         cost_estimate=cost(2e10, 2e7),
@@ -681,71 +720,66 @@
     mlp_s[clip] = mlp[...]
     greet(n, m, clip, wt)
     sends = []
-    order = [*range(1, half), 0]
-    for j in order:
-        spot = lax.rem(chip + j, half)
-        copy = remote(gpack.at[2 * spot + 1 - core], a1.at[j], s1.at[j], r1.at[j], partner, wt)
+
+    def send(*args):
+        copy = remote(*args)
         copy.start()
         sends.append(copy)
+
+    order = [*range(1, half), 0]
+    turns = [*range(1, m), 0]
+    for k in turns:
+        zz = lax.rem(wt + k, m)
+        for j in order:
+            spot = lax.rem(chip + j, half)
+            send(gpack.at[2 * spot + 1 - core, zz], a1.at[j, k], s1.at[j, k], r1.at[j, k], partner, wt)
+    for k in turns:
+        zz = lax.rem(wt + k, m)
+        for j in order:
+            mine = 2 * lax.rem(chip + j, half) + core
+            remote(gpack.at[mine, zz], a1.at[j, k], s1.at[j, k], r1.at[j, k], partner, wt).wait_recv()
+            both = gpack[mine, zz].astype(F32) + a1[j, k].astype(F32)
+            if j == 0:
+                tot[k] = both
+            else:
+                a2s[j, k] = both.astype(BF16)
+                send(a2s.at[j, k], a2r.at[j, k], s2.at[j, k], r2.at[j, k], mine, wt)
     for k in [*range(2, n, 2), *range(1, n, 2)]:
         dest = lax.rem(clip + k, n)
-        copy = remote(gp.at[dest], ret_s.at[clip], gs.at[k], gr.at[k], dest, wt)
-        copy.start()
-        sends.append(copy)
+        send(gp.at[dest], ret_s.at[clip], gs.at[k], gr.at[k], dest, wt)
     ret_s[clip] = gp[clip]
-    for j in range(1, half):
-        copy = remote(mlp_s.at[clip], mlp_s.at[clip], sm.at[j], rm.at[j], lax.rem(clip + 2 * j, n), wt)
-        copy.start()
-        sends.append(copy)
-    copy = remote(mlp_s.at[clip], mlp_s.at[clip], sf.at[0], rf.at[0], partner, wt)
-    copy.start()
-    sends.append(copy)
     for j in order:
-        spot = lax.rem(chip + j, half)
-        mine = 2 * spot + core
-        remote(gpack.at[mine], a1.at[j], s1.at[j], r1.at[j], partner, wt).wait_recv()
-        both = gpack[mine].astype(F32) + a1[j].astype(F32)
-        if j == 0:
-            tot[...] = both
-        else:
-            a2s[j] = both.astype(BF16)
-            copy = remote(a2s.at[j], a2r.at[j], s2.at[j], r2.at[j], mine, wt)
-            copy.start()
-            sends.append(copy)
-    for j in range(1, half):
-        source = lax.rem(clip - 2 * j + n, n)
-        remote(a2s.at[j], a2r.at[j], s2.at[j], r2.at[j], source, wt).wait_recv()
-        tot[...] += a2r[j].astype(F32)
-    tot_b[...] = tot[...].astype(BF16)
+        dest = lax.rem(clip + 2 * j, n) if j else partner
+        send(mlp_s.at[clip], mlp_s.at[clip], sm.at[j], rm.at[j], dest, wt)
+    for k in turns:
+        zz = lax.rem(wt + k, m)
+        total = tot[k]
+        for j in range(1, half):
+            source = lax.rem(clip - 2 * j + n, n)
+            remote(a2s.at[j, k], a2r.at[j, k], s2.at[j, k], r2.at[j, k], source, wt).wait_recv()
+            total = total + a2r[j, k].astype(F32)
+        if k:
+            tot_b[k] = total.astype(BF16)
+            send(tot_b.at[k], brecv.at[k], sb.at[k], rb.at[k], clip, zz)
     for k in range(1, m):
-        zz = lax.rem(wt + k, m)
-        copy = remote(tot_b.at[zz], brecv.at[k], sb.at[k], rb.at[k], clip, zz)
-        copy.start()
-        sends.append(copy)
+        source = lax.rem(wt - k + m, m)
+        remote(tot_b.at[k], brecv.at[k], sb.at[k], rb.at[k], clip, source).wait_recv()
+        total = total + brecv[k].astype(F32)
+    fin_s[clip] = total.astype(BF16)
+    for k in [*range(2, n, 2), *range(1, n, 2)]:
+        send(fin_s.at[clip], fin_s.at[clip], sc.at[k], rc.at[k], lax.rem(clip + k, n), wt)
     for j in range(1, half):
         source = lax.rem(clip - 2 * j + n, n)
         remote(mlp_s.at[source], mlp_s.at[source], sm.at[j], rm.at[j], source, wt).wait_recv()
-        copy = remote(mlp_s.at[source], mlp_s.at[source], sf.at[j], rf.at[j], partner, wt)
-        copy.start()
-        sends.append(copy)
-    total = tot[wt]
-    for k in range(1, m):
-        source = lax.rem(wt - k + m, m)
-        remote(tot_b.at[source], brecv.at[k], sb.at[k], rb.at[k], clip, source).wait_recv()
-        total = total + brecv[k].astype(F32)
-    fin_s[clip] = total.astype(BF16)
-    for k in [*range(2, n, 2), *range(1, n, 2)]:
-        dest = lax.rem(clip + k, n)
-        copy = remote(fin_s.at[clip], fin_s.at[clip], sc.at[k], rc.at[k], dest, wt)
-        copy.start()
-        sends.append(copy)
+        send(mlp_s.at[source], mlp_s.at[source], sf.at[j], rf.at[j], partner, wt)
     for k in range(1, n):
         source = lax.rem(clip - k + n, n)
         remote(gp.at[source], ret_s.at[source], gs.at[k], gr.at[k], source, wt).wait_recv()
     ret[...] = ret_s[...]
     for j in range(half):
         source = lax.rem(partner - 2 * j + n, n)
-        remote(mlp_s.at[source], mlp_s.at[source], sf.at[j], rf.at[j], partner, wt).wait_recv()
+        sems = (sf.at[j], rf.at[j]) if j else (sm.at[0], rm.at[0])
+        remote(mlp_s.at[source], mlp_s.at[source], *sems, partner, wt).wait_recv()
     mlp_out[...] = mlp_s[...]
     for k in range(1, n):
         source = lax.rem(clip - k + n, n)
@@ -772,7 +806,7 @@
             vm((half, m, share, ROWS), BF16), vm((half, m, share, ROWS), BF16), vm((half, m, share, ROWS), BF16),
             vm((m, share, ROWS), F32), vm((m, share, ROWS), BF16), vm((m, share, ROWS), BF16),
             vm((n, share, ROWS), BF16), vm((n, cap, d), BF16), vm((n,) + mlp.shape, BF16),
-            dma((n,)), dma((n,)), dma((half,)), dma((half,)), dma((half,)), dma((half,)),
+            dma((n,)), dma((n,)), dma((half, m)), dma((half, m)), dma((half, m)), dma((half, m)),
             dma((m,)), dma((m,)), dma((n,)), dma((n,)),
             dma((half,)), dma((half,)), dma((half,)), dma((half,)),
         ],
@@ -807,11 +841,11 @@
                 @pl.when(wt == z)
                 def _():
                     for i, ref in enumerate(vecs[:BIAS_E]):
-                        w = ref.shape[1]
-                        ref[...] = piece[i : i + 1, z * w : (z + 1) * w]
-                    w = vecs[BIAS_E].shape[1]
+                        w = ref.shape[0]
+                        ref[...] = piece[i, z * w : (z + 1) * w]
+                    w = vecs[BIAS_E].shape[0]
                     line = BIAS_E + z * w // ROWS
-                    vecs[BIAS_E][...] = piece[line : line + 1, z * w % ROWS : z * w % ROWS + w]
+                    vecs[BIAS_E][...] = piece[line, z * w % ROWS : z * w % ROWS + w]
     for name, r, slot, at in mlp_plan:
         piece = mlp[slot, at : at + SEG].astype(F32)
         if name == "wm":
@@ -830,7 +864,7 @@
     mlp_plan = segments(mlp_parts(d, f, m), mlp.shape[1])
     outs = [shape((held, e), BF16)] + [
         shape((r // m, c), F32) for r, c in ((e, d), (d, 3 * d), (d, d), (d, f), (f, d))
-    ] + [shape((1, d // m), F32)] * BIAS_E + [shape((1, f // m), F32)]
+    ] + [shape((d // m,), F32)] * BIAS_E + [shape((f // m,), F32)]
     return pl.pallas_call(
         functools.partial(finish_kernel, n, m, plan, mlp_plan),
         in_specs=[whole] * 4,
@@ -841,6 +875,21 @@
     )(fin, ret, mlp, wp)
 
 
+def core(n, m, held, seen_len, seen, vis, wp, win, cols, be, wpack, upstream, reduce_mlp=None):
+    d = cols.shape[0]
+    pos = jnp.asarray(position_table(d))
+    stream, q, kv, k_rows, v_rows = pre(seen, vis, wp, cols, pos, win)
+    o, inv, e = attend(k_rows, q, kv)
+    share = up16(-(-wpack.shape[1] // n))
+    dec, ga, do, dsum, mlp, vec = mid(n, m, share, o, inv, stream, upstream.reshape(2, L, d), wpack, be, cols)
+    if reduce_mlp is not None:
+        mlp = reduce_mlp(mlp)
+    dq, dk, dv = attend_back(e, v_rows, q, do, dsum, kv)
+    share = up16(-(-(wp.shape[0] // m + 3 * (d // m) + SEG) // n))
+    gpack, gp = post(n, m, share, held, seen_len, dq, dk, dv, stream, ga, seen, vis, win, cols, vec)
+    return dec, mlp, gpack, gp
+
+
 def per_device(encoded, visible_at, wp, token, gain1, shift1, win, bq, bv, wm, bm, gain2, shift2, we, be, wr, br, upstream):
     n = lax.axis_size("clip")
     m = lax.axis_size("wt")
@@ -848,25 +897,21 @@
     seen_len = visible_at.shape[1]
     d = wp.shape[1]
     f = be.shape[0] * m
-    pieces = [wm] + [we[:, j * ROWS : (j + 1) * ROWS] for j in range(f // ROWS)] + [wr]
-    local = jnp.concatenate(pieces, 0)
+    local = pack_mlp(wm, we, wr)
     wpack = lax.all_gather(local, "wt", axis=0, tiled=True).reshape(m, local.shape[0], ROWS)
     vecs = (token, gain1, shift1, bq, bv, bm, gain2, shift2, br, be)
     seen, vis, wp_full, win_full, cols, be_col = enter(n, m, encoded, visible_at, wp, win, vecs)
-    pos = jnp.asarray(position_table(d))
-    stream, q, kv, k_rows, v_rows = pre(seen, vis, wp_full, cols, pos, win_full)
-    o, lse = attend(k_rows, q, kv)
-    share = up16(-(-local.shape[0] // n))
-    dec, ga, do, dsum, mlp, vec2 = mid(n, m, share, o, stream, upstream.reshape(2, L, d), wpack, be_col, cols)
-    mlp = mlp.reshape(n * m * share, ROWS)
-    mlp = lax.psum_scatter(mlp, "clip", scatter_dimension=0, tiled=True)
-    mlp = lax.psum_scatter(mlp, "wt", scatter_dimension=0, tiled=True)
-    dq, dk, dv = attend_back(k_rows, v_rows, q, lse, do, dsum, kv)
-    share = up16(-(-(wp.shape[0] + 3 * win.shape[0] + SEG) // n))
-    gpack, gp = post(n, m, share, held, seen_len, dq, dk, dv, stream, ga, seen, vis, win_full, cols, vec2)
+
+    def reduce_mlp(mlp):
+        mlp = lax.psum_scatter(mlp.reshape(-1, ROWS), "clip", scatter_dimension=0, tiled=True)
+        return lax.psum_scatter(mlp, "wt", scatter_dimension=0, tiled=True)
+
+    dec, mlp, gpack, gp = core(
+        n, m, held, seen_len, seen, vis, wp_full, win_full, cols, be_col, wpack, upstream, reduce_mlp
+    )
     fin, ret, mlp = leave(n, m, gpack, gp, mlp)
     egrad, dwp, dwin, dwm, dwe, dwr, *small = finish(n, m, held, fin, ret, mlp, wp_full, f)
-    t, g1, s1, vq, vv, vm, g2, s2, vr, ve = [v.reshape(-1) for v in small]
+    t, g1, s1, vq, vv, vm, g2, s2, vr, ve = small
     return (
         dec.reshape(2 * L, d), egrad, dwp, t, g1, s1, dwin, vq, vv, dwm, vm, g2, s2, dwe, ve, dwr, vr,
     )

time: 306 us -> 286 us (0.935)
  Pallas kernels: 279 us -> 269 us
  local copies, waits for them, and re-layouts: 7.59 us -> 0 us
    pallas_call x1, Pallas kernels: 93.1 us -> 66.6 us  [attend_back(): pl.pallas_call(attend_back_kernel, grid=(2 * H,), in_specs=[pl.BlockSpec(...]
    pallas_call x0 -> x1, Pallas kernels: none -> 21.3 us  [pack_mlp(): pl.pallas_call(pack_kernel, in_specs=[pl.BlockSpec(memory_space=pl.ANY)]...]
    unnamed x7 -> x0, local copies, waits for them, and re-layouts: 5.33 us -> none
    pallas_call x1, Pallas kernels: 32.1 us -> 28.9 us  [leave(): pl.pallas_call(functools.partial(leave_kernel, n, m), in_specs=[whole] *...]
  transfers between devices with their start and end apart: 3 -> 3, of which waited for: 0 -> 0; matrix products, arithmetic and copies ran while one was open for 0% -> 0% of each run, Pallas kernels for 63% -> 58%
where the time goes in v3:
time: 286 us; the launch traced here: 283 us
  Pallas kernels  269 us (94%)
  between operations  14 us (5%)
    pallas_call x1, Pallas kernels, attend_back(): pl.pallas_call(attend_back_kernel, grid=(2 * H,), in_specs=[pl.BlockSpec(...  66.6 us
    pallas_call x1, Pallas kernels, mid(): pl.pallas_call(functools.partial(mid_kernel, n, m, share), grid=(2, f //...  50.4 us
    pallas_call x1, Pallas kernels, attend(): pl.pallas_call(attend_kernel, grid=(2 * H,), in_specs=[pl.BlockSpec((1, 1...  35.7 us
    pallas_call x1, Pallas kernels, leave(): pl.pallas_call(functools.partial(leave_kernel, n, m), in_specs=[whole] *...  28.9 us
    pallas_call x1, Pallas kernels, enter(): pl.pallas_call(functools.partial(enter_kernel, n, m, share, cap, seen_pad...  27.7 us
    pallas_call x1, Pallas kernels, pack_mlp(): pl.pallas_call(pack_kernel, in_specs=[pl.BlockSpec(memory_space=pl.ANY)]...  21.3 us
    pallas_call x1, Pallas kernels, post(): pl.pallas_call(functools.partial(post_kernel, n, m, share, held, seen_len...  20.7 us
    pallas_call x1, Pallas kernels, pre(): pl.pallas_call(pre_kernel, grid=(2,), in_specs=[lead(a, e), lead(a, 1), c...  13.8 us
  transfers between devices with their start and end apart: 3, of which 0 were waited for; matrix products, arithmetic and copies ran while one was open for 0% of the time, Pallas kernels for 58%

profile of v3, /device:TPU:0, one launch (start us, length us, event | category | flops | bytes accessed | tf_op | source)
XLA Modules:
  0.0 283.4 jit_solution(13178734183947209855)
XLA Ops:
  7.2 0.0 all-gather.2.cloned.1.call-start
  7.2 21.3 %shard_map.317 = bf16[864,384]{1,0:T(8,128)(2,1)} custom-call(bf16[96,384]{1,0:T(8,128)(2,1)} %wm.1, bf16[96,1536]{1,0:T(8,128)(2,1)} %we.1, bf16[384,384]{1,0:T(8,128)(2,1)} %wr.1), custom_call_target="tpu_custom_call" | custom-call | bytes 1300000 | tf_op jit(solution)/shard_map/pallas_call | solution.py:275
  28.5 0.0 all-gather.2.cloned.1.call-update
  28.5 0.0 reduce-scatter.3.cloned.1.call-start
  28.6 27.7 %shard_map.314 = (bf16[2,160,768]{2,1,0:T(8,128)(2,1)}, f32[2,160,1]{2,1,0:T(8,128)}, bf16[768,384]{1,0:T(8,128)(2,1)}, bf16[384,1152]{1,0:T(8,128)(2,1)}, f32[384,16]{1,0:T(8,128)}, /*index=5*/f32[1536,1]{1,0:T(8,128)}) custom-call(bf16[314,768]{1,0:T(8,128)(2,1)} %refs_0_.1, s32[2,157]{1,0:T(2,128)} %refs_1_.1, bf16[192,384]{1,0:T(8,128)(2,1)} %refs_2_.1, ...), custom_call_target="tpu_custom_call" | custom-call | flops 6000000000 | bytes 4000000 | tf_op jit(solution)/shard_map/pallas_call | solution.py:296
  56.3 13.8 %shard_map.315 = (f32[2,384,1664]{2,1,0:T(8,128)}, bf16[2,384,1664]{2,1,0:T(8,128)(2,1)}, bf16[2,768,1664]{2,1,0:T(8,128)(2,1)}, bf16[2,6,1568,128]{3,2,1,0:T(8,128)(2,1)}, bf16[2,6,1568,128]{3,2,1,0:T(8,128)(2,1)}) custom-call(bf16[2,160,768]{2,1,0:T(8,128)(2,1)} %get-tuple-element.61.seen, f32[2,160,1]{2,1,0:T(8,128)} %get-tuple-element.62.vis, ...), custom_call_target="tpu_custom_call" | custom-call | flops 12000000000 | bytes 20000000 | tf_op jit(solution)/shard_map/pallas_call | solution.py:350
  70.1 35.7 %shard_map.316 = (f32[2,384,1664]{2,1,0:T(8,128)}, f32[2,6,1,1664]{3,2,1,0:T(1,128)}, bf16[2,6,1568,1664]{3,2,1,0:T(8,128)(2,1)}) custom-call(bf16[2,6,1568,128]{3,2,1,0:T(8,128)(2,1)} %get-tuple-element.66.k_rows, bf16[2,384,1664]{2,1,0:T(8,128)(2,1)} %get-tuple-element.67.q, bf16[2,768,1664]{2,1,0:T(8,128)(2,1)} %get-tuple-element.68.kt.vt, ...), custom_call_target="tpu_custom_call" | custom-call | flops 30000001024 | bytes 20000000 | tf_op jit(solution)/shard_map/pallas_call | solution.py:400
  105.8 0.0 all-gather.2.cloned.1.call-done
  105.8 50.4 %shard_map.318 = (bf16[2,1568,384]{2,1,0:T(8,128)(2,1)}, f32[2,384,1664]{2,1,0:T(8,128)}, bf16[2,384,1664]{2,1,0:T(8,128)(2,1)}, bf16[2,6,16,1664]{3,2,1,0:T(8,1...) custom-call(f32[2,384,1664]{2,1,0:T(8,128)} %get-tuple-element.69.o, ...), custom_call_target="tpu_custom_call" | custom-call | flops 49999998976 | bytes 40000000 | tf_op jit(solution)/shard_map/pallas_call | solution.py:592
  156.2 0.0 reduce-scatter.3.cloned.1.call-update
  156.2 0.0 reduce-scatter.5.cloned.1.call-start
  156.3 66.6 %shard_map.319 = (bf16[2,384,1664]{2,1,0:T(8,128)(2,1)}, bf16[2,384,1664]{2,1,0:T(8,128)(2,1)}, bf16[2,384,1664]{2,1,0:T(8,128)(2,1)}) custom-call(bf16[2,6,1568,1664]{3,2,1,0:T(8,128)(2,1)} %get-tuple-element.74.e, bf16[2,6,1568,128]{3,2,1,0:T(8,128)(2,1)} %get-tuple-element.75.v_rows, bf16[2,384,1664]{2,1,0:T(8,128)(2,1)} %get-tuple-element.67.q, ...), custom_call_target="tpu_custom_call" | custom-call | flops 80000000000 | bytes 40000000 | tf_op jit(solution)/shard_map/pallas_call | solution.py:450
  222.9 0.0 reduce-scatter.3.cloned.1.call-done
  222.9 0.0 reduce-scatter.5.cloned.1.call-update
  222.9 20.7 %shard_map.320 = (bf16[8,4,64,384]{3,2,1,0:T(8,128)(2,1)}, bf16[8,48,384]{2,1,0:T(8,128)(2,1)}) custom-call(bf16[2,384,1664]{2,1,0:T(8,128)(2,1)} %get-tuple-element.78.dq, bf16[2,384,1664]{2,1,0:T(8,128)(2,1)} %get-tuple-element.79.dk, bf16[2,384,1664]{2,1,0:T(8,128)(2,1)} %get-tuple-element.80.dv, f32[2,384,1664]{2,1,0:T(8,128)} %get-tuple-element.71.stream, ...), custom_call_target="tpu_custom_call" | custom-call | flops 20000000000 | bytes 20000000 | tf_op jit(solution)/shard_map/pallas_call | solution.py:694
  243.6 0.0 reduce-scatter.5.cloned.1.call-done.mlp
  243.6 28.9 %shard_map.321 = (bf16[8,64,384]{2,1,0:T(8,128)(2,1)}, bf16[8,48,384]{2,1,0:T(8,128)(2,1)}, bf16[8,112,384]{2,1,0:T(8,128)(2,1)}) custom-call(bf16[8,4,64,384]{3,2,1,0:T(8,128)(2,1)} %get-tuple-element.83.gpack, bf16[8,48,384]{2,1,0:T(8,128)(2,1)} %get-tuple-element.84.gp, bf16[112,384]{1,0:T(8,128)(2,1)} %reduce-scatter.5.cloned.1.call-done.mlp), custom_call_target="tpu_custom_call" | custom-call | flops 4000000000 | bytes 4000000 | tf_op jit(solution)/shard_map/pallas_call | solution.py:800
  272.5 4.2 %shard_map.322 = (bf16[314,768]{1,0:T(8,128)(2,1)}, f32[192,384]{1,0:T(8,128)}, f32[96,1152]{1,0:T(8,128)}, f32[96,384]{1,0:T(8,128)}, f32[96,1536]{1,0:T(8,128)...) custom-call(bf16[8,64,384]{2,1,0:T(8,128)(2,1)} %get-tuple-element.8, ...), custom_call_target="tpu_custom_call" | custom-call | flops 1000000000 | bytes 4000000 | tf_op jit(solution)/shard_map/pallas_call | solution.py:868
Async XLA Ops:
  7.2 98.6 %all-gather.2.cloned.1.call-start = ((), (), s32[]{:S(2)}) async-start(), calls=%async_computation.2 | async-start | bytes 3317760 | tf_op jit(solution)/shard_map/all_gather | solution.py:901
  28.5 194.4 %reduce-scatter.3.cloned.1.call-start = ((), (), s32[]{:S(2)}) async-start(), calls=%async_computation.3 | async-start | bytes 3096576 | tf_op jit(solution)/shard_map/reduce_scatter | solution.py:906
  156.2 87.4 %reduce-scatter.5.cloned.1.call-start = ((), (), s32[]{:S(2)}) async-start(), calls=%async_computation.4 | async-start | bytes 430080 | tf_op jit(solution)/shard_map/reduce_scatter | solution.py:907
Sparse Core Ops, SparseCore 0:
  28.6 58.0 all-gather.1
  156.3 43.5 reduce-scatter.2
  223.1 19.5 reduce-scatter.4

commit v4 on v3

--- a/solution.py
+++ b/solution.py
@@ -256,28 +256,25 @@
         copy.wait_send()
 
 
-def pack_kernel(wm, we, wr, out, sems):
+def pack_kernel(wm, we, wr, out):
     rows = wm.shape[0]
-    moves = [(wm, 0, rows)]
-    moves += [(we.at[:, j * ROWS : (j + 1) * ROWS], rows * (j + 1), rows) for j in range(we.shape[1] // ROWS)]
-    moves += [(wr, rows * len(moves), wr.shape[0])]
-    copies = []
-    for i, (src, at, size) in enumerate(moves):
-        copy = pltpu.make_async_copy(src, out.at[at : at + size], sems.at[i])
-        copy.start()
-        copies.append(copy)
-    for copy in copies:
-        copy.wait()
+    out[:rows] = wm[...]
+    at = rows
+    for j in range(we.shape[1] // ROWS):
+        out[at : at + rows] = we[:, j * ROWS : (j + 1) * ROWS]
+        at += rows
+    out[at:] = wr[...]
 
 
 def pack_mlp(wm, we, wr):
     rows = wm.shape[0] + wm.shape[0] * (we.shape[1] // ROWS) + wr.shape[0]
+    whole = pl.BlockSpec(memory_space=pltpu.VMEM)
     return pl.pallas_call(
         pack_kernel,
-        in_specs=[pl.BlockSpec(memory_space=pl.ANY)] * 3,
-        out_specs=pl.BlockSpec(memory_space=pl.ANY),
+        in_specs=[whole] * 3,
+        out_specs=whole,
         out_shape=jax.ShapeDtypeStruct((rows, ROWS), BF16),
-        scratch_shapes=[pltpu.SemaphoreType.DMA((2 + we.shape[1] // ROWS,))],
+        compiler_params=params(),
         cost_estimate=cost(0, 1.3e6),
     )(wm, we, wr)
 

time: 286 us -> 267 us (0.934)
  Pallas kernels: 269 us -> 250 us
    pallas_call x1, Pallas kernels: 21.3 us -> 1.98 us  [pack_mlp(): pl.pallas_call(pack_kernel, in_specs=[whole] * 3, out_specs=whole, out_sh...]
  transfers between devices with their start and end apart: 3 -> 3, of which waited for: 0 -> 0; matrix products, arithmetic and copies ran while one was open for 0% -> 0% of each run, Pallas kernels for 58% -> 62%
where the time goes in v4:
time: 267 us; the launch traced here: 264 us
  Pallas kernels  250 us (94%)
  between operations  14 us (5%)
    pallas_call x1, Pallas kernels, attend_back(): pl.pallas_call(attend_back_kernel, grid=(2 * H,), in_specs=[pl.BlockSpec(...  66.6 us
    pallas_call x1, Pallas kernels, mid(): pl.pallas_call(functools.partial(mid_kernel, n, m, share), grid=(2, f //...  50.4 us
    pallas_call x1, Pallas kernels, attend(): pl.pallas_call(attend_kernel, grid=(2 * H,), in_specs=[pl.BlockSpec((1, 1...  35.8 us
    pallas_call x1, Pallas kernels, leave(): pl.pallas_call(functools.partial(leave_kernel, n, m), in_specs=[whole] *...  28.8 us
    pallas_call x1, Pallas kernels, enter(): pl.pallas_call(functools.partial(enter_kernel, n, m, share, cap, seen_pad...  27.7 us
    pallas_call x1, Pallas kernels, post(): pl.pallas_call(functools.partial(post_kernel, n, m, share, held, seen_len...  20.7 us
    pallas_call x1, Pallas kernels, pre(): pl.pallas_call(pre_kernel, grid=(2,), in_specs=[lead(a, e), lead(a, 1), c...  13.8 us
  transfers between devices with their start and end apart: 3, of which 0 were waited for; matrix products, arithmetic and copies ran while one was open for 0% of the time, Pallas kernels for 62%

profile of v4, /device:TPU:0, one launch (start us, length us, event | category | flops | bytes accessed | tf_op | source)
XLA Modules:
  0.0 264.2 jit_solution(9280613414664794160)
XLA Ops:
  7.2 0.0 all-gather.2.cloned.1.call-start
  7.2 2.0 shard_map.317
  9.2 0.0 all-gather.2.cloned.1.call-update
  9.2 0.0 reduce-scatter.3.cloned.1.call-start
  9.3 27.7 %shard_map.314 = (bf16[2,160,768]{2,1,0:T(8,128)(2,1)}, f32[2,160,1]{2,1,0:T(8,128)}, bf16[768,384]{1,0:T(8,128)(2,1)}, bf16[384,1152]{1,0:T(8,128)(2,1)}, f32[384,16]{1,0:T(8,128)}, /*index=5*/f32[1536,1]{1,0:T(8,128)}) custom-call(bf16[314,768]{1,0:T(8,128)(2,1)} %refs_0_.1, s32[2,157]{1,0:T(2,128)} %refs_1_.1, bf16[192,384]{1,0:T(8,128)(2,1)} %refs_2_.1, ...), custom_call_target="tpu_custom_call" | custom-call | flops 6000000000 | bytes 4000000 | tf_op jit(solution)/shard_map/pallas_call | solution.py:293
  37.0 13.8 %shard_map.315 = (f32[2,384,1664]{2,1,0:T(8,128)}, bf16[2,384,1664]{2,1,0:T(8,128)(2,1)}, bf16[2,768,1664]{2,1,0:T(8,128)(2,1)}, bf16[2,6,1568,128]{3,2,1,0:T(8,128)(2,1)}, bf16[2,6,1568,128]{3,2,1,0:T(8,128)(2,1)}) custom-call(bf16[2,160,768]{2,1,0:T(8,128)(2,1)} %get-tuple-element.61.seen, f32[2,160,1]{2,1,0:T(8,128)} %get-tuple-element.62.vis, ...), custom_call_target="tpu_custom_call" | custom-call | flops 12000000000 | bytes 20000000 | tf_op jit(solution)/shard_map/pallas_call | solution.py:347
  50.9 35.8 %shard_map.316 = (f32[2,384,1664]{2,1,0:T(8,128)}, f32[2,6,1,1664]{3,2,1,0:T(1,128)}, bf16[2,6,1568,1664]{3,2,1,0:T(8,128)(2,1)}) custom-call(bf16[2,6,1568,128]{3,2,1,0:T(8,128)(2,1)} %get-tuple-element.66.k_rows, bf16[2,384,1664]{2,1,0:T(8,128)(2,1)} %get-tuple-element.67.q, bf16[2,768,1664]{2,1,0:T(8,128)(2,1)} %get-tuple-element.68.kt.vt, ...), custom_call_target="tpu_custom_call" | custom-call | flops 30000001024 | bytes 20000000 | tf_op jit(solution)/shard_map/pallas_call | solution.py:397
  86.6 0.0 all-gather.2.cloned.1.call-done
  86.6 50.4 %shard_map.318 = (bf16[2,1568,384]{2,1,0:T(8,128)(2,1)}, f32[2,384,1664]{2,1,0:T(8,128)}, bf16[2,384,1664]{2,1,0:T(8,128)(2,1)}, bf16[2,6,16,1664]{3,2,1,0:T(8,1...) custom-call(f32[2,384,1664]{2,1,0:T(8,128)} %get-tuple-element.69.o, ...), custom_call_target="tpu_custom_call" | custom-call | flops 49999998976 | bytes 40000000 | tf_op jit(solution)/shard_map/pallas_call | solution.py:589
  137.0 0.0 reduce-scatter.3.cloned.1.call-update
  137.1 0.0 reduce-scatter.5.cloned.1.call-start
  137.1 66.6 %shard_map.319 = (bf16[2,384,1664]{2,1,0:T(8,128)(2,1)}, bf16[2,384,1664]{2,1,0:T(8,128)(2,1)}, bf16[2,384,1664]{2,1,0:T(8,128)(2,1)}) custom-call(bf16[2,6,1568,1664]{3,2,1,0:T(8,128)(2,1)} %get-tuple-element.74.e, bf16[2,6,1568,128]{3,2,1,0:T(8,128)(2,1)} %get-tuple-element.75.v_rows, bf16[2,384,1664]{2,1,0:T(8,128)(2,1)} %get-tuple-element.67.q, ...), custom_call_target="tpu_custom_call" | custom-call | flops 80000000000 | bytes 40000000 | tf_op jit(solution)/shard_map/pallas_call | solution.py:447
  203.7 0.0 reduce-scatter.3.cloned.1.call-done
  203.8 0.0 reduce-scatter.5.cloned.1.call-update
  203.8 20.7 %shard_map.320 = (bf16[8,4,64,384]{3,2,1,0:T(8,128)(2,1)}, bf16[8,48,384]{2,1,0:T(8,128)(2,1)}) custom-call(bf16[2,384,1664]{2,1,0:T(8,128)(2,1)} %get-tuple-element.78.dq, bf16[2,384,1664]{2,1,0:T(8,128)(2,1)} %get-tuple-element.79.dk, bf16[2,384,1664]{2,1,0:T(8,128)(2,1)} %get-tuple-element.80.dv, f32[2,384,1664]{2,1,0:T(8,128)} %get-tuple-element.71.stream, ...), custom_call_target="tpu_custom_call" | custom-call | flops 20000000000 | bytes 20000000 | tf_op jit(solution)/shard_map/pallas_call | solution.py:691
  224.5 0.0 reduce-scatter.5.cloned.1.call-done.mlp
  224.5 28.8 %shard_map.321 = (bf16[8,64,384]{2,1,0:T(8,128)(2,1)}, bf16[8,48,384]{2,1,0:T(8,128)(2,1)}, bf16[8,112,384]{2,1,0:T(8,128)(2,1)}) custom-call(bf16[8,4,64,384]{3,2,1,0:T(8,128)(2,1)} %get-tuple-element.83.gpack, bf16[8,48,384]{2,1,0:T(8,128)(2,1)} %get-tuple-element.84.gp, bf16[112,384]{1,0:T(8,128)(2,1)} %reduce-scatter.5.cloned.1.call-done.mlp), custom_call_target="tpu_custom_call" | custom-call | flops 4000000000 | bytes 4000000 | tf_op jit(solution)/shard_map/pallas_call | solution.py:797
  253.2 4.2 %shard_map.322 = (bf16[314,768]{1,0:T(8,128)(2,1)}, f32[192,384]{1,0:T(8,128)}, f32[96,1152]{1,0:T(8,128)}, f32[96,384]{1,0:T(8,128)}, f32[96,1536]{1,0:T(8,128)...) custom-call(bf16[8,64,384]{2,1,0:T(8,128)(2,1)} %get-tuple-element.8, ...), custom_call_target="tpu_custom_call" | custom-call | flops 1000000000 | bytes 4000000 | tf_op jit(solution)/shard_map/pallas_call | solution.py:865
Async XLA Ops:
  7.2 79.4 %all-gather.2.cloned.1.call-start = ((), (), s32[]{:S(2)}) async-start(), calls=%async_computation.2 | async-start | bytes 3317760 | tf_op jit(solution)/shard_map/all_gather | solution.py:898
  9.2 194.5 %reduce-scatter.3.cloned.1.call-start = ((), (), s32[]{:S(2)}) async-start(), calls=%async_computation.3 | async-start | bytes 3096576 | tf_op jit(solution)/shard_map/reduce_scatter | solution.py:903
  137.1 87.4 %reduce-scatter.5.cloned.1.call-start = ((), (), s32[]{:S(2)}) async-start(), calls=%async_computation.4 | async-start | bytes 430080 | tf_op jit(solution)/shard_map/reduce_scatter | solution.py:904
Sparse Core Ops, SparseCore 0:
  10.2 58.1 all-gather.1
  137.2 43.4 reduce-scatter.2
  203.9 19.5 reduce-scatter.4

commit v5 on v4

--- a/solution.py
+++ b/solution.py
@@ -310,157 +310,113 @@
     )(*ins)
 
 
-def pre_kernel(seen, vis, wp, cols, pos, win, stream_out, q_out, kv_out, k_rows, v_rows):
+def front_kernel(seen, vis, wp, cols, pos, win, o_out, inv_out, e_out, stream_hbm, q_hbm, kt_hbm, v_hbm,
+                 stream_s, q_s, k_s, v_s, k_rows, v_rows, v_aug, sems):
+    copy = pl.program_id(0)
+    step = pl.program_id(1)
     width = wp.shape[1]
-    proj = dg(seen[0], wp[...], 1, 0).astype(BF16)
-    hot = one_hot(vis[0], LP)
-    covered = jnp.sum(hot, 0, keepdims=True)
-    stream = dg(proj, hot.astype(BF16), 0, 0) + (1.0 - covered) * cols[:, TOKEN : TOKEN + 1] + pos[...]
-    stream_out[0] = stream
-    scaled, _ = norm_stats(stream)
-    normed = (scaled * cols[:, GAIN1 : GAIN1 + 1] + cols[:, SHIFT1 : SHIFT1 + 1]).astype(BF16)
-    lane = lax.broadcasted_iota(jnp.int32, (KP, LANES), 1)
-    token = lax.broadcasted_iota(jnp.int32, (KP, LANES), 0)
-    ones = ((lane < HEAD + 3) & (token < L)).astype(F32).astype(BF16)
-    for part in range(3):
-        sl = slice(part * width, (part + 1) * width)
-        mixed = dg(win[:, sl], normed, 0, 0)
-        if part == 0:
-            q_out[0] = ((mixed + cols[:, BIAS_Q : BIAS_Q + 1]) * Q_SCALE).astype(BF16)
-        else:
+    moves = [
+        pltpu.make_async_copy(src, dst.at[copy], sems.at[i])
+        for i, (src, dst) in enumerate(
+            ((stream_s, stream_hbm), (q_s, q_hbm), (k_s, kt_hbm), (v_rows, v_hbm))
+        )
+    ]
+
+    @pl.when(step == 0)
+    def _():
+        proj = dg(seen[0], wp[...], 1, 0).astype(BF16)
+        hot = one_hot(vis[0], LP)
+        covered = jnp.sum(hot, 0, keepdims=True)
+        stream = dg(proj, hot.astype(BF16), 0, 0) + (1.0 - covered) * cols[:, TOKEN : TOKEN + 1] + pos[...]
+        stream_s[...] = stream
+        moves[0].start()
+        scaled, _ = norm_stats(stream)
+        normed = (scaled * cols[:, GAIN1 : GAIN1 + 1] + cols[:, SHIFT1 : SHIFT1 + 1]).astype(BF16)
+        lane = lax.broadcasted_iota(jnp.int32, (L, LANES), 1)
+        ones = (lane < HEAD + 3).astype(F32).astype(BF16)
+        for part in (2, 1, 0):
+            sl = slice(part * width, (part + 1) * width)
+            mixed = dg(win[:, sl], normed, 0, 0)
+            if part == 0:
+                q_s[...] = ((mixed + cols[:, BIAS_Q : BIAS_Q + 1]) * Q_SCALE).astype(BF16)
+                moves[1].start()
+                continue
             if part == 2:
                 mixed = mixed + cols[:, BIAS_V : BIAS_V + 1]
             mixed = mixed.astype(BF16)
-            kv_out[0, (part - 1) * width : part * width, :L] = mixed[:, :L]
-            kv_out[0, (part - 1) * width : part * width, L:] = jnp.zeros((width, LP - L), BF16)
-            dst = k_rows if part == 1 else v_rows
+            dst = k_s if part == 1 else v_s
+            dst[:, :L] = mixed[:, :L]
+            dst[:, L:] = jnp.zeros((width, LP - L), BF16)
+            rows = k_rows if part == 1 else v_rows
             for h in range(H):
-                dst[0, h] = ones
-                dst[0, h, :L, :HEAD] = mixed[h * HEAD : (h + 1) * HEAD].T[:L]
-
-
-def pre(seen, vis, wp, cols, pos, win):
+                if part == 2:
+                    rows[h] = ones
+                rows[h, :, :HEAD] = mixed[h * HEAD : (h + 1) * HEAD].T[:L]
+            moves[2 if part == 1 else 3].start()
+
+    @pl.when(step > 0)
+    def _():
+        head = pl.ds(pl.multiple_of((step - 1) * HEAD, HEAD), HEAD)
+        row = lax.broadcasted_iota(jnp.int32, (16, L), 0)
+        v_aug[:HEAD] = v_s[head, :L]
+        v_aug[HEAD:] = (row == 0).astype(F32).astype(BF16)
+        qf = q_s[head, :].astype(F32)
+        kf = k_s[head, :].astype(F32)
+        bound = jnp.max(jnp.sum(qf * qf, 0, keepdims=True)) * jnp.max(jnp.sum(kf * kf, 0, keepdims=True))
+        safe = bound <= SAFE_EXPONENT * SAFE_EXPONENT
+
+        def run(shift):
+            for start, size in Q_BLOCKS:
+                sl = slice(start, start + size)
+                s = dg(k_rows[step - 1, :, :HEAD], q_s[head, sl], 1, 0)
+                if shift:
+                    s = s - jnp.max(s, 0, keepdims=True)
+                e = jnp.exp2(s).astype(BF16)
+                e_out[0, 0, :, sl] = e
+                o = dg(v_aug[...], e, 1, 0)
+                inv = 1.0 / o[HEAD : HEAD + 1]
+                o_out[0, :, sl] = o[:HEAD] * inv
+                inv_out[0, 0, :, sl] = inv
+
+        pl.when(safe)(lambda: run(False))
+        pl.when(jnp.logical_not(safe))(lambda: run(True))
+
+    @pl.when(step == H)
+    def _():
+        for move in moves:
+            move.wait()
+
+
+def front(seen, vis, wp, cols, pos, win):
     _, a, e = seen.shape
     d = wp.shape[1]
-    const = lambda *s: pl.BlockSpec(s, lambda c: (0,) * len(s))
-    lead = lambda *s: pl.BlockSpec((1,) + s, lambda c: (c,) + (0,) * len(s))
+    const = lambda *s: pl.BlockSpec(s, lambda c, i: (0,) * len(s), pipeline_mode=pl.Buffered(1))
+    lead = lambda *s: pl.BlockSpec((1,) + s, lambda c, i: (c,) + (0,) * len(s))
+    head = lambda c, i: (c, jnp.maximum(i - 1, 0), 0)
+    wide = lambda c, i: (c, jnp.maximum(i - 1, 0), 0, 0)
+    any_ = pl.BlockSpec(memory_space=pl.ANY)
+    shape = jax.ShapeDtypeStruct
+    vm = pltpu.VMEM
     return pl.pallas_call(
-        pre_kernel,
-        grid=(2,),
+        front_kernel,
+        grid=(2, H + 1),
         in_specs=[lead(a, e), lead(a, 1), const(e, d), const(d, 16), const(d, LP), const(d, 3 * d)],
-        out_specs=[lead(d, LP), lead(d, LP), lead(2 * d, LP), lead(H, KP, LANES), lead(H, KP, LANES)],
+        out_specs=[
+            pl.BlockSpec((1, HEAD, LP), head), pl.BlockSpec((1, 1, 1, LP), wide), pl.BlockSpec((1, 1, L, LP), wide),
+            any_, any_, any_, any_,
+        ],
         out_shape=[
-            jax.ShapeDtypeStruct((2, d, LP), F32),
-            jax.ShapeDtypeStruct((2, d, LP), BF16),
-            jax.ShapeDtypeStruct((2, 2 * d, LP), BF16),
-            jax.ShapeDtypeStruct((2, H, KP, LANES), BF16),
-            jax.ShapeDtypeStruct((2, H, KP, LANES), BF16),
+            shape((2, d, LP), F32), shape((2, H, 1, LP), F32), shape((2, H, L, LP), BF16),
+            shape((2, d, LP), F32), shape((2, d, LP), BF16), shape((2, d, LP), BF16), shape((2, H, L, LANES), BF16),
+        ],
+        scratch_shapes=[
+            vm((d, LP), F32), vm((d, LP), BF16), vm((d, LP), BF16), vm((d, LP), BF16),
+            vm((H, L, LANES), BF16), vm((H, L, LANES), BF16), vm((HEAD + 16, L), BF16),
+            pltpu.SemaphoreType.DMA((4,)),
         ],
         compiler_params=params(),
-        cost_estimate=cost(12e9, 2e7),
+        cost_estimate=cost(4e10, 8e7),
     )(seen, vis, wp, cols, pos, win)
-
-
-def attend_kernel(k_rows, q, kt, vt, o_out, inv_out, e_out, v_aug):
-    row = lax.broadcasted_iota(jnp.int32, (16, KP), 0)
-    token = lax.broadcasted_iota(jnp.int32, (16, KP), 1)
-    v_aug[:HEAD] = vt[0, :, :KP]
-    v_aug[HEAD:] = ((row == 0) & (token < L)).astype(F32).astype(BF16)
-    qf = q[0].astype(F32)
-    kf = kt[0].astype(F32)
-    bound = jnp.max(jnp.sum(qf * qf, 0, keepdims=True)) * jnp.max(jnp.sum(kf * kf, 0, keepdims=True))
-    safe = bound <= SAFE_EXPONENT * SAFE_EXPONENT
-
-    def run(shift):
-        for start, size in Q_BLOCKS:
-            sl = slice(start, start + size)
-            s = dg(k_rows[0, 0, :, :HEAD], q[0, :, sl], 1, 0)
-            if shift:
-                key = lax.broadcasted_iota(jnp.int32, (KP, size), 0)
-                s = jnp.where(key < L, s, -jnp.inf)
-                s = s - jnp.max(s, 0, keepdims=True)
-            e = jnp.exp2(s).astype(BF16)
-            e_out[0, 0, :, sl] = e
-            o = dg(v_aug[...], e, 1, 0)
-            inv = 1.0 / o[HEAD : HEAD + 1]
-            o_out[0, :, sl] = o[:HEAD] * inv
-            inv_out[0, 0, :, sl] = inv
-
-    pl.when(safe)(lambda: run(False))
-    pl.when(jnp.logical_not(safe))(lambda: run(True))
-
-
-def attend(k_rows, q, kv):
-    d = q.shape[1]
-    head = lambda off: (lambda i: (i // H, i % H + off, 0))
-    wide = lambda i: (i // H, i % H, 0, 0)
-    return pl.pallas_call(
-        attend_kernel,
-        grid=(2 * H,),
-        in_specs=[
-            pl.BlockSpec((1, 1, KP, LANES), wide),
-            pl.BlockSpec((1, HEAD, LP), head(0)),
-            pl.BlockSpec((1, HEAD, LP), head(0)),
-            pl.BlockSpec((1, HEAD, LP), head(H)),
-        ],
-        out_specs=[
-            pl.BlockSpec((1, HEAD, LP), head(0)),
-            pl.BlockSpec((1, 1, 1, LP), wide),
-            pl.BlockSpec((1, 1, KP, LP), wide),
-        ],
-        out_shape=[
-            jax.ShapeDtypeStruct((2, d, LP), F32),
-            jax.ShapeDtypeStruct((2, H, 1, LP), F32),
-            jax.ShapeDtypeStruct((2, H, KP, LP), BF16),
-        ],
-        scratch_shapes=[pltpu.VMEM((HEAD + 16, KP), BF16)],
-        compiler_params=params(),
-        cost_estimate=cost(3e10, 2e7),
-    )(k_rows, q, kv, kv)
-
-
-def attend_back_kernel(e, v_rows, q, do, dsum, kt, dq, dk, dv, do_aug):
-    do_aug[:HEAD] = do[0]
-    do_aug[HEAD : HEAD + 16] = dsum[0, 0]
-    do_aug[HEAD + 16 :] = jnp.zeros((LANES - HEAD - 16, LP), BF16)
-    k_sum = None
-    v_sum = None
-    for start, size in Q_BLOCKS:
-        sl = slice(start, start + size)
-        p = e[0, 0, :, sl]
-        dp = dg(v_rows[0, 0], do_aug[:, sl], 1, 0)
-        ds = (p.astype(F32) * dp).astype(BF16)
-        v_part = dg(do_aug[:HEAD, sl], p, 1, 1)
-        k_part = dg(q[0, :, sl], ds, 1, 1)
-        v_sum = v_part if v_sum is None else v_sum + v_part
-        k_sum = k_part if k_sum is None else k_sum + k_part
-        dq[0, :, sl] = (dg(kt[0, :, :KP], ds, 1, 0) * (1.0 / math.sqrt(HEAD))).astype(BF16)
-    for dst, total in ((dk, k_sum * (1.0 / LOG2E)), (dv, v_sum)):
-        dst[0, :, :L] = total[:, :L].astype(BF16)
-        dst[0, :, L:] = jnp.zeros((HEAD, LP - L), BF16)
-
-
-def attend_back(e, v_rows, q, do, dsum, kv):
-    d = q.shape[1]
-    head = lambda i: (i // H, i % H, 0)
-    wide = lambda i: (i // H, i % H, 0, 0)
-    return pl.pallas_call(
-        attend_back_kernel,
-        grid=(2 * H,),
-        in_specs=[
-            pl.BlockSpec((1, 1, KP, LP), wide),
-            pl.BlockSpec((1, 1, KP, LANES), wide),
-            pl.BlockSpec((1, HEAD, LP), head),
-            pl.BlockSpec((1, HEAD, LP), head),
-            pl.BlockSpec((1, 1, 16, LP), wide),
-            pl.BlockSpec((1, HEAD, LP), head),
-        ],
-        out_specs=[pl.BlockSpec((1, HEAD, LP), head)] * 3,
-        out_shape=[jax.ShapeDtypeStruct((2, d, LP), BF16)] * 3,
-        scratch_shapes=[pltpu.VMEM((LANES, LP), BF16)],
-        compiler_params=params(),
-        cost_estimate=cost(8e10, 4e7),
-    )(e, v_rows, q, do, dsum, kv)
 
 
 def mlp_parts(d, f, m):
@@ -608,47 +564,74 @@
     )(o, inv, stream, up, wpack, be, cols)
 
 
-def post_kernel(n, m, share, held, seen_len, dq, dk, dv, stream, ga, seen, vis, win, cols, vec_in,
-                gpack, gp_out, dwin, dbin, dvec, dwp, n1, gp_s):
+def back_kernel(n, m, share, held, seen_len, e, v_rows, q, do, dsum, kt, stream, ga, seen, vis, win, cols, vec_in,
+                gpack, gp_out, do_aug, gm, kept, qtmp, dwin, dbin, dvec, dwp, n1, gp_s):
     copy = pl.program_id(0)
+    step = pl.program_id(1)
     clip = lax.axis_index("clip")
     d = win.shape[0]
     e_width = dwp.shape[0]
     seen_pad = seen.shape[1]
     cap = gp_out.shape[1]
 
-    @pl.when(copy == 0)
+    @pl.when((copy == 0) & (step == 0))
     def _():
         dwin[...] = jnp.zeros_like(dwin)
         dbin[...] = jnp.zeros_like(dbin)
         dvec[...] = jnp.zeros_like(dvec)
         dwp[...] = jnp.zeros_like(dwp)
-
-    x = stream[0]
-    scaled, recip = norm_stats(x)
-    n1[:d] = (scaled * cols[:, GAIN1 : GAIN1 + 1] + cols[:, SHIFT1 : SHIFT1 + 1]).astype(BF16)
-    row = lax.broadcasted_iota(jnp.int32, (16, LP), 0)
-    n1[d:] = (row == 0).astype(F32).astype(BF16)
-    e = None
-    for part, ref in enumerate((dq, dk, dv)):
-        sl = slice(part * d, (part + 1) * d)
-        grad = dg(n1[...], ref[0], 1, 1)
-        dwin[:, sl] += grad[:d]
-        dbin[:, sl] += grad[d : d + 8]
-        term = dg(win[:, sl], ref[0], 1, 0)
-        e = term if e is None else e + term
-    dvec[:, 0:1] += jnp.sum(e * scaled, 1, keepdims=True)
-    dvec[:, 1:2] += jnp.sum(e, 1, keepdims=True)
-    gs = ga[0] + norm_back(e, scaled, recip, cols[:, GAIN1 : GAIN1 + 1])
-    hot = one_hot(vis[0], LP)
-    token = lax.broadcasted_iota(jnp.int32, (1, LP), 1)
-    masked = jnp.where(token < L, 1.0 - jnp.sum(hot, 0, keepdims=True), 0.0)
-    dvec[:, 2:3] += jnp.sum(gs * masked, 1, keepdims=True)
-    gp = dg(hot.astype(BF16), gs.astype(BF16), 1, 1).astype(BF16)
-    gp_s[pl.ds(pl.multiple_of(copy * seen_pad, SEG), seen_pad), :] = gp
-    dwp[...] += dg(seen[0], gp, 0, 0)
-
-    @pl.when(copy == 1)
+        do_aug[HEAD + 16 :] = jnp.zeros((LANES - HEAD - 16, LP), BF16)
+        kept[...] = jnp.zeros_like(kept)
+
+    @pl.when(step < H)
+    def _():
+        head = pl.ds(pl.multiple_of(step * HEAD, HEAD), HEAD)
+        do_aug[:HEAD] = do[0]
+        do_aug[HEAD : HEAD + 16] = dsum[0, 0]
+        k_sum = None
+        v_sum = None
+        for start, size in Q_BLOCKS:
+            sl = slice(start, start + size)
+            p = e[0, 0, :, sl]
+            dp = dg(v_rows[0, 0], do_aug[:, sl], 1, 0)
+            ds = (p.astype(F32) * dp).astype(BF16)
+            v_part = dg(do_aug[:HEAD, sl], p, 1, 1)
+            k_part = dg(q[0, :, sl], ds, 1, 1)
+            v_sum = v_part if v_sum is None else v_sum + v_part
+            k_sum = k_part if k_sum is None else k_sum + k_part
+            qtmp[:, sl] = (dg(kt[0, :, :L], ds, 1, 0) * (1.0 / math.sqrt(HEAD))).astype(BF16)
+        gm[pl.ds(pl.multiple_of(step * HEAD, HEAD), HEAD), :] = qtmp[...]
+        for part, total in ((1, k_sum * (1.0 / LOG2E)), (2, v_sum)):
+            kept[:, :L] = total.astype(BF16)
+            gm[pl.ds(pl.multiple_of(part * d + step * HEAD, HEAD), HEAD), :] = kept[...]
+
+    @pl.when(step == H)
+    def _():
+        x = stream[0]
+        scaled, recip = norm_stats(x)
+        n1[:d] = (scaled * cols[:, GAIN1 : GAIN1 + 1] + cols[:, SHIFT1 : SHIFT1 + 1]).astype(BF16)
+        row = lax.broadcasted_iota(jnp.int32, (16, LP), 0)
+        n1[d:] = (row == 0).astype(F32).astype(BF16)
+        e = None
+        for part in range(3):
+            sl = slice(part * d, (part + 1) * d)
+            grad = dg(n1[...], gm[sl], 1, 1)
+            dwin[:, sl] += grad[:d]
+            dbin[:, sl] += grad[d : d + 8]
+            term = dg(win[:, sl], gm[sl], 1, 0)
+            e = term if e is None else e + term
+        dvec[:, 0:1] += jnp.sum(e * scaled, 1, keepdims=True)
+        dvec[:, 1:2] += jnp.sum(e, 1, keepdims=True)
+        gs = ga[0] + norm_back(e, scaled, recip, cols[:, GAIN1 : GAIN1 + 1])
+        hot = one_hot(vis[0], LP)
+        token = lax.broadcasted_iota(jnp.int32, (1, LP), 1)
+        masked = jnp.where(token < L, 1.0 - jnp.sum(hot, 0, keepdims=True), 0.0)
+        dvec[:, 2:3] += jnp.sum(gs * masked, 1, keepdims=True)
+        gp = dg(hot.astype(BF16), gs.astype(BF16), 1, 1).astype(BF16)
+        gp_s[pl.ds(pl.multiple_of(copy * seen_pad, SEG), seen_pad), :] = gp
+        dwp[...] += dg(seen[0], gp, 0, 0)
+
+    @pl.when((copy == 1) & (step == H))
     def _():
         for source in range(n):
             pick = interleave(cap, 2 * seen_pad, clip, source, held, seen_len, seen_pad, n, False)
@@ -679,31 +662,34 @@
                 gpack[at // share, z, at % share : at % share + SEG] = jnp.zeros((SEG, ROWS), BF16)
 
 
-def post(n, m, share, held, seen_len, dq, dk, dv, stream, ga, seen, vis, win, cols, vec_in):
-    _, a, e = seen.shape
+def back(n, m, share, held, seen_len, e, v_rows, q, do, dsum, kt, stream, ga, seen, vis, win, cols, vec_in):
+    _, a, width = seen.shape
     d = win.shape[0]
     cap = up16(-(-held // n))
-    once = pl.Buffered(1)
-    const = lambda *s: pl.BlockSpec(s, lambda c: (0,) * len(s), pipeline_mode=once)
-    lead = lambda *s: pl.BlockSpec((1,) + s, lambda c: (c,) + (0,) * len(s))
+    const = lambda *s: pl.BlockSpec(s, lambda c, i: (0,) * len(s), pipeline_mode=pl.Buffered(1))
+    lead = lambda *s: pl.BlockSpec((1,) + s, lambda c, i: (c,) + (0,) * len(s))
+    head = lambda c, i: (c, jnp.minimum(i, H - 1), 0)
+    wide = lambda c, i: (c, jnp.minimum(i, H - 1), 0, 0)
     shape = jax.ShapeDtypeStruct
     vm = pltpu.VMEM
     return pl.pallas_call(
-        functools.partial(post_kernel, n, m, share, held, seen_len),
-        grid=(2,),
+        functools.partial(back_kernel, n, m, share, held, seen_len),
+        grid=(2, H + 1),
         in_specs=[
-            lead(d, LP), lead(d, LP), lead(d, LP), lead(d, LP), lead(d, LP), lead(a, e), lead(a, 1),
-            const(d, 3 * d), const(d, 16), const(16, d),
+            pl.BlockSpec((1, 1, L, LP), wide), pl.BlockSpec((1, 1, L, LANES), wide), pl.BlockSpec((1, HEAD, LP), head),
+            pl.BlockSpec((1, HEAD, LP), head), pl.BlockSpec((1, 1, 16, LP), wide), pl.BlockSpec((1, HEAD, LP), head),
+            lead(d, LP), lead(d, LP), lead(a, width), lead(a, 1), const(d, 3 * d), const(d, 16), const(16, d),
         ],
         out_specs=[const(n, m, share, ROWS), const(n, cap, d)],
         out_shape=[shape((n, m, share, ROWS), BF16), shape((n, cap, d), BF16)],
         scratch_shapes=[
-            vm((d, 3 * d), F32), vm((8, 3 * d), F32), vm((d, LANES), F32), vm((e, d), F32),
+            vm((LANES, LP), BF16), vm((3 * d, LP), BF16), vm((HEAD, LP), BF16), vm((HEAD, LP), BF16),
+            vm((d, 3 * d), F32), vm((8, 3 * d), F32), vm((d, LANES), F32), vm((width, d), F32),
             vm((d + 16, LP), BF16), vm((2 * a, d), BF16),
         ],
         compiler_params=params(),
-        cost_estimate=cost(2e10, 2e7),
-    )(dq, dk, dv, stream, ga, seen, vis, win, cols, vec_in)
+        cost_estimate=cost(1e11, 1e8),
+    )(e, v_rows, q, do, dsum, kt, stream, ga, seen, vis, win, cols, vec_in)
 
 
 def leave_kernel(n, m, gpack, gp, mlp, fin, ret, mlp_out, a1, a2s, a2r, tot, tot_b, brecv, fin_s, ret_s, mlp_s,
@@ -875,15 +861,13 @@
 def core(n, m, held, seen_len, seen, vis, wp, win, cols, be, wpack, upstream, reduce_mlp=None):
     d = cols.shape[0]
     pos = jnp.asarray(position_table(d))
-    stream, q, kv, k_rows, v_rows = pre(seen, vis, wp, cols, pos, win)
-    o, inv, e = attend(k_rows, q, kv)
+    o, inv, e, stream, q, kt, v_rows = front(seen, vis, wp, cols, pos, win)
     share = up16(-(-wpack.shape[1] // n))
     dec, ga, do, dsum, mlp, vec = mid(n, m, share, o, inv, stream, upstream.reshape(2, L, d), wpack, be, cols)
     if reduce_mlp is not None:
         mlp = reduce_mlp(mlp)
-    dq, dk, dv = attend_back(e, v_rows, q, do, dsum, kv)
     share = up16(-(-(wp.shape[0] // m + 3 * (d // m) + SEG) // n))
-    gpack, gp = post(n, m, share, held, seen_len, dq, dk, dv, stream, ga, seen, vis, win, cols, vec)
+    gpack, gp = back(n, m, share, held, seen_len, e, v_rows, q, do, dsum, kt, stream, ga, seen, vis, win, cols, vec)
     return dec, mlp, gpack, gp
 
 

time: 267 us -> 306 us (1.15)
  waiting for transfers between devices: 0.07 us -> 43.6 us
  Pallas kernels: 250 us -> 245 us
    reduce_scatter x1, waiting for transfers between devices: 0.02 us -> 43.5 us  [reduce_mlp(): lax.psum_scatter(mlp.reshape(-1, ROWS), 'clip', scatter_dimension=0, tile...]
    pallas_call x4 -> x2, Pallas kernels: 137 us -> 131 us  [the longest x1 85.1 us: back(): pl.pallas_call(functools.partial(back_kernel, n, m, share, held, seen_len...]
  transfers between devices with their start and end apart: 3 -> 3, of which waited for: 0 -> 1; matrix products, arithmetic and copies ran while one was open for 0% -> 0% of each run, Pallas kernels for 62% -> 52%
where the time goes in v5:
time: 306 us; the launch traced here: 303 us
  Pallas kernels  245 us (80%)
  waiting for transfers between devices  43.6 us (14%)
  between operations  14 us (5%)
    pallas_call x1, Pallas kernels, back(): pl.pallas_call(functools.partial(back_kernel, n, m, share, held, seen_len...  85.1 us
    pallas_call x1, Pallas kernels, mid(): pl.pallas_call(functools.partial(mid_kernel, n, m, share), grid=(2, f //...  50.5 us
    pallas_call x1, Pallas kernels, front(): pl.pallas_call(front_kernel, grid=(2, H + 1), in_specs=[lead(a, e), lead(...  45.5 us
    reduce_scatter x1, waiting for transfers between devices, reduce_mlp(): lax.psum_scatter(mlp.reshape(-1, ROWS), 'clip', scatter_dimension=0, tile...  43.5 us
    pallas_call x1, Pallas kernels, leave(): pl.pallas_call(functools.partial(leave_kernel, n, m), in_specs=[whole] *...  30 us
    pallas_call x1, Pallas kernels, enter(): pl.pallas_call(functools.partial(enter_kernel, n, m, share, cap, seen_pad...  27.8 us
  transfers between devices with their start and end apart: 3, of which 1 were waited for; matrix products, arithmetic and copies ran while one was open for 0% of the time, Pallas kernels for 52%

profile of v5, /device:TPU:0, one launch (start us, length us, event | category | flops | bytes accessed | tf_op | source)
XLA Modules:
  0.0 302.8 jit_solution(4048708223305721899)
XLA Ops:
  7.2 0.0 all-gather.2.cloned.1.call-start
  7.2 2.0 shard_map.316
  9.2 0.0 all-gather.2.cloned.1.call-update
  9.2 0.0 reduce-scatter.3.cloned.1.call-start
  9.3 27.8 %shard_map.314 = (bf16[2,160,768]{2,1,0:T(8,128)(2,1)}, f32[2,160,1]{2,1,0:T(8,128)}, bf16[768,384]{1,0:T(8,128)(2,1)}, bf16[384,1152]{1,0:T(8,128)(2,1)}, f32[384,16]{1,0:T(8,128)}, /*index=5*/f32[1536,1]{1,0:T(8,128)}) custom-call(bf16[314,768]{1,0:T(8,128)(2,1)} %refs_0_.1, s32[2,157]{1,0:T(2,128)} %refs_1_.1, bf16[192,384]{1,0:T(8,128)(2,1)} %refs_2_.1, ...), custom_call_target="tpu_custom_call" | custom-call | flops 6000000000 | bytes 4000000 | tf_op jit(solution)/shard_map/pallas_call | solution.py:293
  37.1 45.5 %shard_map.315 = (f32[2,384,1664]{2,1,0:T(8,128)}, f32[2,6,1,1664]{3,2,1,0:T(1,128)}, bf16[2,6,1568,1664]{3,2,1,0:T(8,128)(2,1)}, f32[2,384,1664]{2,1,0:T(8,128)...) custom-call(bf16[2,160,768]{2,1,0:T(8,128)(2,1)} %get-tuple-element.57.seen, ...), custom_call_target="tpu_custom_call" | custom-call | flops 40000000000 | bytes 80000000 | tf_op jit(solution)/shard_map/pallas_call | solution.py:400
  82.6 0.0 all-gather.2.cloned.1.call-done
  82.7 50.5 %shard_map.317 = (bf16[2,1568,384]{2,1,0:T(8,128)(2,1)}, f32[2,384,1664]{2,1,0:T(8,128)}, bf16[2,384,1664]{2,1,0:T(8,128)(2,1)}, bf16[2,6,16,1664]{3,2,1,0:T(8,1...) custom-call(f32[2,384,1664]{2,1,0:T(8,128)} %get-tuple-element.62.o, ...), custom_call_target="tpu_custom_call" | custom-call | flops 49999998976 | bytes 40000000 | tf_op jit(solution)/shard_map/pallas_call | solution.py:545
  133.1 0.0 reduce-scatter.3.cloned.1.call-update
  133.2 0.0 reduce-scatter.5.cloned.1.call-start
  133.2 43.5 %reduce-scatter.3.cloned.1.call-done = bf16[448,384]{1,0:T(8,128)(2,1)} async-done(((bf16[3584,384]{1,0:T(8,128)(2,1)}), bf16[448,384]{1,0:T(8,128)(2,1)}) %reduce-scatter.3.cloned.1.call-update) | async-done | bytes 344080 | tf_op jit(solution)/shard_map/reduce_scatter | solution.py:887
  176.8 0.0 reduce-scatter.5.cloned.1.call-update
  176.8 85.1 %shard_map.318 = (bf16[8,4,64,384]{3,2,1,0:T(8,128)(2,1)}, bf16[8,48,384]{2,1,0:T(8,128)(2,1)}) custom-call(bf16[2,6,1568,1664]{3,2,1,0:T(8,128)(2,1)} %get-tuple-element.67.e, bf16[2,6,1568,128]{3,2,1,0:T(8,128)(2,1)} %get-tuple-element.68.v_rows, bf16[2,384,1664]{2,1,0:T(8,128)(2,1)} %get-tuple-element.69.q, bf16[2,384,1664]{2,1,0:T(8,128)(2,1)} %get-tuple-element.70.do, ...), custom_call_target="tpu_custom_call" | custom-call | flops 99999997952 | bytes 100000000 | tf_op jit(solution)/shard_map/pallas_call | solution.py:675
  261.9 0.0 reduce-scatter.5.cloned.1.call-done.mlp
  261.9 30.0 %shard_map.319 = (bf16[8,64,384]{2,1,0:T(8,128)(2,1)}, bf16[8,48,384]{2,1,0:T(8,128)(2,1)}, bf16[8,112,384]{2,1,0:T(8,128)(2,1)}) custom-call(bf16[8,4,64,384]{3,2,1,0:T(8,128)(2,1)} %get-tuple-element.75.gpack, bf16[8,48,384]{2,1,0:T(8,128)(2,1)} %get-tuple-element.76.gp, bf16[112,384]{1,0:T(8,128)(2,1)} %reduce-scatter.5.cloned.1.call-done.mlp), custom_call_target="tpu_custom_call" | custom-call | flops 4000000000 | bytes 4000000 | tf_op jit(solution)/shard_map/pallas_call | solution.py:783
  291.9 4.2 %shard_map.320 = (bf16[314,768]{1,0:T(8,128)(2,1)}, f32[192,384]{1,0:T(8,128)}, f32[96,1152]{1,0:T(8,128)}, f32[96,384]{1,0:T(8,128)}, f32[96,1536]{1,0:T(8,128)...) custom-call(bf16[8,64,384]{2,1,0:T(8,128)(2,1)} %get-tuple-element.7, ...), custom_call_target="tpu_custom_call" | custom-call | flops 1000000000 | bytes 4000000 | tf_op jit(solution)/shard_map/pallas_call | solution.py:851
Async XLA Ops:
  7.2 75.5 %all-gather.2.cloned.1.call-start = ((), (), s32[]{:S(2)}) async-start(), calls=%async_computation.2 | async-start | bytes 3317760 | tf_op jit(solution)/shard_map/all_gather | solution.py:882
  9.2 167.5 %reduce-scatter.3.cloned.1.call-start = ((), (), s32[]{:S(2)}) async-start(), calls=%async_computation.3 | async-start | bytes 3096576 | tf_op jit(solution)/shard_map/reduce_scatter | solution.py:887
  133.2 128.7 %reduce-scatter.5.cloned.1.call-start = ((), (), s32[]{:S(2)}) async-start(), calls=%async_computation.4 | async-start | bytes 430080 | tf_op jit(solution)/shard_map/reduce_scatter | solution.py:888
Sparse Core Ops, SparseCore 0:
  10.2 58.0 all-gather.1
  133.3 43.4 reduce-scatter.2
  179.1 20.4 reduce-scatter.4

commit v6 on v5

--- a/solution.py
+++ b/solution.py
@@ -692,15 +692,14 @@
     )(e, v_rows, q, do, dsum, kt, stream, ga, seen, vis, win, cols, vec_in)
 
 
-def leave_kernel(n, m, gpack, gp, mlp, fin, ret, mlp_out, a1, a2s, a2r, tot, tot_b, brecv, fin_s, ret_s, mlp_s,
-                 gs, gr, s1, r1, s2, r2, sb, rb, sc, rc, sm, rm, sf, rf):
+def leave_kernel(n, m, gpack, gp, mlp, fin, ret, mlp_out, a1, a2s, a2r, tot, tot_b, brecv, fin_s, ret_s, mlp_s, mlp_z,
+                 gs, gr, s1, r1, s2, r2, sb, rb, sc, rc, sm, rm, sf, rf, sz, rz):
     clip = lax.axis_index("clip")
     wt = lax.axis_index("wt")
     half = n // 2
     core = lax.rem(clip, 2)
     chip = clip // 2
     partner = clip + 1 - 2 * core
-    mlp_s[clip] = mlp[...]
     greet(n, m, clip, wt)
     sends = []
 
@@ -711,6 +710,9 @@
 
     order = [*range(1, half), 0]
     turns = [*range(1, m), 0]
+    for k in range(1, m):
+        zz = lax.rem(wt + k, m)
+        send(mlp.at[zz], mlp_z.at[k], sz.at[k], rz.at[k], clip, zz)
     for k in turns:
         zz = lax.rem(wt + k, m)
         for j in order:
@@ -731,6 +733,12 @@
         dest = lax.rem(clip + k, n)
         send(gp.at[dest], ret_s.at[clip], gs.at[k], gr.at[k], dest, wt)
     ret_s[clip] = gp[clip]
+    total = mlp[wt].astype(F32)
+    for k in range(1, m):
+        source = lax.rem(wt - k + m, m)
+        remote(mlp.at[source], mlp_z.at[k], sz.at[k], rz.at[k], clip, source).wait_recv()
+        total = total + mlp_z[k].astype(F32)
+    mlp_s[clip] = total.astype(BF16)
     for j in order:
         dest = lax.rem(clip + 2 * j, n) if j else partner
         send(mlp_s.at[clip], mlp_s.at[clip], sm.at[j], rm.at[j], dest, wt)
@@ -784,14 +792,14 @@
         functools.partial(leave_kernel, n, m),
         in_specs=[whole] * 3,
         out_specs=[whole] * 3,
-        out_shape=[shape((n, share, ROWS), BF16), shape((n, cap, d), BF16), shape((n,) + mlp.shape, BF16)],
+        out_shape=[shape((n, share, ROWS), BF16), shape((n, cap, d), BF16), shape((n,) + mlp.shape[1:], BF16)],
         scratch_shapes=[
             vm((half, m, share, ROWS), BF16), vm((half, m, share, ROWS), BF16), vm((half, m, share, ROWS), BF16),
             vm((m, share, ROWS), F32), vm((m, share, ROWS), BF16), vm((m, share, ROWS), BF16),
-            vm((n, share, ROWS), BF16), vm((n, cap, d), BF16), vm((n,) + mlp.shape, BF16),
+            vm((n, share, ROWS), BF16), vm((n, cap, d), BF16), vm((n,) + mlp.shape[1:], BF16), vm(mlp.shape, BF16),
             dma((n,)), dma((n,)), dma((half, m)), dma((half, m)), dma((half, m)), dma((half, m)),
             dma((m,)), dma((m,)), dma((n,)), dma((n,)),
-            dma((half,)), dma((half,)), dma((half,)), dma((half,)),
+            dma((half,)), dma((half,)), dma((half,)), dma((half,)), dma((m,)), dma((m,)),
         ],
         compiler_params=params(collective_id=1, has_side_effects=True),
         cost_estimate=cost(4e9, 4e6),
@@ -884,8 +892,8 @@
     seen, vis, wp_full, win_full, cols, be_col = enter(n, m, encoded, visible_at, wp, win, vecs)
 
     def reduce_mlp(mlp):
-        mlp = lax.psum_scatter(mlp.reshape(-1, ROWS), "clip", scatter_dimension=0, tiled=True)
-        return lax.psum_scatter(mlp, "wt", scatter_dimension=0, tiled=True)
+        part = lax.psum_scatter(mlp.reshape(-1, ROWS), "clip", scatter_dimension=0, tiled=True)
+        return part.reshape(mlp.shape[1:])
 
     dec, mlp, gpack, gp = core(
         n, m, held, seen_len, seen, vis, wp_full, win_full, cols, be_col, wpack, upstream, reduce_mlp

time: 306 us -> 261 us (0.85)
  waiting for transfers between devices: 43.6 us -> 0.07 us
    reduce_scatter x1, waiting for transfers between devices: 43.5 us -> 0.02 us  [reduce_mlp(): lax.psum_scatter(mlp.reshape(-1, ROWS), 'clip', scatter_dimension=0, tile...]
  transfers between devices with their start and end apart: 3 -> 2, of which waited for: 1 -> 0; matrix products, arithmetic and copies ran while one was open for 0% -> 0% of each run, Pallas kernels for 52% -> 61%
where the time goes in v6:
time: 261 us; the launch traced here: 258 us
  Pallas kernels  244 us (93%)
  between operations  14.3 us (5%)
    pallas_call x1, Pallas kernels, back(): pl.pallas_call(functools.partial(back_kernel, n, m, share, held, seen_len...  85.3 us
    pallas_call x1, Pallas kernels, mid(): pl.pallas_call(functools.partial(mid_kernel, n, m, share), grid=(2, f //...  50.5 us
    pallas_call x1, Pallas kernels, front(): pl.pallas_call(front_kernel, grid=(2, H + 1), in_specs=[lead(a, e), lead(...  45.5 us
    pallas_call x1, Pallas kernels, leave(): pl.pallas_call(functools.partial(leave_kernel, n, m), in_specs=[whole] *...  28.4 us
    pallas_call x1, Pallas kernels, enter(): pl.pallas_call(functools.partial(enter_kernel, n, m, share, cap, seen_pad...  27.8 us
  transfers between devices with their start and end apart: 2, of which 0 were waited for; matrix products, arithmetic and copies ran while one was open for 0% of the time, Pallas kernels for 61%

profile of v6, /device:TPU:0, one launch (start us, length us, event | category | flops | bytes accessed | tf_op | source)
XLA Modules:
  0.0 258.2 jit_solution(1249045430636623657)
XLA Ops:
  7.2 0.0 all-gather.2.cloned.1.call-start
  7.2 2.0 shard_map.316
  9.2 0.0 all-gather.2.cloned.1.call-update
  9.2 0.0 reduce-scatter.2.cloned.1.call-start
  9.3 27.8 %shard_map.314 = (bf16[2,160,768]{2,1,0:T(8,128)(2,1)}, f32[2,160,1]{2,1,0:T(8,128)}, bf16[768,384]{1,0:T(8,128)(2,1)}, bf16[384,1152]{1,0:T(8,128)(2,1)}, f32[384,16]{1,0:T(8,128)}, /*index=5*/f32[1536,1]{1,0:T(8,128)}) custom-call(bf16[314,768]{1,0:T(8,128)(2,1)} %refs_0_.1, s32[2,157]{1,0:T(2,128)} %refs_1_.1, bf16[192,384]{1,0:T(8,128)(2,1)} %refs_2_.1, ...), custom_call_target="tpu_custom_call" | custom-call | flops 6000000000 | bytes 4000000 | tf_op jit(solution)/shard_map/pallas_call | solution.py:293
  37.1 45.5 %shard_map.315 = (f32[2,384,1664]{2,1,0:T(8,128)}, f32[2,6,1,1664]{3,2,1,0:T(1,128)}, bf16[2,6,1568,1664]{3,2,1,0:T(8,128)(2,1)}, f32[2,384,1664]{2,1,0:T(8,128)...) custom-call(bf16[2,160,768]{2,1,0:T(8,128)(2,1)} %get-tuple-element.57.seen, ...), custom_call_target="tpu_custom_call" | custom-call | flops 40000000000 | bytes 80000000 | tf_op jit(solution)/shard_map/pallas_call | solution.py:400
  82.6 0.0 all-gather.2.cloned.1.call-done
  82.7 50.5 %shard_map.317 = (bf16[2,1568,384]{2,1,0:T(8,128)(2,1)}, f32[2,384,1664]{2,1,0:T(8,128)}, bf16[2,384,1664]{2,1,0:T(8,128)(2,1)}, bf16[2,6,16,1664]{3,2,1,0:T(8,1...) custom-call(f32[2,384,1664]{2,1,0:T(8,128)} %get-tuple-element.62.o, ...), custom_call_target="tpu_custom_call" | custom-call | flops 49999998976 | bytes 40000000 | tf_op jit(solution)/shard_map/pallas_call | solution.py:545
  133.1 0.0 reduce-scatter.2.cloned.1.call-update
  133.2 85.3 %shard_map.318 = (bf16[8,4,64,384]{3,2,1,0:T(8,128)(2,1)}, bf16[8,48,384]{2,1,0:T(8,128)(2,1)}) custom-call(bf16[2,6,1568,1664]{3,2,1,0:T(8,128)(2,1)} %get-tuple-element.67.e, bf16[2,6,1568,128]{3,2,1,0:T(8,128)(2,1)} %get-tuple-element.68.v_rows, bf16[2,384,1664]{2,1,0:T(8,128)(2,1)} %get-tuple-element.69.q, bf16[2,384,1664]{2,1,0:T(8,128)(2,1)} %get-tuple-element.70.do, ...), custom_call_target="tpu_custom_call" | custom-call | flops 99999997952 | bytes 100000000 | tf_op jit(solution)/shard_map/pallas_call | solution.py:675
  218.4 0.0 reduce-scatter.2.cloned.1.call-done
  218.5 28.4 %shard_map.319 = (bf16[8,64,384]{2,1,0:T(8,128)(2,1)}, bf16[8,48,384]{2,1,0:T(8,128)(2,1)}, bf16[8,112,384]{2,1,0:T(8,128)(2,1)}) custom-call(bf16[8,4,64,384]{3,2,1,0:T(8,128)(2,1)} %get-tuple-element.75.gpack, bf16[8,48,384]{2,1,0:T(8,128)(2,1)} %get-tuple-element.76.gp, bf16[4,112,384]{2,1,0:T(8,128)(2,1)} %bitcast.8), custom_call_target="tpu_custom_call" | custom-call | flops 4000000000 | bytes 4000000 | tf_op jit(solution)/shard_map/pallas_call | solution.py:791
  246.9 4.2 %shard_map.320 = (bf16[314,768]{1,0:T(8,128)(2,1)}, f32[192,384]{1,0:T(8,128)}, f32[96,1152]{1,0:T(8,128)}, f32[96,384]{1,0:T(8,128)}, f32[96,1536]{1,0:T(8,128)...) custom-call(bf16[8,64,384]{2,1,0:T(8,128)(2,1)} %get-tuple-element.7, ...), custom_call_target="tpu_custom_call" | custom-call | flops 1000000000 | bytes 4000000 | tf_op jit(solution)/shard_map/pallas_call | solution.py:859
Async XLA Ops:
  7.2 75.5 %all-gather.2.cloned.1.call-start = ((), (), s32[]{:S(2)}) async-start(), calls=%async_computation.1 | async-start | bytes 3317760 | tf_op jit(solution)/shard_map/all_gather | solution.py:890
  9.2 209.2 %reduce-scatter.2.cloned.1.call-start = ((), (), s32[]{:S(2)}) async-start(), calls=%async_computation.2 | async-start | bytes 3096576 | tf_op jit(solution)/shard_map/reduce_scatter | solution.py:895
Sparse Core Ops, SparseCore 0:
  10.2 58.0 all-gather.1
  133.3 43.4 reduce-scatter.1

commit v7 on v6

--- a/solution.py
+++ b/solution.py
@@ -24,6 +24,7 @@
 VMEM_LIMIT = 60 * 2**20
 FFC = 512
 Q_BLOCKS = ((0, 896), (896, LP - 896))
+FRONT_BLOCKS = ((0, 1024), (1024, LP - 1024))
 F32 = jnp.float32
 BF16 = jnp.bfloat16
 
@@ -366,7 +367,7 @@
         safe = bound <= SAFE_EXPONENT * SAFE_EXPONENT
 
         def run(shift):
-            for start, size in Q_BLOCKS:
+            for start, size in FRONT_BLOCKS:
                 sl = slice(start, start + size)
                 s = dg(k_rows[step - 1, :, :HEAD], q_s[head, sl], 1, 0)
                 if shift:
@@ -564,12 +565,12 @@
     )(o, inv, stream, up, wpack, be, cols)
 
 
-def back_kernel(n, m, share, held, seen_len, e, v_rows, q, do, dsum, kt, stream, ga, seen, vis, win, cols, vec_in,
-                gpack, gp_out, do_aug, gm, kept, qtmp, dwin, dbin, dvec, dwp, n1, gp_s):
+def back_kernel(n, m, share, held, seen_len, e, v_rows, q, do, dsum, kt, stream_hbm, ga_hbm, seen, vis, win_hbm, cols, vec_in,
+                gpack, gp_out, do_aug, gm, kept, qtmp, dwin, dbin, dvec, dwp, n1, gp_s, stream, ga, win, sems):
     copy = pl.program_id(0)
     step = pl.program_id(1)
     clip = lax.axis_index("clip")
-    d = win.shape[0]
+    d = cols.shape[0]
     e_width = dwp.shape[0]
     seen_pad = seen.shape[1]
     cap = gp_out.shape[1]
@@ -582,6 +583,18 @@
         dwp[...] = jnp.zeros_like(dwp)
         do_aug[HEAD + 16 :] = jnp.zeros((LANES - HEAD - 16, LP), BF16)
         kept[...] = jnp.zeros_like(kept)
+
+    loads = [
+        pltpu.make_async_copy(stream_hbm.at[copy], stream, sems.at[0]),
+        pltpu.make_async_copy(ga_hbm.at[copy], ga, sems.at[1]),
+    ]
+    load_win = pltpu.make_async_copy(win_hbm, win, sems.at[2])
+    pl.when((copy == 0) & (step == 0))(load_win.start)
+
+    @pl.when(step == 0)
+    def _():
+        for load in loads:
+            load.start()
 
     @pl.when(step < H)
     def _():
@@ -607,7 +620,10 @@
 
     @pl.when(step == H)
     def _():
-        x = stream[0]
+        pl.when(copy == 0)(load_win.wait)
+        for load in loads:
+            load.wait()
+        x = stream[...]
         scaled, recip = norm_stats(x)
         n1[:d] = (scaled * cols[:, GAIN1 : GAIN1 + 1] + cols[:, SHIFT1 : SHIFT1 + 1]).astype(BF16)
         row = lax.broadcasted_iota(jnp.int32, (16, LP), 0)
@@ -622,7 +638,7 @@
             e = term if e is None else e + term
         dvec[:, 0:1] += jnp.sum(e * scaled, 1, keepdims=True)
         dvec[:, 1:2] += jnp.sum(e, 1, keepdims=True)
-        gs = ga[0] + norm_back(e, scaled, recip, cols[:, GAIN1 : GAIN1 + 1])
+        gs = ga[...] + norm_back(e, scaled, recip, cols[:, GAIN1 : GAIN1 + 1])
         hot = one_hot(vis[0], LP)
         token = lax.broadcasted_iota(jnp.int32, (1, LP), 1)
         masked = jnp.where(token < L, 1.0 - jnp.sum(hot, 0, keepdims=True), 0.0)
@@ -670,6 +686,7 @@
     lead = lambda *s: pl.BlockSpec((1,) + s, lambda c, i: (c,) + (0,) * len(s))
     head = lambda c, i: (c, jnp.minimum(i, H - 1), 0)
     wide = lambda c, i: (c, jnp.minimum(i, H - 1), 0, 0)
+    any_ = pl.BlockSpec(memory_space=pl.ANY)
     shape = jax.ShapeDtypeStruct
     vm = pltpu.VMEM
     return pl.pallas_call(
@@ -678,14 +695,15 @@
         in_specs=[
             pl.BlockSpec((1, 1, L, LP), wide), pl.BlockSpec((1, 1, L, LANES), wide), pl.BlockSpec((1, HEAD, LP), head),
             pl.BlockSpec((1, HEAD, LP), head), pl.BlockSpec((1, 1, 16, LP), wide), pl.BlockSpec((1, HEAD, LP), head),
-            lead(d, LP), lead(d, LP), lead(a, width), lead(a, 1), const(d, 3 * d), const(d, 16), const(16, d),
+            any_, any_, lead(a, width), lead(a, 1), any_, const(d, 16), const(16, d),
         ],
         out_specs=[const(n, m, share, ROWS), const(n, cap, d)],
         out_shape=[shape((n, m, share, ROWS), BF16), shape((n, cap, d), BF16)],
         scratch_shapes=[
             vm((LANES, LP), BF16), vm((3 * d, LP), BF16), vm((HEAD, LP), BF16), vm((HEAD, LP), BF16),
             vm((d, 3 * d), F32), vm((8, 3 * d), F32), vm((d, LANES), F32), vm((width, d), F32),
-            vm((d + 16, LP), BF16), vm((2 * a, d), BF16),
+            vm((d + 16, LP), BF16), vm((2 * a, d), BF16), vm((d, LP), F32), vm((d, LP), F32), vm((d, 3 * d), BF16),
+            pltpu.SemaphoreType.DMA((3,)),
         ],
         compiler_params=params(),
         cost_estimate=cost(1e11, 1e8),

time: 261 us -> 259 us (level)
  Pallas kernels: 244 us -> 241 us
where the time goes in v7:
time: 259 us; the launch traced here: 256 us
  Pallas kernels  241 us (93%)
  between operations  14.3 us (6%)
    pallas_call x1, Pallas kernels, back(): pl.pallas_call(functools.partial(back_kernel, n, m, share, held, seen_len...  83.3 us
    pallas_call x1, Pallas kernels, mid(): pl.pallas_call(functools.partial(mid_kernel, n, m, share), grid=(2, f //...  50.5 us
    pallas_call x1, Pallas kernels, front(): pl.pallas_call(front_kernel, grid=(2, H + 1), in_specs=[lead(a, e), lead(...  44.7 us
    pallas_call x1, Pallas kernels, leave(): pl.pallas_call(functools.partial(leave_kernel, n, m), in_specs=[whole] *...  28.8 us
    pallas_call x1, Pallas kernels, enter(): pl.pallas_call(functools.partial(enter_kernel, n, m, share, cap, seen_pad...  27.8 us
  transfers between devices with their start and end apart: 2, of which 0 were waited for; matrix products, arithmetic and copies ran while one was open for 0% of the time, Pallas kernels for 61%

profile of v7, /device:TPU:0, one launch (start us, length us, event | category | flops | bytes accessed | tf_op | source)
XLA Modules:
  0.0 255.8 jit_solution(12822939134906628765)
XLA Ops:
  7.2 0.0 all-gather.2.cloned.1.call-start
  7.2 2.0 shard_map.316
  9.2 0.0 all-gather.2.cloned.1.call-update
  9.2 0.0 reduce-scatter.2.cloned.1.call-start
  9.3 27.8 %shard_map.314 = (bf16[2,160,768]{2,1,0:T(8,128)(2,1)}, f32[2,160,1]{2,1,0:T(8,128)}, bf16[768,384]{1,0:T(8,128)(2,1)}, bf16[384,1152]{1,0:T(8,128)(2,1)}, f32[384,16]{1,0:T(8,128)}, /*index=5*/f32[1536,1]{1,0:T(8,128)}) custom-call(bf16[314,768]{1,0:T(8,128)(2,1)} %refs_0_.1, s32[2,157]{1,0:T(2,128)} %refs_1_.1, bf16[192,384]{1,0:T(8,128)(2,1)} %refs_2_.1, ...), custom_call_target="tpu_custom_call" | custom-call | flops 6000000000 | bytes 4000000 | tf_op jit(solution)/shard_map/pallas_call | solution.py:294
  37.1 44.7 %shard_map.315 = (f32[2,384,1664]{2,1,0:T(8,128)}, f32[2,6,1,1664]{3,2,1,0:T(1,128)}, bf16[2,6,1568,1664]{3,2,1,0:T(8,128)(2,1)}, f32[2,384,1664]{2,1,0:T(8,128)...) custom-call(bf16[2,160,768]{2,1,0:T(8,128)(2,1)} %get-tuple-element.57.seen, ...), custom_call_target="tpu_custom_call" | custom-call | flops 40000000000 | bytes 80000000 | tf_op jit(solution)/shard_map/pallas_call | solution.py:401
  81.8 0.0 all-gather.2.cloned.1.call-done
  81.9 50.5 %shard_map.317 = (bf16[2,1568,384]{2,1,0:T(8,128)(2,1)}, f32[2,384,1664]{2,1,0:T(8,128)}, bf16[2,384,1664]{2,1,0:T(8,128)(2,1)}, bf16[2,6,16,1664]{3,2,1,0:T(8,1...) custom-call(f32[2,384,1664]{2,1,0:T(8,128)} %get-tuple-element.62.o, ...), custom_call_target="tpu_custom_call" | custom-call | flops 49999998976 | bytes 40000000 | tf_op jit(solution)/shard_map/pallas_call | solution.py:546
  132.4 0.0 reduce-scatter.2.cloned.1.call-update
  132.4 83.3 %shard_map.318 = (bf16[8,4,64,384]{3,2,1,0:T(8,128)(2,1)}, bf16[8,48,384]{2,1,0:T(8,128)(2,1)}) custom-call(bf16[2,6,1568,1664]{3,2,1,0:T(8,128)(2,1)} %get-tuple-element.67.e, bf16[2,6,1568,128]{3,2,1,0:T(8,128)(2,1)} %get-tuple-element.68.v_rows, bf16[2,384,1664]{2,1,0:T(8,128)(2,1)} %get-tuple-element.69.q, bf16[2,384,1664]{2,1,0:T(8,128)(2,1)} %get-tuple-element.70.do, ...), custom_call_target="tpu_custom_call" | custom-call | flops 99999997952 | bytes 100000000 | tf_op jit(solution)/shard_map/pallas_call | solution.py:692
  215.7 0.0 reduce-scatter.2.cloned.1.call-done
  215.7 28.8 %shard_map.319 = (bf16[8,64,384]{2,1,0:T(8,128)(2,1)}, bf16[8,48,384]{2,1,0:T(8,128)(2,1)}, bf16[8,112,384]{2,1,0:T(8,128)(2,1)}) custom-call(bf16[8,4,64,384]{3,2,1,0:T(8,128)(2,1)} %get-tuple-element.75.gpack, bf16[8,48,384]{2,1,0:T(8,128)(2,1)} %get-tuple-element.76.gp, bf16[4,112,384]{2,1,0:T(8,128)(2,1)} %bitcast.8), custom_call_target="tpu_custom_call" | custom-call | flops 4000000000 | bytes 4000000 | tf_op jit(solution)/shard_map/pallas_call | solution.py:809
  244.5 4.2 %shard_map.320 = (bf16[314,768]{1,0:T(8,128)(2,1)}, f32[192,384]{1,0:T(8,128)}, f32[96,1152]{1,0:T(8,128)}, f32[96,384]{1,0:T(8,128)}, f32[96,1536]{1,0:T(8,128)...) custom-call(bf16[8,64,384]{2,1,0:T(8,128)(2,1)} %get-tuple-element.7, ...), custom_call_target="tpu_custom_call" | custom-call | flops 1000000000 | bytes 4000000 | tf_op jit(solution)/shard_map/pallas_call | solution.py:877
Async XLA Ops:
  7.2 74.7 %all-gather.2.cloned.1.call-start = ((), (), s32[]{:S(2)}) async-start(), calls=%async_computation.1 | async-start | bytes 3317760 | tf_op jit(solution)/shard_map/all_gather | solution.py:908
  9.2 206.4 %reduce-scatter.2.cloned.1.call-start = ((), (), s32[]{:S(2)}) async-start(), calls=%async_computation.2 | async-start | bytes 3096576 | tf_op jit(solution)/shard_map/reduce_scatter | solution.py:913
Sparse Core Ops, SparseCore 0:
  10.2 58.0 all-gather.1
  132.5 43.4 reduce-scatter.1

commit v8 on v7

--- a/solution.py
+++ b/solution.py
@@ -339,7 +339,7 @@
             sl = slice(part * width, (part + 1) * width)
             mixed = dg(win[:, sl], normed, 0, 0)
             if part == 0:
-                q_s[...] = ((mixed + cols[:, BIAS_Q : BIAS_Q + 1]) * Q_SCALE).astype(BF16)
+                q_s[...] = (mixed + cols[:, BIAS_Q : BIAS_Q + 1]).astype(BF16)
                 moves[1].start()
                 continue
             if part == 2:
@@ -364,7 +364,7 @@
         qf = q_s[head, :].astype(F32)
         kf = k_s[head, :].astype(F32)
         bound = jnp.max(jnp.sum(qf * qf, 0, keepdims=True)) * jnp.max(jnp.sum(kf * kf, 0, keepdims=True))
-        safe = bound <= SAFE_EXPONENT * SAFE_EXPONENT
+        safe = bound * (Q_SCALE * Q_SCALE) <= SAFE_EXPONENT * SAFE_EXPONENT
 
         def run(shift):
             for start, size in FRONT_BLOCKS:
@@ -372,7 +372,7 @@
                 s = dg(k_rows[step - 1, :, :HEAD], q_s[head, sl], 1, 0)
                 if shift:
                     s = s - jnp.max(s, 0, keepdims=True)
-                e = jnp.exp2(s).astype(BF16)
+                e = jnp.exp2(s * Q_SCALE).astype(BF16)
                 e_out[0, 0, :, sl] = e
                 o = dg(v_aug[...], e, 1, 0)
                 inv = 1.0 / o[HEAD : HEAD + 1]
@@ -614,7 +614,7 @@
             k_sum = k_part if k_sum is None else k_sum + k_part
             qtmp[:, sl] = (dg(kt[0, :, :L], ds, 1, 0) * (1.0 / math.sqrt(HEAD))).astype(BF16)
         gm[pl.ds(pl.multiple_of(step * HEAD, HEAD), HEAD), :] = qtmp[...]
-        for part, total in ((1, k_sum * (1.0 / LOG2E)), (2, v_sum)):
+        for part, total in ((1, k_sum * (1.0 / math.sqrt(HEAD))), (2, v_sum)):
             kept[:, :L] = total.astype(BF16)
             gm[pl.ds(pl.multiple_of(part * d + step * HEAD, HEAD), HEAD), :] = kept[...]
 
@@ -775,12 +775,17 @@
         remote(tot_b.at[k], brecv.at[k], sb.at[k], rb.at[k], clip, source).wait_recv()
         total = total + brecv[k].astype(F32)
     fin_s[clip] = total.astype(BF16)
-    for k in [*range(2, n, 2), *range(1, n, 2)]:
-        send(fin_s.at[clip], fin_s.at[clip], sc.at[k], rc.at[k], lax.rem(clip + k, n), wt)
+    for j in order:
+        dest = lax.rem(clip + 2 * j, n) if j else partner
+        send(fin_s.at[clip], fin_s.at[clip], sc.at[j], rc.at[j], dest, wt)
     for j in range(1, half):
         source = lax.rem(clip - 2 * j + n, n)
         remote(mlp_s.at[source], mlp_s.at[source], sm.at[j], rm.at[j], source, wt).wait_recv()
         send(mlp_s.at[source], mlp_s.at[source], sf.at[j], rf.at[j], partner, wt)
+    for j in range(1, half):
+        source = lax.rem(clip - 2 * j + n, n)
+        remote(fin_s.at[source], fin_s.at[source], sc.at[j], rc.at[j], source, wt).wait_recv()
+        send(fin_s.at[source], fin_s.at[source], sc.at[half + j], rc.at[half + j], partner, wt)
     for k in range(1, n):
         source = lax.rem(clip - k + n, n)
         remote(gp.at[source], ret_s.at[source], gs.at[k], gr.at[k], source, wt).wait_recv()
@@ -790,9 +795,10 @@
         sems = (sf.at[j], rf.at[j]) if j else (sm.at[0], rm.at[0])
         remote(mlp_s.at[source], mlp_s.at[source], *sems, partner, wt).wait_recv()
     mlp_out[...] = mlp_s[...]
-    for k in range(1, n):
-        source = lax.rem(clip - k + n, n)
-        remote(fin_s.at[source], fin_s.at[source], sc.at[k], rc.at[k], source, wt).wait_recv()
+    for j in range(half):
+        source = lax.rem(partner - 2 * j + n, n)
+        at = half + j if j else 0
+        remote(fin_s.at[source], fin_s.at[source], sc.at[at], rc.at[at], partner, wt).wait_recv()
     fin[...] = fin_s[...]
     for copy in sends:
         copy.wait_send()

time: 259 us -> 258 us (level)
  no operation moved by 1% of the time
where the time goes in v8:
time: 258 us; the launch traced here: 254 us
  Pallas kernels  240 us (93%)
  between operations  14.3 us (6%)
    pallas_call x1, Pallas kernels, back(): pl.pallas_call(functools.partial(back_kernel, n, m, share, held, seen_len...  83.3 us
    pallas_call x1, Pallas kernels, mid(): pl.pallas_call(functools.partial(mid_kernel, n, m, share), grid=(2, f //...  50.5 us
    pallas_call x1, Pallas kernels, front(): pl.pallas_call(front_kernel, grid=(2, H + 1), in_specs=[lead(a, e), lead(...  44.9 us
    pallas_call x1, Pallas kernels, enter(): pl.pallas_call(functools.partial(enter_kernel, n, m, share, cap, seen_pad...  27.8 us
    pallas_call x1, Pallas kernels, leave(): pl.pallas_call(functools.partial(leave_kernel, n, m), in_specs=[whole] *...  27.3 us
  transfers between devices with their start and end apart: 2, of which 0 were waited for; matrix products, arithmetic and copies ran while one was open for 0% of the time, Pallas kernels for 61%

profile of v8, /device:TPU:0, one launch (start us, length us, event | category | flops | bytes accessed | tf_op | source)
XLA Modules:
  0.0 254.4 jit_solution(16118995334091535206)
XLA Ops:
  7.2 0.0 all-gather.2.cloned.1.call-start
  7.2 2.0 shard_map.316
  9.2 0.0 all-gather.2.cloned.1.call-update
  9.2 0.0 reduce-scatter.2.cloned.1.call-start
  9.3 27.8 %shard_map.314 = (bf16[2,160,768]{2,1,0:T(8,128)(2,1)}, f32[2,160,1]{2,1,0:T(8,128)}, bf16[768,384]{1,0:T(8,128)(2,1)}, bf16[384,1152]{1,0:T(8,128)(2,1)}, f32[384,16]{1,0:T(8,128)}, /*index=5*/f32[1536,1]{1,0:T(8,128)}) custom-call(bf16[314,768]{1,0:T(8,128)(2,1)} %refs_0_.1, s32[2,157]{1,0:T(2,128)} %refs_1_.1, bf16[192,384]{1,0:T(8,128)(2,1)} %refs_2_.1, ...), custom_call_target="tpu_custom_call" | custom-call | flops 6000000000 | bytes 4000000 | tf_op jit(solution)/shard_map/pallas_call | solution.py:294
  37.1 44.9 %shard_map.315 = (f32[2,384,1664]{2,1,0:T(8,128)}, f32[2,6,1,1664]{3,2,1,0:T(1,128)}, bf16[2,6,1568,1664]{3,2,1,0:T(8,128)(2,1)}, f32[2,384,1664]{2,1,0:T(8,128)...) custom-call(bf16[2,160,768]{2,1,0:T(8,128)(2,1)} %get-tuple-element.57.seen, ...), custom_call_target="tpu_custom_call" | custom-call | flops 40000000000 | bytes 80000000 | tf_op jit(solution)/shard_map/pallas_call | solution.py:401
  82.0 0.0 all-gather.2.cloned.1.call-done
  82.1 50.5 %shard_map.317 = (bf16[2,1568,384]{2,1,0:T(8,128)(2,1)}, f32[2,384,1664]{2,1,0:T(8,128)}, bf16[2,384,1664]{2,1,0:T(8,128)(2,1)}, bf16[2,6,16,1664]{3,2,1,0:T(8,1...) custom-call(f32[2,384,1664]{2,1,0:T(8,128)} %get-tuple-element.62.o, ...), custom_call_target="tpu_custom_call" | custom-call | flops 49999998976 | bytes 40000000 | tf_op jit(solution)/shard_map/pallas_call | solution.py:546
  132.6 0.0 reduce-scatter.2.cloned.1.call-update
  132.6 83.3 %shard_map.318 = (bf16[8,4,64,384]{3,2,1,0:T(8,128)(2,1)}, bf16[8,48,384]{2,1,0:T(8,128)(2,1)}) custom-call(bf16[2,6,1568,1664]{3,2,1,0:T(8,128)(2,1)} %get-tuple-element.67.e, bf16[2,6,1568,128]{3,2,1,0:T(8,128)(2,1)} %get-tuple-element.68.v_rows, bf16[2,384,1664]{2,1,0:T(8,128)(2,1)} %get-tuple-element.69.q, bf16[2,384,1664]{2,1,0:T(8,128)(2,1)} %get-tuple-element.70.do, ...), custom_call_target="tpu_custom_call" | custom-call | flops 99999997952 | bytes 100000000 | tf_op jit(solution)/shard_map/pallas_call | solution.py:692
  215.8 0.0 reduce-scatter.2.cloned.1.call-done
  215.9 27.3 %shard_map.319 = (bf16[8,64,384]{2,1,0:T(8,128)(2,1)}, bf16[8,48,384]{2,1,0:T(8,128)(2,1)}, bf16[8,112,384]{2,1,0:T(8,128)(2,1)}) custom-call(bf16[8,4,64,384]{3,2,1,0:T(8,128)(2,1)} %get-tuple-element.75.gpack, bf16[8,48,384]{2,1,0:T(8,128)(2,1)} %get-tuple-element.76.gp, bf16[4,112,384]{2,1,0:T(8,128)(2,1)} %bitcast.8), custom_call_target="tpu_custom_call" | custom-call | flops 4000000000 | bytes 4000000 | tf_op jit(solution)/shard_map/pallas_call | solution.py:815
  243.2 4.2 %shard_map.320 = (bf16[314,768]{1,0:T(8,128)(2,1)}, f32[192,384]{1,0:T(8,128)}, f32[96,1152]{1,0:T(8,128)}, f32[96,384]{1,0:T(8,128)}, f32[96,1536]{1,0:T(8,128)...) custom-call(bf16[8,64,384]{2,1,0:T(8,128)(2,1)} %get-tuple-element.7, ...), custom_call_target="tpu_custom_call" | custom-call | flops 1000000000 | bytes 4000000 | tf_op jit(solution)/shard_map/pallas_call | solution.py:883
Async XLA Ops:
  7.2 74.9 %all-gather.2.cloned.1.call-start = ((), (), s32[]{:S(2)}) async-start(), calls=%async_computation.1 | async-start | bytes 3317760 | tf_op jit(solution)/shard_map/all_gather | solution.py:914
  9.2 206.6 %reduce-scatter.2.cloned.1.call-start = ((), (), s32[]{:S(2)}) async-start(), calls=%async_computation.2 | async-start | bytes 3096576 | tf_op jit(solution)/shard_map/reduce_scatter | solution.py:919
Sparse Core Ops, SparseCore 0:
  10.2 58.0 all-gather.1
  132.7 43.4 reduce-scatter.1

commit v9 on v8

--- a/solution.py
+++ b/solution.py
@@ -333,8 +333,14 @@
         moves[0].start()
         scaled, _ = norm_stats(stream)
         normed = (scaled * cols[:, GAIN1 : GAIN1 + 1] + cols[:, SHIFT1 : SHIFT1 + 1]).astype(BF16)
-        lane = lax.broadcasted_iota(jnp.int32, (L, LANES), 1)
-        ones = (lane < HEAD + 3).astype(F32).astype(BF16)
+
+        @pl.when(copy == 0)
+        def _():
+            lane = lax.broadcasted_iota(jnp.int32, (L, LANES), 1)
+            ones = (lane < HEAD + 3).astype(F32).astype(BF16)
+            for h in range(H):
+                v_rows[h] = ones
+
         for part in (2, 1, 0):
             sl = slice(part * width, (part + 1) * width)
             mixed = dg(win[:, sl], normed, 0, 0)
@@ -350,8 +356,6 @@
             dst[:, L:] = jnp.zeros((width, LP - L), BF16)
             rows = k_rows if part == 1 else v_rows
             for h in range(H):
-                if part == 2:
-                    rows[h] = ones
                 rows[h, :, :HEAD] = mixed[h * HEAD : (h + 1) * HEAD].T[:L]
             moves[2 if part == 1 else 3].start()
 

time: 258 us -> 259 us (level)
  no operation moved by 1% of the time
where the time goes in v9:
time: 259 us; the launch traced here: 255 us
  Pallas kernels  241 us (93%)
  between operations  14.3 us (6%)
    pallas_call x1, Pallas kernels, back(): pl.pallas_call(functools.partial(back_kernel, n, m, share, held, seen_len...  83.3 us
    pallas_call x1, Pallas kernels, mid(): pl.pallas_call(functools.partial(mid_kernel, n, m, share), grid=(2, f //...  50.5 us
    pallas_call x1, Pallas kernels, front(): pl.pallas_call(front_kernel, grid=(2, H + 1), in_specs=[lead(a, e), lead(...  45.8 us
    pallas_call x1, Pallas kernels, enter(): pl.pallas_call(functools.partial(enter_kernel, n, m, share, cap, seen_pad...  27.8 us
    pallas_call x1, Pallas kernels, leave(): pl.pallas_call(functools.partial(leave_kernel, n, m), in_specs=[whole] *...  27.4 us
  transfers between devices with their start and end apart: 2, of which 0 were waited for; matrix products, arithmetic and copies ran while one was open for 0% of the time, Pallas kernels for 61%

profile of v9, /device:TPU:0, one launch (start us, length us, event | category | flops | bytes accessed | tf_op | source)
XLA Modules:
  0.0 255.5 jit_solution(1583739324949125757)
XLA Ops:
  7.2 0.0 all-gather.2.cloned.1.call-start
  7.2 2.0 shard_map.316
  9.2 0.0 all-gather.2.cloned.1.call-update
  9.2 0.0 reduce-scatter.2.cloned.1.call-start
  9.3 27.8 %shard_map.314 = (bf16[2,160,768]{2,1,0:T(8,128)(2,1)}, f32[2,160,1]{2,1,0:T(8,128)}, bf16[768,384]{1,0:T(8,128)(2,1)}, bf16[384,1152]{1,0:T(8,128)(2,1)}, f32[384,16]{1,0:T(8,128)}, /*index=5*/f32[1536,1]{1,0:T(8,128)}) custom-call(bf16[314,768]{1,0:T(8,128)(2,1)} %refs_0_.1, s32[2,157]{1,0:T(2,128)} %refs_1_.1, bf16[192,384]{1,0:T(8,128)(2,1)} %refs_2_.1, ...), custom_call_target="tpu_custom_call" | custom-call | flops 6000000000 | bytes 4000000 | tf_op jit(solution)/shard_map/pallas_call | solution.py:294
  37.1 45.8 %shard_map.315 = (f32[2,384,1664]{2,1,0:T(8,128)}, f32[2,6,1,1664]{3,2,1,0:T(1,128)}, bf16[2,6,1568,1664]{3,2,1,0:T(8,128)(2,1)}, f32[2,384,1664]{2,1,0:T(8,128)...) custom-call(bf16[2,160,768]{2,1,0:T(8,128)(2,1)} %get-tuple-element.57.seen, ...), custom_call_target="tpu_custom_call" | custom-call | flops 40000000000 | bytes 80000000 | tf_op jit(solution)/shard_map/pallas_call | solution.py:405
  83.0 0.0 all-gather.2.cloned.1.call-done
  83.0 50.5 %shard_map.317 = (bf16[2,1568,384]{2,1,0:T(8,128)(2,1)}, f32[2,384,1664]{2,1,0:T(8,128)}, bf16[2,384,1664]{2,1,0:T(8,128)(2,1)}, bf16[2,6,16,1664]{3,2,1,0:T(8,1...) custom-call(f32[2,384,1664]{2,1,0:T(8,128)} %get-tuple-element.62.o, ...), custom_call_target="tpu_custom_call" | custom-call | flops 49999998976 | bytes 40000000 | tf_op jit(solution)/shard_map/pallas_call | solution.py:550
  133.5 0.0 reduce-scatter.2.cloned.1.call-update
  133.5 83.3 %shard_map.318 = (bf16[8,4,64,384]{3,2,1,0:T(8,128)(2,1)}, bf16[8,48,384]{2,1,0:T(8,128)(2,1)}) custom-call(bf16[2,6,1568,1664]{3,2,1,0:T(8,128)(2,1)} %get-tuple-element.67.e, bf16[2,6,1568,128]{3,2,1,0:T(8,128)(2,1)} %get-tuple-element.68.v_rows, bf16[2,384,1664]{2,1,0:T(8,128)(2,1)} %get-tuple-element.69.q, bf16[2,384,1664]{2,1,0:T(8,128)(2,1)} %get-tuple-element.70.do, ...), custom_call_target="tpu_custom_call" | custom-call | flops 99999997952 | bytes 100000000 | tf_op jit(solution)/shard_map/pallas_call | solution.py:696
  216.8 0.0 reduce-scatter.2.cloned.1.call-done
  216.8 27.4 %shard_map.319 = (bf16[8,64,384]{2,1,0:T(8,128)(2,1)}, bf16[8,48,384]{2,1,0:T(8,128)(2,1)}, bf16[8,112,384]{2,1,0:T(8,128)(2,1)}) custom-call(bf16[8,4,64,384]{3,2,1,0:T(8,128)(2,1)} %get-tuple-element.75.gpack, bf16[8,48,384]{2,1,0:T(8,128)(2,1)} %get-tuple-element.76.gp, bf16[4,112,384]{2,1,0:T(8,128)(2,1)} %bitcast.8), custom_call_target="tpu_custom_call" | custom-call | flops 4000000000 | bytes 4000000 | tf_op jit(solution)/shard_map/pallas_call | solution.py:819
  244.2 4.2 %shard_map.320 = (bf16[314,768]{1,0:T(8,128)(2,1)}, f32[192,384]{1,0:T(8,128)}, f32[96,1152]{1,0:T(8,128)}, f32[96,384]{1,0:T(8,128)}, f32[96,1536]{1,0:T(8,128)...) custom-call(bf16[8,64,384]{2,1,0:T(8,128)(2,1)} %get-tuple-element.7, ...), custom_call_target="tpu_custom_call" | custom-call | flops 1000000000 | bytes 4000000 | tf_op jit(solution)/shard_map/pallas_call | solution.py:887
Async XLA Ops:
  7.2 75.8 %all-gather.2.cloned.1.call-start = ((), (), s32[]{:S(2)}) async-start(), calls=%async_computation.1 | async-start | bytes 3317760 | tf_op jit(solution)/shard_map/all_gather | solution.py:918
  9.2 207.6 %reduce-scatter.2.cloned.1.call-start = ((), (), s32[]{:S(2)}) async-start(), calls=%async_computation.2 | async-start | bytes 3096576 | tf_op jit(solution)/shard_map/reduce_scatter | solution.py:923
Sparse Core Ops, SparseCore 0:
  10.2 58.0 all-gather.1
  133.6 43.4 reduce-scatter.1
